TPU v7x, 128 devices: a whole 4x4x4 slice. The times are simulated.
128 devices in a mesh: row: 32 (over z, x, core), rep: 4 (over y).
Axes of the slice: x: 4, y: 4, z: 4, core: 2. Of those that a mesh axis runs over, the one named last changes fastest.
Arguments:
- grad_out: bfloat16 [65536, 256], P(('row', 'rep')), may hold values from -6 to 6
- preact: bfloat16 [65536, 256], P(('row', 'rep')), may hold values from -6 to 6
- features: bfloat16 [65536, 256], P(('row', 'rep')), may hold values from -6 to 6
- weight: bfloat16 [256, 256], replicated, may hold values from -0.375 to 0.375
- adj_values: bfloat16 [512, 128, 128, 128], P('row', 'rep'), may hold values from -0.0625 to 0.0625
- adj_cols: int32 [512, 128], P('row', 'rep'), may hold values from 0 to 511, as said below
- adj_counts: int32 [512, 4], P('row', 'rep'), may hold values from 1 to 32, as said below
Outputs:
- grad_features: bfloat16 [65536, 256], P(('row', 'rep'))
- grad_weight: float32 [256, 256], replicated
Inputs may be any that keep to these rules, and one draw needn't show every extreme that they name: `adj_cols`: the stored block at slot p * 32 + s of a block row has a column block j with (j % 16) // 4 == p; the column blocks of one block row are all different; blocks past the live count still carry a valid column block. `adj_counts`: some entry equals 32.
All inputs are finite; a program needn't handle non-finite values.
Results may differ from a plain program's by a relative error of at most 0.019.
Values may be sent and summed in bfloat16 or wider, within the bound.
No kernel may reach another device: no remote copies, remote signals or barrier semaphores. Data moves between devices by JAX's collectives and lax.ppermute only.
A program may use at most 128 MiB of HBM per device.

v0:
```python
import jax
import jax.numpy as jnp
from jax import lax
from jax.sharding import PartitionSpec as P


def body(grad_out, preact, features, weight, adj_values, adj_cols, adj_counts):
    masked_local = jnp.where(preact > 0, grad_out, jnp.zeros_like(grad_out))
    grad_pre = lax.all_gather(masked_local, "rep", axis=0, tiled=True)
    rows_here = adj_values.shape[0]
    slot_count = adj_values.shape[1]
    block_size = adj_values.shape[2]
    feat_width = grad_pre.shape[1]
    replicas = lax.axis_size("rep")
    groups = lax.axis_size("row")
    share_blocks = rows_here // replicas
    targets = groups * share_blocks
    grad_blocks = grad_pre.reshape(rows_here, block_size, feat_width)
    alive_slots = lax.broadcasted_iota(jnp.int32, (rows_here, slot_count), 1) < adj_counts
    local_index = adj_cols // rows_here * share_blocks + adj_cols % rows_here % share_blocks

    def row_step(index, partial_value):
        messages = jnp.einsum(
            "sij,if->sjf", adj_values[index], grad_blocks[index], preferred_element_type=jnp.float32
        )
        messages = jnp.where(alive_slots[index][:, None, None], messages, jnp.zeros_like(messages))
        return partial_value.at[local_index[index]].add(messages)

    partial_value = lax.fori_loop(
        0, rows_here, row_step, jnp.zeros((targets, block_size, feat_width), jnp.float32)
    )
    outgoing = partial_value.astype(jnp.bfloat16).reshape(
        groups, share_blocks * block_size, feat_width
    )
    incoming = lax.all_to_all(outgoing, "row", split_axis=0, concat_axis=0, tiled=True)
    aggregated = jnp.sum(incoming.astype(jnp.float32), axis=0)
    grad_agg = aggregated.astype(jnp.bfloat16)
    weight_term = jnp.dot(features.T, grad_agg, preferred_element_type=jnp.float32)
    grad_weight = lax.psum(weight_term, ("row", "rep"))
    grad_features = jnp.dot(grad_agg, weight.T, preferred_element_type=jnp.float32).astype(
        jnp.bfloat16
    )
    return (grad_features, grad_weight)


def solution(mesh):
    placed = (
        P(("row", "rep"), None),
        P(("row", "rep"), None),
        P(("row", "rep"), None),
        P(),
        P("row", "rep", None, None),
        P("row", "rep"),
        P("row", "rep"),
    )
    return jax.shard_map(
        body, mesh=mesh, in_specs=placed, out_specs=(P(("row", "rep"), None), P()), check_vma=False
    )
```

profile of v0, /device:TPU:1, one launch (start us, length us, event | category | flops | bytes accessed | tf_op | source)
XLA Modules:
  0.0 536.3 jit_solution(1760739400142764587)
XLA Ops:
  10.5 26.0 %all-gather.2.cloned.1.call-done = bf16[2048,256]{1,0:T(8,128)(2,1)} async-done(((bf16[512,256]{1,0:T(8,128)(2,1)}), bf16[2048,256]{1,0:T(8,128)(2,1)}) %all-gather.2.cloned.1.call-update) | async-done | bytes 1048592 | tf_op jit(solution)/shard_map/all_gather | solution.py:9
  36.6 7.8 %broadcast_in_dim.26 = f32[128,128,256]{2,1,0:T(8,128)} broadcast(f32[]{:T(128)} %constant.73.clone.1), dimensions={} | broadcast | bytes 16777220 | tf_op jit(solution)/shard_map/broadcast_in_dim | solution.py:30
  44.4 227.3 %while.13 = (s32[]{:T(128)}, f32[128,128,256]{2,1,0:T(8,128)}, s32[16,32]{1,0:T(8,128)S(1)}, pred[16,32]{1,0:T(8,128)(4,1)S(1)}, bf16[16,32,128,128]{3,2,1,0:T(8...) while((s32[]{:T(128)}, f32[128,128,256]{2,1,0:T(8,128)}, s32[16,32]{1,0:T(8,128)S(1)}, ...), condition=%wide.region_2.3_spmd, body=%wide.region_0.2_spmd.sunk | while | flops 270532704 | bytes 17892924 | solution.py:29
  48.4 10.2 %scatter_fusion = f32[128,128,256]{2,1,0:T(8,128)} fusion(f32[128,128,256]{2,1,0:T(8,128)} %get-tuple-element.177, s32[32]{0:T(128)S(1)} %fusion.21, f32[32,128,256]{2,1,0:T(8,128)} %convolution_select_fusion.2), kind=kCustom, calls=%fused_computation.clone.1 | custom fusion | flops 1048576 | bytes 12583040 | tf_op jit(solution)/shard_map/while/body/eval_jaxpr/scatter-add | solution.py:27
  62.6 10.2 %scatter_fusion = f32[128,128,256]{2,1,0:T(8,128)} fusion(f32[128,128,256]{2,1,0:T(8,128)} %get-tuple-element.177, s32[32]{0:T(128)S(1)} %fusion.21, f32[32,128,256]{2,1,0:T(8,128)} %convolution_select_fusion.2), kind=kCustom, calls=%fused_computation.clone.1 | custom fusion | flops 1048576 | bytes 12583040 | tf_op jit(solution)/shard_map/while/body/eval_jaxpr/scatter-add | solution.py:27
  72.8 4.0 convolution_select_fusion.2
  76.8 10.3 %scatter_fusion = f32[128,128,256]{2,1,0:T(8,128)} fusion(f32[128,128,256]{2,1,0:T(8,128)} %get-tuple-element.177, s32[32]{0:T(128)S(1)} %fusion.21, f32[32,128,256]{2,1,0:T(8,128)} %convolution_select_fusion.2), kind=kCustom, calls=%fused_computation.clone.1 | custom fusion | flops 1048576 | bytes 12583040 | tf_op jit(solution)/shard_map/while/body/eval_jaxpr/scatter-add | solution.py:27
  91.0 10.2 %scatter_fusion = f32[128,128,256]{2,1,0:T(8,128)} fusion(f32[128,128,256]{2,1,0:T(8,128)} %get-tuple-element.177, s32[32]{0:T(128)S(1)} %fusion.21, f32[32,128,256]{2,1,0:T(8,128)} %convolution_select_fusion.2), kind=kCustom, calls=%fused_computation.clone.1 | custom fusion | flops 1048576 | bytes 12583040 | tf_op jit(solution)/shard_map/while/body/eval_jaxpr/scatter-add | solution.py:27
  101.3 4.0 convolution_select_fusion.2
  105.2 10.2 %scatter_fusion = f32[128,128,256]{2,1,0:T(8,128)} fusion(f32[128,128,256]{2,1,0:T(8,128)} %get-tuple-element.177, s32[32]{0:T(128)S(1)} %fusion.21, f32[32,128,256]{2,1,0:T(8,128)} %convolution_select_fusion.2), kind=kCustom, calls=%fused_computation.clone.1 | custom fusion | flops 1048576 | bytes 12583040 | tf_op jit(solution)/shard_map/while/body/eval_jaxpr/scatter-add | solution.py:27
  115.5 4.0 convolution_select_fusion.2
  119.4 10.2 %scatter_fusion = f32[128,128,256]{2,1,0:T(8,128)} fusion(f32[128,128,256]{2,1,0:T(8,128)} %get-tuple-element.177, s32[32]{0:T(128)S(1)} %fusion.21, f32[32,128,256]{2,1,0:T(8,128)} %convolution_select_fusion.2), kind=kCustom, calls=%fused_computation.clone.1 | custom fusion | flops 1048576 | bytes 12583040 | tf_op jit(solution)/shard_map/while/body/eval_jaxpr/scatter-add | solution.py:27
  129.7 4.0 convolution_select_fusion.2
  133.6 10.3 %scatter_fusion = f32[128,128,256]{2,1,0:T(8,128)} fusion(f32[128,128,256]{2,1,0:T(8,128)} %get-tuple-element.177, s32[32]{0:T(128)S(1)} %fusion.21, f32[32,128,256]{2,1,0:T(8,128)} %convolution_select_fusion.2), kind=kCustom, calls=%fused_computation.clone.1 | custom fusion | flops 1048576 | bytes 12583040 | tf_op jit(solution)/shard_map/while/body/eval_jaxpr/scatter-add | solution.py:27
  143.9 4.0 convolution_select_fusion.2
  147.9 10.2 %scatter_fusion = f32[128,128,256]{2,1,0:T(8,128)} fusion(f32[128,128,256]{2,1,0:T(8,128)} %get-tuple-element.177, s32[32]{0:T(128)S(1)} %fusion.21, f32[32,128,256]{2,1,0:T(8,128)} %convolution_select_fusion.2), kind=kCustom, calls=%fused_computation.clone.1 | custom fusion | flops 1048576 | bytes 12583040 | tf_op jit(solution)/shard_map/while/body/eval_jaxpr/scatter-add | solution.py:27
  158.1 4.0 convolution_select_fusion.2
  162.1 10.2 %scatter_fusion = f32[128,128,256]{2,1,0:T(8,128)} fusion(f32[128,128,256]{2,1,0:T(8,128)} %get-tuple-element.177, s32[32]{0:T(128)S(1)} %fusion.21, f32[32,128,256]{2,1,0:T(8,128)} %convolution_select_fusion.2), kind=kCustom, calls=%fused_computation.clone.1 | custom fusion | flops 1048576 | bytes 12583040 | tf_op jit(solution)/shard_map/while/body/eval_jaxpr/scatter-add | solution.py:27
  176.3 10.2 %scatter_fusion = f32[128,128,256]{2,1,0:T(8,128)} fusion(f32[128,128,256]{2,1,0:T(8,128)} %get-tuple-element.177, s32[32]{0:T(128)S(1)} %fusion.21, f32[32,128,256]{2,1,0:T(8,128)} %convolution_select_fusion.2), kind=kCustom, calls=%fused_computation.clone.1 | custom fusion | flops 1048576 | bytes 12583040 | tf_op jit(solution)/shard_map/while/body/eval_jaxpr/scatter-add | solution.py:27
  186.5 4.0 convolution_select_fusion.2
  190.5 10.2 %scatter_fusion = f32[128,128,256]{2,1,0:T(8,128)} fusion(f32[128,128,256]{2,1,0:T(8,128)} %get-tuple-element.177, s32[32]{0:T(128)S(1)} %fusion.21, f32[32,128,256]{2,1,0:T(8,128)} %convolution_select_fusion.2), kind=kCustom, calls=%fused_computation.clone.1 | custom fusion | flops 1048576 | bytes 12583040 | tf_op jit(solution)/shard_map/while/body/eval_jaxpr/scatter-add | solution.py:27
  200.7 4.0 convolution_select_fusion.2
  204.7 10.3 %scatter_fusion = f32[128,128,256]{2,1,0:T(8,128)} fusion(f32[128,128,256]{2,1,0:T(8,128)} %get-tuple-element.177, s32[32]{0:T(128)S(1)} %fusion.21, f32[32,128,256]{2,1,0:T(8,128)} %convolution_select_fusion.2), kind=kCustom, calls=%fused_computation.clone.1 | custom fusion | flops 1048576 | bytes 12583040 | tf_op jit(solution)/shard_map/while/body/eval_jaxpr/scatter-add | solution.py:27
  219.0 10.2 %scatter_fusion = f32[128,128,256]{2,1,0:T(8,128)} fusion(f32[128,128,256]{2,1,0:T(8,128)} %get-tuple-element.177, s32[32]{0:T(128)S(1)} %fusion.21, f32[32,128,256]{2,1,0:T(8,128)} %convolution_select_fusion.2), kind=kCustom, calls=%fused_computation.clone.1 | custom fusion | flops 1048576 | bytes 12583040 | tf_op jit(solution)/shard_map/while/body/eval_jaxpr/scatter-add | solution.py:27
  233.2 10.2 %scatter_fusion = f32[128,128,256]{2,1,0:T(8,128)} fusion(f32[128,128,256]{2,1,0:T(8,128)} %get-tuple-element.177, s32[32]{0:T(128)S(1)} %fusion.21, f32[32,128,256]{2,1,0:T(8,128)} %convolution_select_fusion.2), kind=kCustom, calls=%fused_computation.clone.1 | custom fusion | flops 1048576 | bytes 12583040 | tf_op jit(solution)/shard_map/while/body/eval_jaxpr/scatter-add | solution.py:27
  247.3 10.2 %scatter_fusion = f32[128,128,256]{2,1,0:T(8,128)} fusion(f32[128,128,256]{2,1,0:T(8,128)} %get-tuple-element.177, s32[32]{0:T(128)S(1)} %fusion.21, f32[32,128,256]{2,1,0:T(8,128)} %convolution_select_fusion.2), kind=kCustom, calls=%fused_computation.clone.1 | custom fusion | flops 1048576 | bytes 12583040 | tf_op jit(solution)/shard_map/while/body/eval_jaxpr/scatter-add | solution.py:27
  257.5 4.0 convolution_select_fusion.2
  261.5 10.3 %scatter_fusion = f32[128,128,256]{2,1,0:T(8,128)} fusion(f32[128,128,256]{2,1,0:T(8,128)} %get-tuple-element.177, s32[32]{0:T(128)S(1)} %fusion.21, f32[32,128,256]{2,1,0:T(8,128)} %convolution_select_fusion.2), kind=kCustom, calls=%fused_computation.clone.1 | custom fusion | flops 1048576 | bytes 12583040 | tf_op jit(solution)/shard_map/while/body/eval_jaxpr/scatter-add | solution.py:27
  271.7 6.5 %convert_element_type.8 = bf16[128,128,256]{2,1,0:T(8,128)(2,1)S(1)} convert(f32[128,128,256]{2,1,0:T(8,128)} %get-tuple-element.111) | non-fusion elementwise | flops 4194304 | bytes 25165824 | tf_op jit(solution)/shard_map/convert_element_type | solution.py:32
  278.3 104.3 %all_to_all.5 = bf16[32,512,256]{2,1,0:T(8,128)(2,1)} all-to-all(bf16[32,512,256]{2,1,0:T(8,128)(2,1)S(1)} %bitcast.37), channel_id=1, replica_groups=mesh['row'=32,'rep'=4] {'row'}, dimensions={0} | all-to-all | bytes 16777216 | tf_op jit(solution)/shard_map/all_to_all | solution.py:35
  382.5 4.7 reduce_sum.12
  389.3 138.4 %all-reduce.2.cloned.1.call-done = f32[256,256]{0,1:T(8,128)} async-done(((f32[256,256]{0,1:T(8,128)}), f32[256,256]{0,1:T(8,128)}) %all-reduce.2.cloned.1.call-update) | async-done | bytes 262160 | tf_op jit(solution)/shard_map/psum | solution.py:39
  (53 shorter events, 35.2 us)
Async XLA Ops:
  7.2 380.1 %copy-start = (bf16[512,256]{1,0:T(8,128)(2,1)S(1)}, bf16[512,256]{1,0:T(8,128)(2,1)}, u32[]{:S(2)}) copy-start(bf16[512,256]{1,0:T(8,128)(2,1)} %param.11) | copy-start | bytes 786436
  7.2 29.4 %all-gather.2.cloned.1.call-start = ((), (), s32[]{:S(2)}) async-start(), calls=%async_computation.1 | async-start | bytes 1310720 | tf_op jit(solution)/shard_map/all_gather | solution.py:9
  9.0 518.6 %all-reduce.2.cloned.1.call-start = ((), (), s32[]{:S(2)}) async-start(), calls=%async_computation.2 | async-start | bytes 524288 | tf_op jit(solution)/shard_map/psum | solution.py:39
  278.3 110.0 %copy-start.1 = (bf16[256,256]{1,0:T(8,128)(2,1)S(1)}, bf16[256,256]{1,0:T(8,128)(2,1)}, u32[]{:S(2)}) copy-start(bf16[256,256]{1,0:T(8,128)(2,1)} %param.12) | copy-start | bytes 393220
Sparse Core Ops, SparseCore 0:
  10.3 26.2 all-gather.1
  388.4 139.2 all-reduce.1
where the time goes:
time: 537 us; the launch traced here: 536 us
  other arithmetic  178 us (33%)
  waiting for transfers between devices  164 us (31%)
  blocking collectives  104 us (19%)
  matrix products  65.6 us (12%)
  between operations  14.1 us (3%)
  local copies, waits for them, and re-layouts  9.77 us (2%)
    scatter-add x16, other arithmetic, row_step(): return partial_value.at[local_index[index]].add(messages)  163 us
    psum x1, waiting for transfers between devices, body(): grad_weight = lax.psum(weight_term, ('row', 'rep'))  138 us
    all_to_all x1, blocking collectives, body(): lax.all_to_all(outgoing, 'row', split_axis=0, concat_axis=0, tiled=True)  104 us
    dot_general x16, matrix products, row_step(): jnp.einsum('sij,if->sjf', adj_values[index], grad_blocks[index], preferre...  63.6 us
    all_gather x1, waiting for transfers between devices, body(): grad_pre = lax.all_gather(masked_local, 'rep', axis=0, tiled=True)  26 us
  transfers between devices with their start and end apart: 2, of which 2 were waited for; matrix products, arithmetic and copies ran while one was open for 0% of the time, Pallas kernels for 0%

commit v1 on v0

v1 whole, which is shorter than its diff:
```python
import functools

import jax
import jax.numpy as jnp
import numpy as np
from jax import lax
from jax.experimental import pallas as pl
from jax.experimental.pallas import tpu as pltpu
from jax.sharding import PartitionSpec as P

AXES = ("row", "rep")
RING = 4
BLOCK = 128
FEAT = 256
SHARE_BLOCKS = 4
ROWBLK = 16
SLOTS = 32
CALLS = 8
CALL_SLOTS = 16
MAX_PAIRS = 128
UNROLL = 4
NO_BLOCK = ROWBLK << 9

FLIP = {"x0": ("x", 1), "x1": ("x", 3), "z0": ("z", 1), "z1": ("z", 3), "y0": ("y", 1), "y1": ("y", 3)}
ORDER = (
    (("x0", "z0", "x1", "z1"), ("z0", "x0", "z1", "x1")),
    (("x1", "z1", "x0", "z0"), ("z1", "x1", "z0", "x0")),
)


def linear(z, x, c, y):
    return ((z * RING + x) * 2 + c) * RING + y


def exchange_pairs(first, second):
    pairs = []
    for z in range(RING):
        for x in range(RING):
            for c in range(2):
                for y in range(RING):
                    at = {"z": z, "x": x, "c": c, "y": y}
                    axis, mask = FLIP[first if c == 0 else second]
                    at[axis] ^= mask
                    pairs.append((linear(z, x, c, y), linear(**at)))
    return pairs


def exchange(value, first, second):
    return lax.ppermute(value, AXES, exchange_pairs(first, second))


def swap_cores(value):
    pairs = [(d, d ^ RING) for d in range(RING * RING * 2 * RING)]
    return lax.ppermute(value, AXES, pairs)


def target_flips():
    out = np.zeros((2, 2, 16, 2), np.int32)
    for part in range(2):
        for core in range(2):
            for place in range(16):
                for bit, dim in enumerate(ORDER[part][core]):
                    if place >> (3 - bit) & 1:
                        axis, mask = FLIP[dim]
                        out[part, core, place, 0 if axis == "z" else 1] ^= mask
    return out


def plan(adj_cols, adj_counts, z, x, c, y):
    flips = jnp.asarray(target_flips())
    cores = jnp.stack([c, 1 - c])
    chosen = jnp.where(cores[None, :, None, None] == 0, flips[:, 0][:, None], flips[:, 1][:, None])
    group = ((z ^ chosen[..., 0]) * RING + (x ^ chosen[..., 1])) * 2 + cores[None, :, None]
    base = group * ROWBLK + y * SHARE_BLOCKS + jnp.arange(2, dtype=jnp.int32)[:, None, None] * 2
    target = base[..., None] + jnp.arange(2, dtype=jnp.int32)
    target = target.reshape(CALLS, CALL_SLOTS)

    slot = jnp.arange(SLOTS, dtype=jnp.int32)
    cols = jnp.where(slot[None, :] < adj_counts, adj_cols, -1)
    hit = target[:, :, None, None] == cols
    found = jnp.sum(jnp.where(hit, slot + 1, 0), axis=-1)
    present = (found > 0).astype(jnp.int32)
    row = jnp.arange(ROWBLK, dtype=jnp.int32)
    before = row[:, None] < row[None, :]
    place = jnp.sum(jnp.where(before, present[..., :, None], 0), axis=-2)
    pairs = jnp.maximum((jnp.sum(present, axis=-1) + 1) // 2, 1)
    start = jnp.sum(jnp.where(before, pairs[..., :, None], 0), axis=-2)
    key = jnp.where(present > 0, (start[..., None] + place // 2) * 2 + place % 2, -1)
    step = (row // SHARE_BLOCKS) ^ y
    first = jnp.where(c == 0, 1, 3)
    rel = jnp.where(step == 0, 0, jnp.where(step == first, 1, jnp.where(step == 2, 3, 2)))
    grad = rel * SHARE_BLOCKS + row % SHARE_BLOCKS
    code = row * SLOTS + found - 1 + (grad << 9) - NO_BLOCK
    position = jnp.arange(2 * MAX_PAIRS, dtype=jnp.int32)
    take = key.reshape(CALLS, 1, -1) == position[:, None]
    flat = jnp.sum(jnp.where(take, code.reshape(CALLS, 1, -1), 0), axis=-1) + NO_BLOCK
    pair = jnp.arange(MAX_PAIRS, dtype=jnp.int32)[:, None]
    ended = jnp.sum(((start + pairs)[:, None, :] <= pair).astype(jnp.int32), axis=-1)
    opens = jnp.sum((start[:, None, :] == pair).astype(jnp.int32), axis=-1)
    meta = (jnp.minimum(ended, CALL_SLOTS - 1) + opens * CALL_SLOTS) << 14
    words = flat.reshape(CALLS, MAX_PAIRS, 2) + jnp.stack([meta, jnp.zeros_like(meta)], axis=-1)
    totals = jnp.sum(pairs, axis=-1)
    return words.reshape(-1), totals


def mask_kernel(grad_ref, preact_ref, out_ref):
    for b in range(SHARE_BLOCKS):
        rows = pl.ds(b * BLOCK, BLOCK)
        grad = grad_ref[rows, :].astype(jnp.float32)
        kept = jnp.where(preact_ref[rows, :].astype(jnp.float32) > 0, grad, 0.0)
        out_ref[b] = kept.T.astype(jnp.bfloat16)


def mask(grad_out, preact):
    return pl.pallas_call(
        mask_kernel,
        out_shape=jax.ShapeDtypeStruct((SHARE_BLOCKS, FEAT, BLOCK), jnp.bfloat16),
        compiler_params=pltpu.CompilerParams(vmem_limit_bytes=4 << 20),
        name="masked_gradient",
    )(grad_out, preact)


def products_kernel(call, words_ref, totals_ref, grad_ref, adj_ref, out_ref):
    base = call * 2 * MAX_PAIRS

    def pair(p, acc):
        w0 = words_ref[base + 2 * p]
        w1 = words_ref[base + 2 * p + 1]
        slot = (w0 >> 14) & (CALL_SLOTS - 1)
        keep = jnp.where((w0 >> 18) == 0, 1.0, 0.0).astype(jnp.float32)
        lhs = jnp.concatenate([grad_ref[(w0 >> 9) & 31], grad_ref[(w1 >> 9) & 31]], axis=1)
        rhs = jnp.concatenate([adj_ref[w0 & 511], adj_ref[w1 & 511]], axis=0)
        acc = acc * keep + jnp.dot(lhs, rhs, preferred_element_type=jnp.float32)
        out_ref[slot] = acc.astype(jnp.bfloat16)
        return acc

    def steps(i, acc):
        for u in range(UNROLL):
            acc = pair(i * UNROLL + u, acc)
        return acc

    count = (totals_ref[call] + UNROLL - 1) // UNROLL
    lax.fori_loop(0, count, steps, jnp.zeros((FEAT, BLOCK), jnp.float32))


def products(call, words, totals, grad_t, adj):
    smem = pl.BlockSpec(memory_space=pltpu.SMEM)
    vmem = pl.BlockSpec(memory_space=pltpu.VMEM)
    return pl.pallas_call(
        functools.partial(products_kernel, call),
        out_shape=pltpu.VMEM((CALL_SLOTS, FEAT, BLOCK), jnp.bfloat16),
        in_specs=[smem, smem, vmem, vmem],
        out_specs=vmem,
        cost_estimate=pl.CostEstimate(flops=2 * 48 * 2 * BLOCK * BLOCK * FEAT, bytes_accessed=6 << 20, transcendentals=0),
        compiler_params=pltpu.CompilerParams(vmem_limit_bytes=4 << 20),
        name=f"products_{call}",
    )(
        words,
        totals,
        pltpu.with_memory_space_constraint(grad_t, pltpu.VMEM),
        pltpu.with_memory_space_constraint(adj, pltpu.VMEM),
    )


def add(a, b):
    return (a.astype(jnp.float32) + b.astype(jnp.float32)).astype(jnp.bfloat16)


def body(grad_out, preact, features, weight, adj_values, adj_cols, adj_counts):
    row, y = lax.axis_index("row"), lax.axis_index("rep")
    z, x, c = row // (2 * RING), row // 2 % RING, row % 2

    own = mask(grad_out, preact)
    words, totals = plan(adj_cols, adj_counts, z, x, c, y)
    adj = adj_values.reshape(ROWBLK * SLOTS, BLOCK, BLOCK)

    half = jnp.concatenate([own, exchange(own, "y0", "y1")])
    rest = exchange(half, "y1", "y0")
    grad_t = jnp.concatenate([half, rest, jnp.zeros((1, FEAT, BLOCK), jnp.bfloat16)])

    def product(part, sent, upper):
        return products(part * 4 + sent * 2 + upper, words, totals, grad_t, adj)

    sums = {}
    for upper in (1, 0):
        for part in (0, 1):
            sent = swap_cores(product(part, 1, upper))
            sums[part, upper] = add(product(part, 0, upper), sent)

    parts = []
    for part in (0, 1):
        lower, upper = sums[part, 0], sums[part, 1]
        for step in range(4):
            got = exchange(upper, ORDER[part][0][step], ORDER[part][1][step])
            value = add(lower, got)
            n = value.shape[0] // 2
            if step < 3:
                lower, upper = value[:n], value[n:]
        parts.append(value)
    grad_agg_t = jnp.concatenate(parts)

    feat = features.reshape(SHARE_BLOCKS, BLOCK, FEAT)
    term = jnp.einsum("bfn,bnc->cf", grad_agg_t, feat, preferred_element_type=jnp.float32)
    n = FEAT // 2
    mine = lax.dynamic_slice(term, (c * n, 0), (n, FEAT))
    other = lax.dynamic_slice(term, ((1 - c) * n, 0), (n, FEAT))
    mine = mine + swap_cores(other)
    for dims in (("x0", "z0"), ("z0", "x0"), ("y0", "x1"), ("x1", "y0"), ("z1", "y1"), ("y1", "z1")):
        mine = mine + exchange(mine, *dims)
    theirs = swap_cores(mine)
    low = jnp.where(c == 0, mine, theirs)
    high = jnp.where(c == 0, theirs, mine)
    grad_weight = jnp.concatenate([low, high])

    grad_features = jnp.einsum("bfn,cf->bnc", grad_agg_t, weight, preferred_element_type=jnp.float32)
    return grad_features.astype(jnp.bfloat16).reshape(features.shape), grad_weight


def solution(mesh):
    placed = (
        P(AXES, None),
        P(AXES, None),
        P(AXES, None),
        P(),
        P("row", "rep", None, None),
        P("row", "rep"),
        P("row", "rep"),
    )
    return jax.shard_map(body, mesh=mesh, in_specs=placed, out_specs=(P(AXES, None), P()), check_vma=False)
```

time: 537 us -> 130 us (0.24)
  other arithmetic: 178 us -> 8.66 us
  waiting for transfers between devices: 164 us -> 47.9 us
  blocking collectives: 104 us -> 0 us
  matrix products: 65.6 us -> 1.25 us
  starting transfers between devices: 0.08 us -> 40.4 us
  Pallas kernels: 0 us -> 20.1 us
  between operations: 14.1 us -> 1.19 us
    scatter-add x16 -> x0, other arithmetic: 163 us -> none  [row_step(): return partial_value.at[local_index[index]].add(messages)]
    psum x1 -> x0, waiting for transfers between devices: 138 us -> none  [body(): grad_weight = lax.psum(weight_term, ('row', 'rep'))]
    all_to_all x1 -> x0, blocking collectives: 104 us -> none  [body(): lax.all_to_all(outgoing, 'row', split_axis=0, concat_axis=0, tiled=True)]
    dot_general x18 -> x2, matrix products: 65.6 us -> 1.25 us  [the longest x1 0.98 us: body(): jnp.einsum('bfn,cf->bnc', grad_agg_t, weight, preferred_element_type=jnp....]
    ppermute x0 -> x22, waiting for transfers between devices: none -> 47.9 us  [the longest x16 46.9 us: exchange(): return lax.ppermute(value, AXES, exchange_pairs(first, second))]
    ppermute x0 -> x22, starting transfers between devices: none -> 40.4 us  [the longest x16 25.6 us: exchange(): return lax.ppermute(value, AXES, exchange_pairs(first, second))]
    all_gather x1 -> x0, waiting for transfers between devices: 26 us -> none  [body(): grad_pre = lax.all_gather(masked_local, 'rep', axis=0, tiled=True)]
    pallas_call x0 -> x9, Pallas kernels: none -> 20.1 us  [the longest x8 19.9 us: products(): pl.pallas_call(functools.partial(products_kernel, call), out_shape=pltpu....]
  transfers between devices with their start and end apart: 2 -> 22, of which waited for: 2 -> 15; matrix products, arithmetic and copies ran while one was open for 0% -> 8% of each run, Pallas kernels for 0% -> 13%
where the time goes in v1:
time: 130 us; the launch traced here: 129 us
  waiting for transfers between devices  47.9 us (37%)
  starting transfers between devices  40.4 us (31%)
  Pallas kernels  20.1 us (15%)
  local copies, waits for them, and re-layouts  9.88 us (8%)
  other arithmetic  8.66 us (7%)
    ppermute x16, waiting for transfers between devices, exchange(): return lax.ppermute(value, AXES, exchange_pairs(first, second))  46.9 us
    ppermute x16, starting transfers between devices, exchange(): return lax.ppermute(value, AXES, exchange_pairs(first, second))  25.6 us
    pallas_call x8, Pallas kernels, products(): pl.pallas_call(functools.partial(products_kernel, call), out_shape=pltpu....  19.9 us
    ppermute x6, starting transfers between devices, swap_cores(): return lax.ppermute(value, AXES, pairs)  14.9 us
    unnamed x18, local copies, waits for them, and re-layouts  7.74 us
  transfers between devices with their start and end apart: 22, of which 15 were waited for; matrix products, arithmetic and copies ran while one was open for 8% of the time, Pallas kernels for 13%

profile of v1, /device:TPU:1, one launch (start us, length us, event | category | flops | bytes accessed | tf_op | source)
XLA Modules:
  0.0 129.4 jit_solution(11747945253498288154)
XLA Ops:
  2.7 3.6 %collective-permute-start = (bf16[4,256,128]{2,1,0:T(8,128)(2,1)S(1)}, bf16[4,256,128]{2,1,0:T(8,128)(2,1)S(1)}, u32[]{:S(2)}, u32[]{:S(2)}) collective-permute-start(bf16[4,256,128]{2,1,0:T(8,128)(2,1)S(1)} %masked_gradient.1), channel_id=1, source_target_pairs={{0,1},{1,0},{2,3},{3,2},{4,7},{5,6},{6,5},{7,4},{8,9},{9,8},{10,11... | collective-permute-start | bytes 786440 | tf_op jit(solution)/shard_map/ppermute | solution.py:49
  8.3 2.4 %select_reduce_fusion.2 = s32[8,16,16]{2,1,0:T(8,128)S(1)} fusion(s32[32]{0:T(128)S(1)} %iota_add_fusion.1, s32[16,32]{1,0:T(8,128)S(1)} %fusion.7, s32[8,16]{1,0:T(8,128)S(1)} %add.295), kind=kLoop, calls=%fused_computation.14 | loop fusion | flops 194560 | bytes 10880 | tf_op jit(solution)/shard_map/reduce_sum | solution.py:81
  14.4 6.4 %collective-permute-done.1 = bf16[8,256,128]{2,1,0:T(8,128)(2,1)S(1)} collective-permute-done((bf16[8,256,128]{2,1,0:T(8,128)(2,1)S(1)}, bf16[8,256,128]{2,1,0:T(8,128)(2,1)S(1)}, u32[]{:S(2)}, u32[]{:S(2)}) %collective-permute-start.1) | collective-permute-done | bytes 524320 | tf_op jit(solution)/shard_map/ppermute | solution.py:49
  20.9 5.8 %copy-done.1 = bf16[16,32,128,128]{3,2,1,0:T(8,128)(2,1)S(1)} copy-done((bf16[16,32,128,128]{3,2,1,0:T(8,128)(2,1)S(1)}, bf16[16,32,128,128]{3,2,1,0:T(8,128)(2,1)}, u32[]{:S(2)}) %copy-start.1) | copy-done | bytes 16777240
  26.7 2.7 %products_3.1 = bf16[16,256,128]{2,1,0:T(8,128)(2,1)S(1)} custom-call(s32[2048]{0:T(1024)S(1)} %reshape.256.words_ref, s32[8]{0:T(128)S(1)} %get-tuple-element.2.totals_ref, bf16[17,256,128]{2,1,0:T(8,128)(2,1)S(1)} %maximum_maximum_fusion.grad_ref, bf16[512,128,128]{2,1,0:T(8,128)(2,1)S(1)} %bitcast.25), custom_call_target="tpu_custom_call" | custom-call | flops 805306368 | bytes 6291456 | tf_op jit(solution)/shard_map/products_3/pallas_call | solution.py:149
  30.8 2.4 %products_7.1 = bf16[16,256,128]{2,1,0:T(8,128)(2,1)S(1)} custom-call(s32[2048]{0:T(1024)S(1)} %reshape.256.words_ref, s32[8]{0:T(128)S(1)} %get-tuple-element.2.totals_ref, bf16[17,256,128]{2,1,0:T(8,128)(2,1)S(1)} %maximum_maximum_fusion.grad_ref, bf16[512,128,128]{2,1,0:T(8,128)(2,1)S(1)} %bitcast.26), custom_call_target="tpu_custom_call" | custom-call | flops 805306368 | bytes 6291456 | tf_op jit(solution)/shard_map/products_7/pallas_call | solution.py:149
  33.3 2.4 %products_2.1 = bf16[16,256,128]{2,1,0:T(8,128)(2,1)S(1)} custom-call(s32[2048]{0:T(1024)S(1)} %reshape.256.words_ref, s32[8]{0:T(128)S(1)} %get-tuple-element.2.totals_ref, bf16[17,256,128]{2,1,0:T(8,128)(2,1)S(1)} %maximum_maximum_fusion.grad_ref, bf16[512,128,128]{2,1,0:T(8,128)(2,1)S(1)} %bitcast.27), custom_call_target="tpu_custom_call" | custom-call | flops 805306368 | bytes 6291456 | tf_op jit(solution)/shard_map/products_2/pallas_call | solution.py:149
  36.0 2.4 %products_1.1 = bf16[16,256,128]{2,1,0:T(8,128)(2,1)S(1)} custom-call(s32[2048]{0:T(1024)S(1)} %reshape.256.words_ref, s32[8]{0:T(128)S(1)} %get-tuple-element.2.totals_ref, bf16[17,256,128]{2,1,0:T(8,128)(2,1)S(1)} %maximum_maximum_fusion.grad_ref, bf16[512,128,128]{2,1,0:T(8,128)(2,1)S(1)} %bitcast.28), custom_call_target="tpu_custom_call" | custom-call | flops 805306368 | bytes 6291456 | tf_op jit(solution)/shard_map/products_1/pallas_call | solution.py:149
  38.5 2.4 %products_5.1 = bf16[16,256,128]{2,1,0:T(8,128)(2,1)S(1)} custom-call(s32[2048]{0:T(1024)S(1)} %reshape.256.words_ref, s32[8]{0:T(128)S(1)} %get-tuple-element.2.totals_ref, bf16[17,256,128]{2,1,0:T(8,128)(2,1)S(1)} %maximum_maximum_fusion.grad_ref, bf16[512,128,128]{2,1,0:T(8,128)(2,1)S(1)} %bitcast.29), custom_call_target="tpu_custom_call" | custom-call | flops 805306368 | bytes 6291456 | tf_op jit(solution)/shard_map/products_5/pallas_call | solution.py:149
  41.2 2.0 %collective-permute-start.4 = (bf16[16,256,128]{2,1,0:T(8,128)(2,1)S(1)}, bf16[16,256,128]{2,1,0:T(8,128)(2,1)S(1)}, u32[]{:S(2)}, u32[]{:S(2)}) collective-permute-start(bf16[16,256,128]{2,1,0:T(8,128)(2,1)S(1)} %add_convert_fusion.4), channel_id=1, source_target_pairs={{0,8},{1,9},{2,10},{3,11},{4,36},{5,37},{6,38},{7,39},{8,0},{9,1},... | collective-permute-start | bytes 3145736 | tf_op jit(solution)/shard_map/ppermute | solution.py:49
  43.2 2.7 %products_6.1 = bf16[16,256,128]{2,1,0:T(8,128)(2,1)S(1)} custom-call(s32[2048]{0:T(1024)S(1)} %reshape.256.words_ref, s32[8]{0:T(128)S(1)} %get-tuple-element.2.totals_ref, bf16[17,256,128]{2,1,0:T(8,128)(2,1)S(1)} %maximum_maximum_fusion.grad_ref, bf16[512,128,128]{2,1,0:T(8,128)(2,1)S(1)} %bitcast.32), custom_call_target="tpu_custom_call" | custom-call | flops 805306368 | bytes 6291456 | tf_op jit(solution)/shard_map/products_6/pallas_call | solution.py:149
  46.4 4.2 %collective-permute-start.10 = (bf16[16,256,128]{2,1,0:T(8,128)(2,1)S(1)}, bf16[16,256,128]{2,1,0:T(8,128)(2,1)S(1)}, u32[]{:S(2)}, u32[]{:S(2)}) collective-permute-start(bf16[16,256,128]{2,1,0:T(8,128)(2,1)S(1)} %add_convert_fusion.1), channel_id=1, source_target_pairs={{0,24},{1,25},{2,26},{3,27},{4,100},{5,101},{6,102},{7,103},{8,16}... | collective-permute-start | bytes 3145736 | tf_op jit(solution)/shard_map/ppermute | solution.py:49
  50.6 2.7 %products_0.1 = bf16[16,256,128]{2,1,0:T(8,128)(2,1)S(1)} custom-call(s32[2048]{0:T(1024)S(1)} %reshape.256.words_ref, s32[8]{0:T(128)S(1)} %get-tuple-element.2.totals_ref, bf16[17,256,128]{2,1,0:T(8,128)(2,1)S(1)} %maximum_maximum_fusion.grad_ref, bf16[512,128,128]{2,1,0:T(8,128)(2,1)S(1)} %bitcast.33), custom_call_target="tpu_custom_call" | custom-call | flops 805306368 | bytes 6291456 | tf_op jit(solution)/shard_map/products_0/pallas_call | solution.py:149
  53.3 2.1 %products_4.1 = bf16[16,256,128]{2,1,0:T(8,128)(2,1)S(1)} custom-call(s32[2048]{0:T(1024)S(1)} %reshape.256.words_ref, s32[8]{0:T(128)S(1)} %get-tuple-element.2.totals_ref, bf16[17,256,128]{2,1,0:T(8,128)(2,1)S(1)} %maximum_maximum_fusion.grad_ref, bf16[512,128,128]{2,1,0:T(8,128)(2,1)S(1)} %bitcast.34), custom_call_target="tpu_custom_call" | custom-call | flops 805306368 | bytes 6291456 | tf_op jit(solution)/shard_map/products_4/pallas_call | solution.py:149
  56.1 1.9 %collective-permute-start.5 = (bf16[8,256,128]{2,1,0:T(8,128)(2,1)S(1)}, bf16[8,256,128]{2,1,0:T(8,128)(2,1)S(1)}, u32[]{:S(2)}, u32[]{:S(2)}) collective-permute-start(bf16[8,256,128]{2,1,0:T(8,128)(2,1)S(1)} %slice.67), channel_id=1, source_target_pairs={{0,32},{1,33},{2,34},{3,35},{4,12},{5,13},{6,14},{7,15},{8,40},{9,... | collective-permute-start | bytes 1572872 | tf_op jit(solution)/shard_map/ppermute | solution.py:49
  58.0 4.8 %collective-permute-done.10 = bf16[16,256,128]{2,1,0:T(8,128)(2,1)S(1)} collective-permute-done((bf16[16,256,128]{2,1,0:T(8,128)(2,1)S(1)}, bf16[16,256,128]{2,1,0:T(8,128)(2,1)S(1)}, u32[]{:S(2)}, u32[]{:S(2)}) %collective-permute-start.10) | collective-permute-done | bytes 1048608 | tf_op jit(solution)/shard_map/ppermute | solution.py:49
  63.2 1.6 %collective-permute-start.11 = (bf16[8,256,128]{2,1,0:T(8,128)(2,1)S(1)}, bf16[8,256,128]{2,1,0:T(8,128)(2,1)S(1)}, u32[]{:S(2)}, u32[]{:S(2)}) collective-permute-start(bf16[8,256,128]{2,1,0:T(8,128)(2,1)S(1)} %slice.73), channel_id=1, source_target_pairs={{0,96},{1,97},{2,98},{3,99},{4,28},{5,29},{6,30},{7,31},{8,104},{9... | collective-permute-start | bytes 1572872 | tf_op jit(solution)/shard_map/ppermute | solution.py:49
  65.0 4.4 %collective-permute-start.6 = (bf16[4,256,128]{2,1,0:T(8,128)(2,1)S(1)}, bf16[4,256,128]{2,1,0:T(8,128)(2,1)S(1)}, u32[]{:S(2)}, u32[]{:S(2)}) collective-permute-start(bf16[4,256,128]{2,1,0:T(8,128)(2,1)S(1)} %slice.69), channel_id=1, source_target_pairs={{0,24},{1,25},{2,26},{3,27},{4,100},{5,101},{6,102},{7,103},{8,16}... | collective-permute-start | bytes 786440 | tf_op jit(solution)/shard_map/ppermute | solution.py:49
  69.5 3.9 %collective-permute-done.11 = bf16[8,256,128]{2,1,0:T(8,128)(2,1)S(1)} collective-permute-done((bf16[8,256,128]{2,1,0:T(8,128)(2,1)S(1)}, bf16[8,256,128]{2,1,0:T(8,128)(2,1)S(1)}, u32[]{:S(2)}, u32[]{:S(2)}) %collective-permute-start.11) | collective-permute-done | bytes 524320 | tf_op jit(solution)/shard_map/ppermute | solution.py:49
  73.7 2.7 %collective-permute-done.6 = bf16[4,256,128]{2,1,0:T(8,128)(2,1)S(1)} collective-permute-done((bf16[4,256,128]{2,1,0:T(8,128)(2,1)S(1)}, bf16[4,256,128]{2,1,0:T(8,128)(2,1)S(1)}, u32[]{:S(2)}, u32[]{:S(2)}) %collective-permute-start.6) | collective-permute-done | bytes 262176 | tf_op jit(solution)/shard_map/ppermute | solution.py:49
  79.1 2.5 %collective-permute-done.7 = bf16[2,256,128]{2,1,0:T(8,128)(2,1)S(1)} collective-permute-done((bf16[2,256,128]{2,1,0:T(8,128)(2,1)S(1)}, bf16[2,256,128]{2,1,0:T(8,128)(2,1)S(1)}, u32[]{:S(2)}, u32[]{:S(2)}) %collective-permute-start.7) | collective-permute-done | bytes 131104 | tf_op jit(solution)/shard_map/ppermute | solution.py:49
  81.6 2.9 %collective-permute-done.13 = bf16[2,256,128]{2,1,0:T(8,128)(2,1)S(1)} collective-permute-done((bf16[2,256,128]{2,1,0:T(8,128)(2,1)S(1)}, bf16[2,256,128]{2,1,0:T(8,128)(2,1)S(1)}, u32[]{:S(2)}, u32[]{:S(2)}) %collective-permute-start.13) | collective-permute-done | bytes 131104 | tf_op jit(solution)/shard_map/ppermute | solution.py:49
  84.9 6.1 %collective-permute-start.14 = (f32[128,256]{1,0:T(8,128)S(1)}, f32[128,256]{1,0:T(8,128)S(1)}, u32[]{:S(2)}, u32[]{:S(2)}) collective-permute-start(f32[128,256]{1,0:T(8,128)S(1)} %dynamic-slice_bitcast_fusion), channel_id=1, source_target_pairs={{0,4},{1,5},{2,6},{3,7},{4,0},{5,1},{6,2},{7,3},{8,12},{9,13},{10,... | collective-permute-start | bytes 393224 | tf_op jit(solution)/shard_map/ppermute | solution.py:54
  92.1 4.1 %collective-permute-done.15 = f32[128,256]{1,0:T(8,128)S(1)} collective-permute-done((f32[128,256]{1,0:T(8,128)S(1)}, f32[128,256]{1,0:T(8,128)S(1)}, u32[]{:S(2)}, u32[]{:S(2)}) %collective-permute-start.15) | collective-permute-done | bytes 131104 | tf_op jit(solution)/shard_map/ppermute | solution.py:49
  96.3 3.8 %collective-permute-done.16 = f32[128,256]{1,0:T(8,128)S(1)} collective-permute-done((f32[128,256]{1,0:T(8,128)S(1)}, f32[128,256]{1,0:T(8,128)S(1)}, u32[]{:S(2)}, u32[]{:S(2)}) %collective-permute-start.16) | collective-permute-done | bytes 131104 | tf_op jit(solution)/shard_map/ppermute | solution.py:49
  100.2 1.6 %collective-permute-start.17 = (f32[128,256]{1,0:T(8,128)S(1)}, f32[128,256]{1,0:T(8,128)S(1)}, u32[]{:S(2)}, u32[]{:S(2)}) collective-permute-start(f32[128,256]{1,0:T(8,128)S(1)} %add.336), channel_id=1, source_target_pairs={{0,1},{1,0},{2,3},{3,2},{4,28},{5,29},{6,30},{7,31},{8,9},{9,8},{1... | collective-permute-start | bytes 393224 | tf_op jit(solution)/shard_map/ppermute | solution.py:49
  101.8 3.5 %collective-permute-done.17 = f32[128,256]{1,0:T(8,128)S(1)} collective-permute-done((f32[128,256]{1,0:T(8,128)S(1)}, f32[128,256]{1,0:T(8,128)S(1)}, u32[]{:S(2)}, u32[]{:S(2)}) %collective-permute-start.17) | collective-permute-done | bytes 131104 | tf_op jit(solution)/shard_map/ppermute | solution.py:49
  105.4 3.8 %collective-permute-done.18 = f32[128,256]{1,0:T(8,128)S(1)} collective-permute-done((f32[128,256]{1,0:T(8,128)S(1)}, f32[128,256]{1,0:T(8,128)S(1)}, u32[]{:S(2)}, u32[]{:S(2)}) %collective-permute-start.18) | collective-permute-done | bytes 131104 | tf_op jit(solution)/shard_map/ppermute | solution.py:49
  110.6 3.7 %collective-permute-done.19 = f32[128,256]{1,0:T(8,128)S(1)} collective-permute-done((f32[128,256]{1,0:T(8,128)S(1)}, f32[128,256]{1,0:T(8,128)S(1)}, u32[]{:S(2)}, u32[]{:S(2)}) %collective-permute-start.19) | collective-permute-done | bytes 131104 | tf_op jit(solution)/shard_map/ppermute | solution.py:49
  114.3 3.0 %collective-permute-start.20 = (f32[128,256]{1,0:T(8,128)S(1)}, f32[128,256]{1,0:T(8,128)S(1)}, u32[]{:S(2)}, u32[]{:S(2)}) collective-permute-start(f32[128,256]{1,0:T(8,128)S(1)} %add.339), channel_id=1, source_target_pairs={{0,3},{1,2},{2,1},{3,0},{4,100},{5,101},{6,102},{7,103},{8,11},{9,... | collective-permute-start | bytes 393224 | tf_op jit(solution)/shard_map/ppermute | solution.py:49
  117.4 3.5 %collective-permute-done.20 = f32[128,256]{1,0:T(8,128)S(1)} collective-permute-done((f32[128,256]{1,0:T(8,128)S(1)}, f32[128,256]{1,0:T(8,128)S(1)}, u32[]{:S(2)}, u32[]{:S(2)}) %collective-permute-start.20) | collective-permute-done | bytes 131104 | tf_op jit(solution)/shard_map/ppermute | solution.py:49
  120.9 6.8 %collective-permute-start.21 = (f32[128,256]{1,0:T(8,128)S(1)}, f32[128,256]{1,0:T(8,128)S(1)}, u32[]{:S(2)}, u32[]{:S(2)}) collective-permute-start(f32[128,256]{1,0:T(8,128)S(1)} %add.340), channel_id=1, source_target_pairs={{0,4},{1,5},{2,6},{3,7},{4,0},{5,1},{6,2},{7,3},{8,12},{9,13},{10,... | collective-permute-start | bytes 393224 | tf_op jit(solution)/shard_map/ppermute | solution.py:54
  (107 shorter events, 19.3 us)
Async XLA Ops:
  0.6 84.0 %copy-start = (bf16[512,256]{1,0:T(8,128)(2,1)S(1)}, bf16[512,256]{1,0:T(8,128)(2,1)}, u32[]{:S(2)}) copy-start(bf16[512,256]{1,0:T(8,128)(2,1)} %param.10) | copy-start | bytes 786436
  0.6 1.0 copy-start.2
  1.6 0.9 copy-start.3
  2.7 9.5 %collective-permute-start = (bf16[4,256,128]{2,1,0:T(8,128)(2,1)S(1)}, bf16[4,256,128]{2,1,0:T(8,128)(2,1)S(1)}, u32[]{:S(2)}, u32[]{:S(2)}) collective-permute-start(bf16[4,256,128]{2,1,0:T(8,128)(2,1)S(1)} %masked_gradient.1), channel_id=1, source_target_pairs={{0,1},{1,0},{2,3},{3,2},{4,7},{5,6},{6,5},{7,4},{8,9},{9,8},{10,11... | collective-permute-start | bytes 786440 | tf_op jit(solution)/shard_map/ppermute | solution.py:49
  12.3 8.4 %collective-permute-start.1 = (bf16[8,256,128]{2,1,0:T(8,128)(2,1)S(1)}, bf16[8,256,128]{2,1,0:T(8,128)(2,1)S(1)}, u32[]{:S(2)}, u32[]{:S(2)}) collective-permute-start(bf16[8,256,128]{2,1,0:T(8,128)(2,1)S(1)} %pad_maximum_fusion), channel_id=1, source_target_pairs={{0,3},{1,2},{2,1},{3,0},{4,5},{5,4},{6,7},{7,6},{8,11},{9,10},{10,... | collective-permute-start | bytes 1572872 | tf_op jit(solution)/shard_map/ppermute | solution.py:49
  20.9 5.8 %copy-start.1 = (bf16[16,32,128,128]{3,2,1,0:T(8,128)(2,1)S(1)}, bf16[16,32,128,128]{3,2,1,0:T(8,128)(2,1)}, u32[]{:S(2)}) copy-start(bf16[16,32,128,128]{3,2,1,0:T(8,128)(2,1)} %param.12) | copy-start | bytes 50331652
  29.4 11.5 %collective-permute-start.3 = (bf16[16,256,128]{2,1,0:T(8,128)(2,1)S(1)}, bf16[16,256,128]{2,1,0:T(8,128)(2,1)S(1)}, u32[]{:S(2)}, u32[]{:S(2)}) collective-permute-start(bf16[16,256,128]{2,1,0:T(8,128)(2,1)S(1)} %products_3.1), channel_id=1, source_target_pairs={{0,4},{1,5},{2,6},{3,7},{4,0},{5,1},{6,2},{7,3},{8,12},{9,13},{10,... | collective-permute-start | bytes 3145736 | tf_op jit(solution)/shard_map/ppermute | solution.py:54
  33.2 12.9 %collective-permute-start.9 = (bf16[16,256,128]{2,1,0:T(8,128)(2,1)S(1)}, bf16[16,256,128]{2,1,0:T(8,128)(2,1)S(1)}, u32[]{:S(2)}, u32[]{:S(2)}) collective-permute-start(bf16[16,256,128]{2,1,0:T(8,128)(2,1)S(1)} %products_7.1), channel_id=1, source_target_pairs={{0,4},{1,5},{2,6},{3,7},{4,0},{5,1},{6,2},{7,3},{8,12},{9,13},{10,... | collective-permute-start | bytes 3145736 | tf_op jit(solution)/shard_map/ppermute | solution.py:54
  35.7 19.7 %collective-permute-start.2 = (bf16[16,256,128]{2,1,0:T(8,128)(2,1)S(1)}, bf16[16,256,128]{2,1,0:T(8,128)(2,1)S(1)}, u32[]{:S(2)}, u32[]{:S(2)}) collective-permute-start(bf16[16,256,128]{2,1,0:T(8,128)(2,1)S(1)} %products_2.1), channel_id=1, source_target_pairs={{0,4},{1,5},{2,6},{3,7},{4,0},{5,1},{6,2},{7,3},{8,12},{9,13},{10,... | collective-permute-start | bytes 3145736 | tf_op jit(solution)/shard_map/ppermute | solution.py:54
  36.0 7.2 %slice-start = ((s8[16777216]{0:T(1024)(128)(4,1)}), s8[4194304]{0:T(1024)(128)(4,1)S(1)}, s32[]{:S(2)}) async-start(s8[16777216]{0:T(1024)(128)(4,1)} %bitcast.30), calls=%async_computation | async-start | bytes 8388608
  36.0 7.2 %slice-start.1 = ((s8[16777216]{0:T(1024)(128)(4,1)}), s8[4194304]{0:T(1024)(128)(4,1)S(1)}, s32[]{:S(2)}) async-start(s8[16777216]{0:T(1024)(128)(4,1)} %bitcast.30), calls=%async_computation.1 | async-start | bytes 8388608
  38.4 4.7 %slice-start.2 = ((s8[16777216]{0:T(1024)(128)(4,1)}), s8[4194304]{0:T(1024)(128)(4,1)S(1)}, s32[]{:S(2)}) async-start(s8[16777216]{0:T(1024)(128)(4,1)} %bitcast.30), calls=%async_computation.2 | async-start | bytes 8388608
  38.4 4.7 %slice-start.3 = ((s8[16777216]{0:T(1024)(128)(4,1)}), s8[4194304]{0:T(1024)(128)(4,1)S(1)}, s32[]{:S(2)}) async-start(s8[16777216]{0:T(1024)(128)(4,1)} %bitcast.30), calls=%async_computation.3 | async-start | bytes 8388608
  41.2 14.5 %collective-permute-start.4 = (bf16[16,256,128]{2,1,0:T(8,128)(2,1)S(1)}, bf16[16,256,128]{2,1,0:T(8,128)(2,1)S(1)}, u32[]{:S(2)}, u32[]{:S(2)}) collective-permute-start(bf16[16,256,128]{2,1,0:T(8,128)(2,1)S(1)} %add_convert_fusion.4), channel_id=1, source_target_pairs={{0,8},{1,9},{2,10},{3,11},{4,36},{5,37},{6,38},{7,39},{8,0},{9,1},... | collective-permute-start | bytes 3145736 | tf_op jit(solution)/shard_map/ppermute | solution.py:49
  45.9 12.1 %collective-permute-start.8 = (bf16[16,256,128]{2,1,0:T(8,128)(2,1)S(1)}, bf16[16,256,128]{2,1,0:T(8,128)(2,1)S(1)}, u32[]{:S(2)}, u32[]{:S(2)}) collective-permute-start(bf16[16,256,128]{2,1,0:T(8,128)(2,1)S(1)} %products_6.1), channel_id=1, source_target_pairs={{0,4},{1,5},{2,6},{3,7},{4,0},{5,1},{6,2},{7,3},{8,12},{9,13},{10,... | collective-permute-start | bytes 3145736 | tf_op jit(solution)/shard_map/ppermute | solution.py:54
  46.4 16.3 %collective-permute-start.10 = (bf16[16,256,128]{2,1,0:T(8,128)(2,1)S(1)}, bf16[16,256,128]{2,1,0:T(8,128)(2,1)S(1)}, u32[]{:S(2)}, u32[]{:S(2)}) collective-permute-start(bf16[16,256,128]{2,1,0:T(8,128)(2,1)S(1)} %add_convert_fusion.1), channel_id=1, source_target_pairs={{0,24},{1,25},{2,26},{3,27},{4,100},{5,101},{6,102},{7,103},{8,16}... | collective-permute-start | bytes 3145736 | tf_op jit(solution)/shard_map/ppermute | solution.py:49
  56.1 8.7 %collective-permute-start.5 = (bf16[8,256,128]{2,1,0:T(8,128)(2,1)S(1)}, bf16[8,256,128]{2,1,0:T(8,128)(2,1)S(1)}, u32[]{:S(2)}, u32[]{:S(2)}) collective-permute-start(bf16[8,256,128]{2,1,0:T(8,128)(2,1)S(1)} %slice.67), channel_id=1, source_target_pairs={{0,32},{1,33},{2,34},{3,35},{4,12},{5,13},{6,14},{7,15},{8,40},{9,... | collective-permute-start | bytes 1572872 | tf_op jit(solution)/shard_map/ppermute | solution.py:49
  63.2 10.1 %collective-permute-start.11 = (bf16[8,256,128]{2,1,0:T(8,128)(2,1)S(1)}, bf16[8,256,128]{2,1,0:T(8,128)(2,1)S(1)}, u32[]{:S(2)}, u32[]{:S(2)}) collective-permute-start(bf16[8,256,128]{2,1,0:T(8,128)(2,1)S(1)} %slice.73), channel_id=1, source_target_pairs={{0,96},{1,97},{2,98},{3,99},{4,28},{5,29},{6,30},{7,31},{8,104},{9... | collective-permute-start | bytes 1572872 | tf_op jit(solution)/shard_map/ppermute | solution.py:49
  65.0 11.3 %collective-permute-start.6 = (bf16[4,256,128]{2,1,0:T(8,128)(2,1)S(1)}, bf16[4,256,128]{2,1,0:T(8,128)(2,1)S(1)}, u32[]{:S(2)}, u32[]{:S(2)}) collective-permute-start(bf16[4,256,128]{2,1,0:T(8,128)(2,1)S(1)} %slice.69), channel_id=1, source_target_pairs={{0,24},{1,25},{2,26},{3,27},{4,100},{5,101},{6,102},{7,103},{8,16}... | collective-permute-start | bytes 786440 | tf_op jit(solution)/shard_map/ppermute | solution.py:49
  73.6 5.3 %collective-permute-start.12 = (bf16[4,256,128]{2,1,0:T(8,128)(2,1)S(1)}, bf16[4,256,128]{2,1,0:T(8,128)(2,1)S(1)}, u32[]{:S(2)}, u32[]{:S(2)}) collective-permute-start(bf16[4,256,128]{2,1,0:T(8,128)(2,1)S(1)} %slice.75), channel_id=1, source_target_pairs={{0,8},{1,9},{2,10},{3,11},{4,36},{5,37},{6,38},{7,39},{8,0},{9,1},... | collective-permute-start | bytes 786440 | tf_op jit(solution)/shard_map/ppermute | solution.py:49
  76.5 5.1 %collective-permute-start.7 = (bf16[2,256,128]{2,1,0:T(8,128)(2,1)S(1)}, bf16[2,256,128]{2,1,0:T(8,128)(2,1)S(1)}, u32[]{:S(2)}, u32[]{:S(2)}) collective-permute-start(bf16[2,256,128]{2,1,0:T(8,128)(2,1)S(1)} %slice.71), channel_id=1, source_target_pairs={{0,96},{1,97},{2,98},{3,99},{4,28},{5,29},{6,30},{7,31},{8,104},{9... | collective-permute-start | bytes 393224 | tf_op jit(solution)/shard_map/ppermute | solution.py:49
  79.0 5.6 %collective-permute-start.13 = (bf16[2,256,128]{2,1,0:T(8,128)(2,1)S(1)}, bf16[2,256,128]{2,1,0:T(8,128)(2,1)S(1)}, u32[]{:S(2)}, u32[]{:S(2)}) collective-permute-start(bf16[2,256,128]{2,1,0:T(8,128)(2,1)S(1)} %slice.77), channel_id=1, source_target_pairs={{0,32},{1,33},{2,34},{3,35},{4,12},{5,13},{6,14},{7,15},{8,40},{9,... | collective-permute-start | bytes 393224 | tf_op jit(solution)/shard_map/ppermute | solution.py:49
  81.6 46.0 %copy-start.4 = (bf16[256,256]{1,0:T(8,128)(2,1)S(1)}, bf16[256,256]{1,0:T(8,128)(2,1)}, u32[]{:S(2)}) copy-start(bf16[256,256]{1,0:T(8,128)(2,1)} %param.11) | copy-start | bytes 393220
  84.9 7.1 %collective-permute-start.14 = (f32[128,256]{1,0:T(8,128)S(1)}, f32[128,256]{1,0:T(8,128)S(1)}, u32[]{:S(2)}, u32[]{:S(2)}) collective-permute-start(f32[128,256]{1,0:T(8,128)S(1)} %dynamic-slice_bitcast_fusion), channel_id=1, source_target_pairs={{0,4},{1,5},{2,6},{3,7},{4,0},{5,1},{6,2},{7,3},{8,12},{9,13},{10,... | collective-permute-start | bytes 393224 | tf_op jit(solution)/shard_map/ppermute | solution.py:54
  92.0 4.2 %collective-permute-start.15 = (f32[128,256]{1,0:T(8,128)S(1)}, f32[128,256]{1,0:T(8,128)S(1)}, u32[]{:S(2)}, u32[]{:S(2)}) collective-permute-start(f32[128,256]{1,0:T(8,128)S(1)} %bitcast_add_fusion), channel_id=1, source_target_pairs={{0,8},{1,9},{2,10},{3,11},{4,36},{5,37},{6,38},{7,39},{8,0},{9,1},... | collective-permute-start | bytes 393224 | tf_op jit(solution)/shard_map/ppermute | solution.py:49
  96.2 3.9 %collective-permute-start.16 = (f32[128,256]{1,0:T(8,128)S(1)}, f32[128,256]{1,0:T(8,128)S(1)}, u32[]{:S(2)}, u32[]{:S(2)}) collective-permute-start(f32[128,256]{1,0:T(8,128)S(1)} %add.335), channel_id=1, source_target_pairs={{0,32},{1,33},{2,34},{3,35},{4,12},{5,13},{6,14},{7,15},{8,40},{9,... | collective-permute-start | bytes 393224 | tf_op jit(solution)/shard_map/ppermute | solution.py:49
  100.2 5.1 %collective-permute-start.17 = (f32[128,256]{1,0:T(8,128)S(1)}, f32[128,256]{1,0:T(8,128)S(1)}, u32[]{:S(2)}, u32[]{:S(2)}) collective-permute-start(f32[128,256]{1,0:T(8,128)S(1)} %add.336), channel_id=1, source_target_pairs={{0,1},{1,0},{2,3},{3,2},{4,28},{5,29},{6,30},{7,31},{8,9},{9,8},{1... | collective-permute-start | bytes 393224 | tf_op jit(solution)/shard_map/ppermute | solution.py:49
  105.3 3.9 %collective-permute-start.18 = (f32[128,256]{1,0:T(8,128)S(1)}, f32[128,256]{1,0:T(8,128)S(1)}, u32[]{:S(2)}, u32[]{:S(2)}) collective-permute-start(f32[128,256]{1,0:T(8,128)S(1)} %add.337), channel_id=1, source_target_pairs={{0,24},{1,25},{2,26},{3,27},{4,5},{5,4},{6,7},{7,6},{8,16},{9,17},... | collective-permute-start | bytes 393224 | tf_op jit(solution)/shard_map/ppermute | solution.py:49
  109.2 5.1 %collective-permute-start.19 = (f32[128,256]{1,0:T(8,128)S(1)}, f32[128,256]{1,0:T(8,128)S(1)}, u32[]{:S(2)}, u32[]{:S(2)}) collective-permute-start(f32[128,256]{1,0:T(8,128)S(1)} %add.338), channel_id=1, source_target_pairs={{0,96},{1,97},{2,98},{3,99},{4,7},{5,6},{6,5},{7,4},{8,104},{9,105... | collective-permute-start | bytes 393224 | tf_op jit(solution)/shard_map/ppermute | solution.py:49
  114.3 6.5 %collective-permute-start.20 = (f32[128,256]{1,0:T(8,128)S(1)}, f32[128,256]{1,0:T(8,128)S(1)}, u32[]{:S(2)}, u32[]{:S(2)}) collective-permute-start(f32[128,256]{1,0:T(8,128)S(1)} %add.339), channel_id=1, source_target_pairs={{0,3},{1,2},{2,1},{3,0},{4,100},{5,101},{6,102},{7,103},{8,11},{9,... | collective-permute-start | bytes 393224 | tf_op jit(solution)/shard_map/ppermute | solution.py:49
  120.9 7.7 %collective-permute-start.21 = (f32[128,256]{1,0:T(8,128)S(1)}, f32[128,256]{1,0:T(8,128)S(1)}, u32[]{:S(2)}, u32[]{:S(2)}) collective-permute-start(f32[128,256]{1,0:T(8,128)S(1)} %add.340), channel_id=1, source_target_pairs={{0,4},{1,5},{2,6},{3,7},{4,0},{5,1},{6,2},{7,3},{8,12},{9,13},{10,... | collective-permute-start | bytes 393224 | tf_op jit(solution)/shard_map/ppermute | solution.py:54

commit v2 on v0

v2 whole, which is shorter than its diff:
```python
import functools

import jax
import jax.numpy as jnp
from jax import lax
from jax.experimental import pallas as pl
from jax.experimental.pallas import tpu as pltpu
from jax.sharding import PartitionSpec as P

AXES = ("row", "rep")
RING = 4
BLOCK = 128
FEAT = 256
SHARE_BLOCKS = 4
ROWBLK = 16
SLOTS = 32
CALLS = 4
CALL_SLOTS = 32
MAX_PAIRS = 256
UNROLL = 16
AFTER = {1: 2, 3: 3}
NO_BLOCK = ROWBLK << 9

FLIP = {"x0": ("x", 1), "x1": ("x", 3), "z0": ("z", 1), "z1": ("z", 3), "y0": ("y", 1), "y1": ("y", 3)}
ORDER = (
    (("x0", "z0", "x1", "z1"), ("z0", "x0", "z1", "x1")),
    (("x1", "z1", "x0", "z0"), ("z1", "x1", "z0", "x0")),
)


def linear(z, x, c, y):
    return ((z * RING + x) * 2 + c) * RING + y


def exchange_pairs(first, second):
    pairs = []
    for z in range(RING):
        for x in range(RING):
            for c in range(2):
                for y in range(RING):
                    at = {"z": z, "x": x, "c": c, "y": y}
                    axis, mask = FLIP[first if c == 0 else second]
                    at[axis] ^= mask
                    pairs.append((linear(z, x, c, y), linear(**at)))
    return pairs


def exchange(value, first, second):
    return lax.ppermute(value, AXES, exchange_pairs(first, second))


def swap_cores(value):
    pairs = [(d, d ^ RING) for d in range(RING * RING * 2 * RING)]
    return lax.ppermute(value, AXES, pairs)


def prepare_kernel(where_ref, counts_ref, cols_ref, adj_ref, *refs):
    out_ref, words_refs, sem = refs[-CALLS - 2], refs[-CALLS - 1 : -1], refs[-1]

    def copies(action):
        for r in range(ROWBLK):
            count = counts_ref[r]
            for bit in range(6):
                size = 1 << bit
                offset = r * SLOTS + (count & ~(2 * size - 1))

                @pl.when((count & size) != 0)
                def _(offset=offset, size=size):
                    at = pl.ds(offset, size)
                    action(pltpu.make_async_copy(adj_ref.at[at], out_ref.at[at], sem))

    copies(lambda copy: copy.start())
    plan(where_ref, counts_ref, cols_ref, words_refs)
    copies(lambda copy: copy.wait())


def plan(where_ref, counts_ref, cols_ref, words_refs):
    i32 = jnp.int32
    z, x, c, y = (where_ref[i] for i in range(4))
    slots = CALLS * CALL_SLOTS

    lane = lax.broadcasted_iota(i32, (8, slots), 1)
    sent, upper, part = lane >> 6, (lane >> 5) & 1, (lane >> 4) & 1
    core = c ^ sent
    place = upper * 8 + ((lane & 15) >> 1)
    at = {"z": jnp.zeros_like(lane) + z, "x": jnp.zeros_like(lane) + x}
    for bit in range(4):
        on = (place >> (3 - bit)) & 1
        for p in range(2):
            for k in range(2):
                axis, mask = FLIP[ORDER[p][k][bit]]
                at[axis] = at[axis] ^ jnp.where((part == p) & (core == k), on * mask, 0)
    group = (at["z"] * RING + at["x"]) * 2 + core
    target = (group * ROWBLK + y * SHARE_BLOCKS + part * 2 + (lane & 1))[:1]

    index = lax.broadcasted_iota(i32, (ROWBLK, SLOTS), 0)
    live = jnp.zeros((ROWBLK, SLOTS), i32)
    for r in range(ROWBLK):
        live = jnp.where(index == r, counts_ref[r], live)
    cols = jnp.where(lax.broadcasted_iota(i32, (ROWBLK, SLOTS), 1) < live, cols_ref[...], -1)
    found = jnp.zeros((ROWBLK, slots), i32)
    for s in range(SLOTS):
        found = found + jnp.where(cols[:, s : s + 1] == target, s + 1, 0)
    present = jnp.where(found > 0, 1, 0)
    before, count = [], jnp.zeros((1, slots), i32)
    for r in range(ROWBLK):
        before.append(count)
        count = count + present[r : r + 1]
    before = jnp.concatenate(before, axis=0)
    pairs = jnp.maximum((count + 1) >> 1, 1)
    i0 = lax.broadcasted_iota(i32, (slots, slots), 0)
    i1 = lax.broadcasted_iota(i32, (slots, slots), 1)
    earlier = jnp.where((i0 >> 5 == i1 >> 5) & (i0 < i1), 1.0, 0.0).astype(jnp.bfloat16)
    wide = jnp.broadcast_to(pairs, (16, slots)).astype(jnp.float32).astype(jnp.bfloat16)
    start = jnp.dot(wide, earlier, preferred_element_type=jnp.float32).astype(i32)

    key = jnp.where(found > 0, start + (before >> 1) + (before & 1) * MAX_PAIRS, -1)
    row = lax.broadcasted_iota(i32, (ROWBLK, slots), 0)
    step = (row >> 2) ^ y
    first = jnp.where(c == 0, 1, 3)
    rel = jnp.where(step == 0, 0, jnp.where(step == first, 1, jnp.where(step == 2, 3, 2)))
    grad = rel * SHARE_BLOCKS + (row & 3)
    code = row * SLOTS + found - 1 + (grad << 9) - NO_BLOCK

    key_t, code_t, start_t = key.T, code.T, start.T
    end_t = start_t + jnp.broadcast_to(pairs, (16, slots)).T
    position = lax.broadcasted_iota(i32, (CALL_SLOTS, 2 * MAX_PAIRS), 1)
    pair = position[:, :MAX_PAIRS]
    for call in range(CALLS):
        rows = slice(call * CALL_SLOTS, (call + 1) * CALL_SLOTS)
        flat = jnp.zeros((CALL_SLOTS, 2 * MAX_PAIRS), i32)
        for r in range(ROWBLK):
            flat = flat + jnp.where(key_t[rows, r : r + 1] == position, code_t[rows, r : r + 1], 0)
        words = jnp.sum(flat, axis=0, keepdims=True) + NO_BLOCK
        ended = jnp.sum(jnp.where(end_t[rows, :1] <= pair, 1, 0), axis=0, keepdims=True)
        opens = jnp.sum(jnp.where(start_t[rows, :1] == pair, 1, 0), axis=0, keepdims=True)
        meta = (jnp.minimum(ended, CALL_SLOTS - 1) + opens * CALL_SLOTS) << 14
        last = end_t[call * CALL_SLOTS + CALL_SLOTS - 1 : (call + 1) * CALL_SLOTS, :1]
        words_refs[call][:, :MAX_PAIRS] = words[:, :MAX_PAIRS] + meta
        words_refs[call][:, MAX_PAIRS : 2 * MAX_PAIRS] = words[:, MAX_PAIRS:]
        words_refs[call][:, 2 * MAX_PAIRS :] = jnp.broadcast_to(last, (1, BLOCK))

def prepare(adj_values, adj_cols, adj_counts, where, gates):
    shape = (ROWBLK * SLOTS, BLOCK, BLOCK)
    words = pltpu.VMEM((1, 2 * MAX_PAIRS + BLOCK), jnp.int32)
    return pl.pallas_call(
        prepare_kernel,
        out_shape=(pltpu.VMEM(shape, jnp.bfloat16),) + (words,) * CALLS,
        in_specs=[IN_SMEM, IN_SMEM, IN_VMEM, ANYWHERE] + [ANYWHERE] * len(gates),
        out_specs=(IN_VMEM,) * (1 + CALLS),
        scratch_shapes=[pltpu.SemaphoreType.DMA],
        compiler_params=pltpu.CompilerParams(vmem_limit_bytes=4 << 20),
        cost_estimate=TINY,
        name="prepare",
    )(
        where,
        pltpu.with_memory_space_constraint(adj_counts.reshape(-1), pltpu.HBM),
        pltpu.with_memory_space_constraint(adj_cols, pltpu.HBM),
        pltpu.with_memory_space_constraint(adj_values.reshape(shape), pltpu.HBM),
        *gates,
    )


TINY = pl.CostEstimate(flops=0, bytes_accessed=1024, transcendentals=0)
ANYWHERE = pl.BlockSpec(memory_space=pl.ANY)
IN_VMEM = pl.BlockSpec(memory_space=pltpu.VMEM)
IN_SMEM = pl.BlockSpec(memory_space=pltpu.SMEM)


def in_vmem(value):
    return pltpu.with_memory_space_constraint(value, pltpu.VMEM)


def load_kernel(grad_ref, preact_ref, feat_ref, own_ref, feat0_ref, feat1_ref, grad, preact, sems):
    first = pltpu.make_async_copy(grad_ref, grad, sems.at[0])
    second = pltpu.make_async_copy(preact_ref, preact, sems.at[1])
    third = pltpu.make_async_copy(feat_ref.at[pl.ds(0, 2)], feat0_ref, sems.at[2])
    fourth = pltpu.make_async_copy(feat_ref.at[pl.ds(2, 2)], feat1_ref, sems.at[3])
    copies = (first, second, third, fourth)
    for copy in copies:
        copy.start()
    for copy in copies:
        copy.wait()
    for b in range(SHARE_BLOCKS):
        value = grad[b].astype(jnp.float32)
        own_ref[b] = jnp.where(preact[b].astype(jnp.float32) > 0, value, 0.0).astype(jnp.bfloat16)


def load(grad_out, preact, features):
    whole, part = (SHARE_BLOCKS, BLOCK, FEAT), (2, BLOCK, FEAT)
    return pl.pallas_call(
        load_kernel,
        out_shape=tuple(pltpu.VMEM(s, jnp.bfloat16) for s in (whole, part, part)),
        in_specs=[ANYWHERE] * 3,
        out_specs=(IN_VMEM,) * 3,
        scratch_shapes=[pltpu.VMEM(whole, jnp.bfloat16)] * 2 + [pltpu.SemaphoreType.DMA((4,))],
        compiler_params=pltpu.CompilerParams(vmem_limit_bytes=4 << 20),
        cost_estimate=TINY,
        name="load",
    )(*(pltpu.with_memory_space_constraint(v.reshape(whole), pltpu.HBM) for v in (grad_out, preact, features)))


def join_kernel(n, *refs):
    out_ref = refs[-1]
    at = 0
    for ref in refs[:n]:
        size = ref.shape[0]
        out_ref[at : at + size] = ref[...]
        at += size
    if at < out_ref.shape[0]:
        out_ref[at:] = jnp.zeros_like(out_ref[at:])


def join(pieces, gates=(), zeros=0):
    size = sum(p.shape[0] for p in pieces) + zeros
    return pl.pallas_call(
        functools.partial(join_kernel, len(pieces)),
        out_shape=pltpu.VMEM((size, *pieces[0].shape[1:]), pieces[0].dtype),
        in_specs=[IN_VMEM] * len(pieces) + [ANYWHERE] * len(gates),
        out_specs=IN_VMEM,
        compiler_params=pltpu.CompilerParams(vmem_limit_bytes=4 << 20),
        cost_estimate=TINY,
        name="join",
    )(*(in_vmem(p) for p in pieces), *gates)


def fold_kernel(n, kept_ref, got_ref, *refs):
    at = 0
    for ref in refs[-n:]:
        size = ref.shape[0]
        for b in range(size):
            ref[b] = (kept_ref[at + b].astype(jnp.float32) + got_ref[at + b].astype(jnp.float32)).astype(jnp.bfloat16)
        at += size


def fold(kept, got, halves, gates=()):
    size, *rest = kept.shape
    out = tuple(pltpu.VMEM((size // halves, *rest), jnp.bfloat16) for _ in range(halves))
    return pl.pallas_call(
        functools.partial(fold_kernel, halves),
        out_shape=out,
        in_specs=[IN_VMEM] * 2 + [ANYWHERE] * len(gates),
        out_specs=(IN_VMEM,) * halves,
        compiler_params=pltpu.CompilerParams(vmem_limit_bytes=4 << 20),
        cost_estimate=TINY,
        name="fold",
    )(in_vmem(kept), in_vmem(got), *gates)


def features_kernel(first_ref, second_ref, weight_ref, out_ref):
    for k, ref in enumerate((first_ref, second_ref)):
        for b in range(2):
            rows = pl.ds((2 * k + b) * BLOCK, BLOCK)
            value = lax.dot_general(
                ref[b], weight_ref[...], (((1,), (1,)), ((), ())), preferred_element_type=jnp.float32
            )
            out_ref[rows, :] = value.astype(jnp.bfloat16)


def features_gradient(first, second, weight):
    return pl.pallas_call(
        features_kernel,
        out_shape=jax.ShapeDtypeStruct((SHARE_BLOCKS * BLOCK, FEAT), jnp.bfloat16),
        in_specs=[IN_VMEM] * 3,
        out_specs=IN_VMEM,
        compiler_params=pltpu.CompilerParams(vmem_limit_bytes=4 << 20),
        cost_estimate=TINY,
        name="features_gradient",
    )(in_vmem(first), in_vmem(second), weight)


def weight_kernel(core_ref, *refs):
    ins, outs = refs[:-2], refs[-2:]
    n = FEAT // 2
    for k, out_ref in enumerate(outs):
        rows = pl.ds(pl.multiple_of((core_ref[0] ^ k) * n, n), n)
        total = jnp.zeros((n, FEAT), jnp.float32)
        for feat, held in zip(ins[::2], ins[1::2]):
            size = feat.shape[0] * BLOCK
            left = feat[:, :, rows].reshape(size, n)
            total = total + lax.dot_general(
                left, held[...].reshape(size, FEAT), (((0,), (0,)), ((), ())), preferred_element_type=jnp.float32
            )
        out_ref[...] = total.astype(out_ref.dtype)


def weight_terms(core, pairs):
    flat = [in_vmem(v) for pair in pairs for v in pair]
    return pl.pallas_call(
        weight_kernel,
        out_shape=tuple(pltpu.VMEM((FEAT // 2, FEAT), t) for t in (jnp.float32, jnp.bfloat16)),
        in_specs=[IN_SMEM] + [IN_VMEM] * len(flat),
        out_specs=(IN_VMEM,) * 2,
        compiler_params=pltpu.CompilerParams(vmem_limit_bytes=8 << 20),
        cost_estimate=TINY,
        name="weight_terms",
    )(core.reshape(1), *flat)


def products_kernel(words_ref, grad_ref, adj_ref, *refs):
    out_ref = refs[-1]

    def pair(p, acc):
        w0 = words_ref[0, p]
        w1 = words_ref[0, MAX_PAIRS + p]
        slot = (w0 >> 14) & (CALL_SLOTS - 1)
        keep = jnp.where((w0 >> 19) == 0, 1.0, 0.0).astype(jnp.float32)
        grad = jnp.concatenate([grad_ref[(w0 >> 9) & 31], grad_ref[(w1 >> 9) & 31]], axis=0)
        adj = jnp.concatenate([adj_ref[w0 & 511], adj_ref[w1 & 511]], axis=0)
        term = lax.dot_general(adj, grad, (((0,), (0,)), ((), ())), preferred_element_type=jnp.float32)
        acc = acc * keep + term
        out_ref[slot] = acc.astype(jnp.bfloat16)
        return acc

    def steps(i, acc):
        for u in range(UNROLL):
            acc = pair(i * UNROLL + u, acc)
        return acc

    count = (words_ref[0, 2 * MAX_PAIRS] + UNROLL - 1) // UNROLL
    lax.fori_loop(0, count, steps, jnp.zeros((BLOCK, FEAT), jnp.float32))


def products(name, words, grad, adj, gates):
    return pl.pallas_call(
        products_kernel,
        out_shape=pltpu.VMEM((CALL_SLOTS, BLOCK, FEAT), jnp.bfloat16),
        in_specs=[IN_SMEM, IN_VMEM, IN_VMEM] + [ANYWHERE] * len(gates),
        out_specs=IN_VMEM,
        compiler_params=pltpu.CompilerParams(vmem_limit_bytes=4 << 20),
        cost_estimate=TINY,
        name=f"products_{name}",
    )(
        words,
        in_vmem(grad),
        in_vmem(adj),
        *gates,
    )


def body(grad_out, preact, features, weight, adj_values, adj_cols, adj_counts):
    row, y = lax.axis_index("row"), lax.axis_index("rep")
    z, x, c = row // (2 * RING), row // 2 % RING, row % 2
    core = c.astype(jnp.int32)

    own, *mine = load(grad_out, preact, features)
    got = exchange(own, "y0", "y1")
    near = [exchange(mine[p], ORDER[p][0][3], ORDER[p][1][3]) for p in (0, 1)]
    half = join([own, got], near)
    got = exchange(half, "y1", "y0")
    feats = [join([mine[p], near[p]], [half]) for p in (0, 1)]
    far = [exchange(feats[p], ORDER[p][0][2], ORDER[p][1][2]) for p in (0, 1)]
    where = jnp.stack([z, x, c, y]).astype(jnp.int32)
    adj, *words = prepare(adj_values, adj_cols, adj_counts, where, feats)
    grad = join([half, got], [adj, *far], zeros=1)

    def product(sent, upper, gates=()):
        call = sent * 2 + upper
        return products(call, words[call], grad, adj, gates)

    sent_upper = product(1, 1)
    sent_lower = product(1, 0, [sent_upper])
    kept_upper = product(0, 1, [sent_lower])
    upper = list(fold(kept_upper, swap_cores(sent_upper), 2))
    kept_lower = product(0, 0, upper)
    lower = list(fold(kept_lower, swap_cores(sent_lower), 2))

    def halve(step, gates=()):
        for p in (0, 1):
            got = exchange(upper[p], ORDER[p][0][step], ORDER[p][1][step])
            lower[p], *rest = fold(lower[p], got, 2 if step < 3 else 1, gates)
            upper[p] = rest[0] if rest else None
        return list(lower)

    halve(0)
    halve(1)
    held = [(v[p], w[p]) for p in (0, 1) for v, w in ((feats, lower), (far, upper))]
    term, other = weight_terms(core, held)
    (term,) = fold(term, swap_cores(other), 1)
    for k, dims in enumerate((("y0", "y1"), ("y1", "y0"), ("x0", "z0"), ("z0", "x0"), ("x1", "z1"), ("z1", "x1"))):
        got = exchange(term, *dims)
        gates = halve(AFTER[k], [term]) if k in AFTER else ()
        (term,) = fold(term, got, 1, gates)
    theirs = swap_cores(term)
    grad_weight = jnp.concatenate([jnp.where(c == 0, term, theirs), jnp.where(c == 0, theirs, term)])
    return features_gradient(*lower, weight), grad_weight.astype(jnp.float32)


def solution(mesh):
    placed = (
        P(AXES, None),
        P(AXES, None),
        P(AXES, None),
        P(),
        P("row", "rep", None, None),
        P("row", "rep"),
        P("row", "rep"),
    )
    return jax.shard_map(body, mesh=mesh, in_specs=placed, out_specs=(P(AXES, None), P()), check_vma=False)
```

time: 537 us -> 99.3 us (0.18)
  other arithmetic: 178 us -> 0.81 us
  waiting for transfers between devices: 164 us -> 42.9 us
  blocking collectives: 104 us -> 0 us
  matrix products: 65.6 us -> 0 us
  starting transfers between devices: 0.08 us -> 34.5 us
  Pallas kernels: 0 us -> 20.9 us
  between operations: 14.1 us -> 0.95 us
  local copies, waits for them, and re-layouts: 9.77 us -> 0.01 us
    scatter-add x16 -> x0, other arithmetic: 163 us -> none  [row_step(): return partial_value.at[local_index[index]].add(messages)]
    psum x1 -> x0, waiting for transfers between devices: 138 us -> none  [body(): grad_weight = lax.psum(weight_term, ('row', 'rep'))]
    all_to_all x1 -> x0, blocking collectives: 104 us -> none  [body(): lax.all_to_all(outgoing, 'row', split_axis=0, concat_axis=0, tiled=True)]
    dot_general x18 -> x0, matrix products: 65.6 us -> none  [the longest x16 63.6 us: row_step(): jnp.einsum('sij,if->sjf', adj_values[index], grad_blocks[index], preferre...]
    ppermute x0 -> x24, waiting for transfers between devices: none -> 42.9 us  [the longest x20 42 us: exchange(): return lax.ppermute(value, AXES, exchange_pairs(first, second))]
    ppermute x0 -> x24, starting transfers between devices: none -> 34.5 us  [the longest x20 18 us: exchange(): return lax.ppermute(value, AXES, exchange_pairs(first, second))]
    all_gather x1 -> x0, waiting for transfers between devices: 26 us -> none  [body(): grad_pre = lax.all_gather(masked_local, 'rep', axis=0, tiled=True)]
    pallas_call x0 -> x29, Pallas kernels: none -> 20.9 us  [the longest x4 9.56 us: products(): pl.pallas_call(products_kernel, out_shape=pltpu.VMEM((CALL_SLOTS, BLOCK,...]
  transfers between devices with their start and end apart: 2 -> 24, of which waited for: 2 -> 12; matrix products, arithmetic and copies ran while one was open for 0% -> 0% of each run, Pallas kernels for 0% -> 17%
where the time goes in v2:
time: 99.3 us; the launch traced here: 100 us
  waiting for transfers between devices  42.9 us (43%)
  starting transfers between devices  34.5 us (35%)
  Pallas kernels  20.9 us (21%)
    ppermute x20, waiting for transfers between devices, exchange(): return lax.ppermute(value, AXES, exchange_pairs(first, second))  42 us
    ppermute x20, starting transfers between devices, exchange(): return lax.ppermute(value, AXES, exchange_pairs(first, second))  18 us
    ppermute x4, starting transfers between devices, swap_cores(): return lax.ppermute(value, AXES, pairs)  16.5 us
    pallas_call x4, Pallas kernels, products(): pl.pallas_call(products_kernel, out_shape=pltpu.VMEM((CALL_SLOTS, BLOCK,...  9.56 us
    pallas_call x1, Pallas kernels, prepare(): pl.pallas_call(prepare_kernel, out_shape=(pltpu.VMEM(shape, jnp.bfloat16)...  5.6 us
    pallas_call x17, Pallas kernels, fold(): pl.pallas_call(functools.partial(fold_kernel, halves), out_shape=out, in_...  2.9 us
  transfers between devices with their start and end apart: 24, of which 12 were waited for; matrix products, arithmetic and copies ran while one was open for 0% of the time, Pallas kernels for 17%

profile of v2, /device:TPU:1, one launch (start us, length us, event | category | flops | bytes accessed | tf_op | source)
XLA Modules:
  0.0 100.0 jit_solution(3922219034540266494)
XLA Ops:
  0.6 1.2 %load.1 = (bf16[4,128,256]{2,1,0:T(8,128)(2,1)S(1)}, bf16[2,128,256]{2,1,0:T(8,128)(2,1)S(1)}, bf16[2,128,256]{2,1,0:T(8,128)(2,1)S(1)}) custom-call(bf16[4,128,256]{2,1,0:T(8,128)(2,1)} %bitcast.10, bf16[4,128,256]{2,1,0:T(8,128)(2,1)} %bitcast.11, bf16[4,128,256]{2,1,0:T(8,128)(2,1)} %bitcast.12), custom_call_target="tpu_custom_call" | custom-call | bytes 1024 | tf_op jit(solution)/shard_map/load/pallas_call | solution.py:191
  1.9 3.6 %collective-permute-start.1 = (bf16[4,128,256]{2,1,0:T(8,128)(2,1)S(1)}, bf16[4,128,256]{2,1,0:T(8,128)(2,1)S(1)}, u32[]{:S(2)}, u32[]{:S(2)}) collective-permute-start(bf16[4,128,256]{2,1,0:T(8,128)(2,1)S(1)} %get-tuple-element.29.refs_0_), channel_id=1, source_target_pairs={{0,1},{1,0},{2,3},{3,2},{4,7},{5,6},{6,5},{7,4},{8,9},{9,8},{10,11... | collective-permute-start | bytes 786440 | tf_op jit(solution)/shard_map/ppermute | solution.py:49
  5.5 2.5 %collective-permute-start = (bf16[2,128,256]{2,1,0:T(8,128)(2,1)S(1)}, bf16[2,128,256]{2,1,0:T(8,128)(2,1)S(1)}, u32[]{:S(2)}, u32[]{:S(2)}) collective-permute-start(bf16[2,128,256]{2,1,0:T(8,128)(2,1)S(1)} %get-tuple-element.28.refs_0_), channel_id=1, source_target_pairs={{0,96},{1,97},{2,98},{3,99},{4,28},{5,29},{6,30},{7,31},{8,104},{9... | collective-permute-start | bytes 393224 | tf_op jit(solution)/shard_map/ppermute | solution.py:49
  8.0 2.8 %collective-permute-done.refs_2_.refs_1_ = bf16[2,128,256]{2,1,0:T(8,128)(2,1)S(1)} collective-permute-done((bf16[2,128,256]{2,1,0:T(8,128)(2,1)S(1)}, bf16[2,128,256]{2,1,0:T(8,128)(2,1)S(1)}, u32[]{:S(2)}, u32[]{:S(2)}) %collective-permute-start) | collective-permute-done | bytes 131104 | tf_op jit(solution)/shard_map/ppermute | solution.py:49
  10.8 1.0 collective-permute-done.2.refs_3_.refs_1_
  12.0 3.8 %collective-permute-start.4 = (bf16[4,128,256]{2,1,0:T(8,128)(2,1)S(1)}, bf16[4,128,256]{2,1,0:T(8,128)(2,1)S(1)}, u32[]{:S(2)}, u32[]{:S(2)}) collective-permute-start(bf16[4,128,256]{2,1,0:T(8,128)(2,1)S(1)} %join.5.refs_0_), channel_id=1, source_target_pairs={{0,24},{1,25},{2,26},{3,27},{4,100},{5,101},{6,102},{7,103},{8,16}... | collective-permute-start | bytes 786440 | tf_op jit(solution)/shard_map/ppermute | solution.py:49
  16.0 5.6 %prepare.1 = (bf16[512,128,128]{2,1,0:T(8,128)(2,1)S(1)}, s32[1,640]{1,0:T(1,128)S(1)}, s32[1,640]{1,0:T(1,128)S(1)}, s32[1,640]{1,0:T(1,128)S(1)}, s32[1,640]{1,0:T(1,128)S(1)}) custom-call(s32[4]{0:T(128)S(1)} %pad_add_fusion.where_ref, s32[16]{0:T(128)} %bitcast.13, s32[16,32]{1,0:T(8,128)} %cols_ref.1, bf16[512,128,128]{2,1,0:T(8,128)(2,1)} %bitcast.9, ...), custom_call_target="tpu_custom_call" | custom-call | bytes 1024 | tf_op jit(solution)/shard_map/prepare/pallas_call | solution.py:146
  21.7 2.1 %products_3.1.refs_0_ = bf16[32,128,256]{2,1,0:T(8,128)(2,1)S(1)} custom-call(s32[1,640]{1,0:T(1,128)S(1)} %get-tuple-element.35.words_ref, bf16[17,128,256]{2,1,0:T(8,128)(2,1)S(1)} %join.7.grad_ref, bf16[512,128,128]{2,1,0:T(8,128)(2,1)S(1)} %get-tuple-element.32.refs_2_.adj_ref), custom_call_target="tpu_custom_call" | custom-call | bytes 1024 | tf_op jit(solution)/shard_map/products_3/pallas_call | solution.py:325
  23.9 4.1 %collective-permute-start.6 = (bf16[32,128,256]{2,1,0:T(8,128)(2,1)S(1)}, bf16[32,128,256]{2,1,0:T(8,128)(2,1)S(1)}, u32[]{:S(2)}, u32[]{:S(2)}) collective-permute-start(bf16[32,128,256]{2,1,0:T(8,128)(2,1)S(1)} %products_3.1.refs_0_), channel_id=1, source_target_pairs={{0,4},{1,5},{2,6},{3,7},{4,0},{5,1},{6,2},{7,3},{8,12},{9,13},{10,... | collective-permute-start | bytes 6291464 | tf_op jit(solution)/shard_map/ppermute | solution.py:54
  28.0 2.1 %products_2.1.refs_0_ = bf16[32,128,256]{2,1,0:T(8,128)(2,1)S(1)} custom-call(s32[1,640]{1,0:T(1,128)S(1)} %get-tuple-element.34.words_ref, bf16[17,128,256]{2,1,0:T(8,128)(2,1)S(1)} %join.7.grad_ref, bf16[512,128,128]{2,1,0:T(8,128)(2,1)S(1)} %get-tuple-element.32.refs_2_.adj_ref, bf16[32,128,256]{2,1,0:T(8,128)(2,1)S(1)} %products_3.1.refs_0_), custom_call_target="tpu_custom_call" | custom-call | bytes 1024 | tf_op jit(solution)/shard_map/products_2/pallas_call | solution.py:325
  30.2 2.7 %products_1.1.kept_ref = bf16[32,128,256]{2,1,0:T(8,128)(2,1)S(1)} custom-call(s32[1,640]{1,0:T(1,128)S(1)} %get-tuple-element.33.words_ref, bf16[17,128,256]{2,1,0:T(8,128)(2,1)S(1)} %join.7.grad_ref, bf16[512,128,128]{2,1,0:T(8,128)(2,1)S(1)} %get-tuple-element.32.refs_2_.adj_ref, bf16[32,128,256]{2,1,0:T(8,128)(2,1)S(1)} %products_2.1.refs_0_), custom_call_target="tpu_custom_call" | custom-call | bytes 1024 | tf_op jit(solution)/shard_map/products_1/pallas_call | solution.py:325
  33.9 2.6 %products_0.1.kept_ref = bf16[32,128,256]{2,1,0:T(8,128)(2,1)S(1)} custom-call(s32[1,640]{1,0:T(1,128)S(1)} %get-tuple-element.31.words_ref, bf16[17,128,256]{2,1,0:T(8,128)(2,1)S(1)} %join.7.grad_ref, bf16[512,128,128]{2,1,0:T(8,128)(2,1)S(1)} %get-tuple-element.32.refs_2_.adj_ref, bf16[16,128,256]{2,1,0:T(8,128)(2,1)S(1)} %get-tuple-element.36.refs_0_, ...), custom_call_target="tpu_custom_call" | custom-call | bytes 1024 | tf_op jit(solution)/shard_map/products_0/pallas_call | solution.py:325
  36.6 0.5 fold.18
  37.1 10.2 %collective-permute-done.8.got_ref = bf16[16,128,256]{2,1,0:T(8,128)(2,1)S(1)} collective-permute-done((bf16[16,128,256]{2,1,0:T(8,128)(2,1)S(1)}, bf16[16,128,256]{2,1,0:T(8,128)(2,1)S(1)}, u32[]{:S(2)}, u32[]{:S(2)}) %collective-permute-start.8) | collective-permute-done | bytes 1048608 | tf_op jit(solution)/shard_map/ppermute | solution.py:49
  47.6 1.5 %collective-permute-start.9 = (bf16[8,128,256]{2,1,0:T(8,128)(2,1)S(1)}, bf16[8,128,256]{2,1,0:T(8,128)(2,1)S(1)}, u32[]{:S(2)}, u32[]{:S(2)}) collective-permute-start(bf16[8,128,256]{2,1,0:T(8,128)(2,1)S(1)} %get-tuple-element.40), channel_id=1, source_target_pairs={{0,32},{1,33},{2,34},{3,35},{4,12},{5,13},{6,14},{7,15},{8,40},{9,... | collective-permute-start | bytes 1572872 | tf_op jit(solution)/shard_map/ppermute | solution.py:49
  49.4 1.1 %collective-permute-start.12 = (bf16[8,128,256]{2,1,0:T(8,128)(2,1)S(1)}, bf16[8,128,256]{2,1,0:T(8,128)(2,1)S(1)}, u32[]{:S(2)}, u32[]{:S(2)}) collective-permute-start(bf16[8,128,256]{2,1,0:T(8,128)(2,1)S(1)} %get-tuple-element.45), channel_id=1, source_target_pairs={{0,96},{1,97},{2,98},{3,99},{4,28},{5,29},{6,30},{7,31},{8,104},{9... | collective-permute-start | bytes 1572872 | tf_op jit(solution)/shard_map/ppermute | solution.py:49
  50.5 5.6 %collective-permute-done.9.got_ref = bf16[8,128,256]{2,1,0:T(8,128)(2,1)S(1)} collective-permute-done((bf16[8,128,256]{2,1,0:T(8,128)(2,1)S(1)}, bf16[8,128,256]{2,1,0:T(8,128)(2,1)S(1)}, u32[]{:S(2)}, u32[]{:S(2)}) %collective-permute-start.9) | collective-permute-done | bytes 524320 | tf_op jit(solution)/shard_map/ppermute | solution.py:49
  56.2 0.5 collective-permute-start.10
  56.7 2.3 %collective-permute-done.12.got_ref = bf16[8,128,256]{2,1,0:T(8,128)(2,1)S(1)} collective-permute-done((bf16[8,128,256]{2,1,0:T(8,128)(2,1)S(1)}, bf16[8,128,256]{2,1,0:T(8,128)(2,1)S(1)}, u32[]{:S(2)}, u32[]{:S(2)}) %collective-permute-start.12) | collective-permute-done | bytes 524320 | tf_op jit(solution)/shard_map/ppermute | solution.py:49
  59.7 6.2 %collective-permute-start.13 = (bf16[128,256]{1,0:T(8,128)(2,1)S(1)}, bf16[128,256]{1,0:T(8,128)(2,1)S(1)}, u32[]{:S(2)}, u32[]{:S(2)}) collective-permute-start(bf16[128,256]{1,0:T(8,128)(2,1)S(1)} %get-tuple-element.49), channel_id=1, source_target_pairs={{0,4},{1,5},{2,6},{3,7},{4,0},{5,1},{6,2},{7,3},{8,12},{9,13},{10,... | collective-permute-start | bytes 196616 | tf_op jit(solution)/shard_map/ppermute | solution.py:54
  65.9 0.9 collective-permute-done.13.got_ref
  67.1 4.3 %collective-permute-done.14.got_ref = bf16[128,256]{1,0:T(8,128)(2,1)S(1)} collective-permute-done((bf16[128,256]{1,0:T(8,128)(2,1)S(1)}, bf16[128,256]{1,0:T(8,128)(2,1)S(1)}, u32[]{:S(2)}, u32[]{:S(2)}) %collective-permute-start.14) | collective-permute-done | bytes 65568 | tf_op jit(solution)/shard_map/ppermute | solution.py:49
  71.9 1.8 %collective-permute-start.19 = (bf16[2,128,256]{2,1,0:T(8,128)(2,1)S(1)}, bf16[2,128,256]{2,1,0:T(8,128)(2,1)S(1)}, u32[]{:S(2)}, u32[]{:S(2)}) collective-permute-start(bf16[2,128,256]{2,1,0:T(8,128)(2,1)S(1)} %get-tuple-element.53), channel_id=1, source_target_pairs={{0,32},{1,33},{2,34},{3,35},{4,12},{5,13},{6,14},{7,15},{8,40},{9,... | collective-permute-start | bytes 393224 | tf_op jit(solution)/shard_map/ppermute | solution.py:49
  73.7 1.0 %collective-permute-done.16.got_ref = bf16[128,256]{1,0:T(8,128)(2,1)S(1)} collective-permute-done((bf16[128,256]{1,0:T(8,128)(2,1)S(1)}, bf16[128,256]{1,0:T(8,128)(2,1)S(1)}, u32[]{:S(2)}, u32[]{:S(2)}) %collective-permute-start.16) | collective-permute-done | bytes 65568 | tf_op jit(solution)/shard_map/ppermute | solution.py:49
  75.0 4.1 %collective-permute-done.18.got_ref = bf16[128,256]{1,0:T(8,128)(2,1)S(1)} collective-permute-done((bf16[128,256]{1,0:T(8,128)(2,1)S(1)}, bf16[128,256]{1,0:T(8,128)(2,1)S(1)}, u32[]{:S(2)}, u32[]{:S(2)}) %collective-permute-start.18) | collective-permute-done | bytes 65568 | tf_op jit(solution)/shard_map/ppermute | solution.py:49
  79.2 1.8 %collective-permute-start.20 = (bf16[128,256]{1,0:T(8,128)(2,1)S(1)}, bf16[128,256]{1,0:T(8,128)(2,1)S(1)}, u32[]{:S(2)}, u32[]{:S(2)}) collective-permute-start(bf16[128,256]{1,0:T(8,128)(2,1)S(1)} %fold.28.refs_0_.kept_ref), channel_id=1, source_target_pairs={{0,32},{1,33},{2,34},{3,35},{4,12},{5,13},{6,14},{7,15},{8,40},{9,... | collective-permute-start | bytes 196616 | tf_op jit(solution)/shard_map/ppermute | solution.py:49
  81.1 1.6 %collective-permute-done.20.got_ref = bf16[128,256]{1,0:T(8,128)(2,1)S(1)} collective-permute-done((bf16[128,256]{1,0:T(8,128)(2,1)S(1)}, bf16[128,256]{1,0:T(8,128)(2,1)S(1)}, u32[]{:S(2)}, u32[]{:S(2)}) %collective-permute-start.20) | collective-permute-done | bytes 65568 | tf_op jit(solution)/shard_map/ppermute | solution.py:49
  82.8 4.3 %collective-permute-done.21.got_ref = bf16[128,256]{1,0:T(8,128)(2,1)S(1)} collective-permute-done((bf16[128,256]{1,0:T(8,128)(2,1)S(1)}, bf16[128,256]{1,0:T(8,128)(2,1)S(1)}, u32[]{:S(2)}, u32[]{:S(2)}) %collective-permute-start.21) | collective-permute-done | bytes 65568 | tf_op jit(solution)/shard_map/ppermute | solution.py:49
  87.4 4.6 %collective-permute-done.22.got_ref = bf16[128,256]{1,0:T(8,128)(2,1)S(1)} collective-permute-done((bf16[128,256]{1,0:T(8,128)(2,1)S(1)}, bf16[128,256]{1,0:T(8,128)(2,1)S(1)}, u32[]{:S(2)}, u32[]{:S(2)}) %collective-permute-start.22) | collective-permute-done | bytes 65568 | tf_op jit(solution)/shard_map/ppermute | solution.py:49
  92.1 6.1 %collective-permute-start.23 = (bf16[128,256]{1,0:T(8,128)(2,1)S(1)}, bf16[128,256]{1,0:T(8,128)(2,1)S(1)}, u32[]{:S(2)}, u32[]{:S(2)}) collective-permute-start(bf16[128,256]{1,0:T(8,128)(2,1)S(1)} %fold.33), channel_id=1, source_target_pairs={{0,4},{1,5},{2,6},{3,7},{4,0},{5,1},{6,2},{7,3},{8,12},{9,13},{10,... | collective-permute-start | bytes 196616 | tf_op jit(solution)/shard_map/ppermute | solution.py:54
  98.3 1.0 %features_gradient.1 = bf16[512,256]{1,0:T(8,128)(2,1)} custom-call(bf16[2,128,256]{2,1,0:T(8,128)(2,1)S(1)} %fold.29.first_ref.refs_0_, bf16[2,128,256]{2,1,0:T(8,128)(2,1)S(1)} %fold.30.second_ref.refs_1_, bf16[256,256]{1,0:T(8,128)(2,1)S(1)} %copy-done), custom_call_target="tpu_custom_call" | custom-call | bytes 1024 | tf_op jit(solution)/shard_map/features_gradient/pallas_call | solution.py:261
  99.3 0.7 maximum_convert_fusion
  (50 shorter events, 4.6 us)
Async XLA Ops:
  1.9 9.9 %collective-permute-start.1 = (bf16[4,128,256]{2,1,0:T(8,128)(2,1)S(1)}, bf16[4,128,256]{2,1,0:T(8,128)(2,1)S(1)}, u32[]{:S(2)}, u32[]{:S(2)}) collective-permute-start(bf16[4,128,256]{2,1,0:T(8,128)(2,1)S(1)} %get-tuple-element.29.refs_0_), channel_id=1, source_target_pairs={{0,1},{1,0},{2,3},{3,2},{4,7},{5,6},{6,5},{7,4},{8,9},{9,8},{10,11... | collective-permute-start | bytes 786440 | tf_op jit(solution)/shard_map/ppermute | solution.py:49
  5.5 5.3 %collective-permute-start = (bf16[2,128,256]{2,1,0:T(8,128)(2,1)S(1)}, bf16[2,128,256]{2,1,0:T(8,128)(2,1)S(1)}, u32[]{:S(2)}, u32[]{:S(2)}) collective-permute-start(bf16[2,128,256]{2,1,0:T(8,128)(2,1)S(1)} %get-tuple-element.28.refs_0_), channel_id=1, source_target_pairs={{0,96},{1,97},{2,98},{3,99},{4,28},{5,29},{6,30},{7,31},{8,104},{9... | collective-permute-start | bytes 393224 | tf_op jit(solution)/shard_map/ppermute | solution.py:49
  8.0 3.8 %collective-permute-start.2 = (bf16[2,128,256]{2,1,0:T(8,128)(2,1)S(1)}, bf16[2,128,256]{2,1,0:T(8,128)(2,1)S(1)}, u32[]{:S(2)}, u32[]{:S(2)}) collective-permute-start(bf16[2,128,256]{2,1,0:T(8,128)(2,1)S(1)} %get-tuple-element.30.refs_0_), channel_id=1, source_target_pairs={{0,32},{1,33},{2,34},{3,35},{4,12},{5,13},{6,14},{7,15},{8,40},{9,... | collective-permute-start | bytes 393224 | tf_op jit(solution)/shard_map/ppermute | solution.py:49
  11.8 9.8 %collective-permute-start.3 = (bf16[8,128,256]{2,1,0:T(8,128)(2,1)S(1)}, bf16[8,128,256]{2,1,0:T(8,128)(2,1)S(1)}, u32[]{:S(2)}, u32[]{:S(2)}) collective-permute-start(bf16[8,128,256]{2,1,0:T(8,128)(2,1)S(1)} %join.4.refs_2_.refs_0_), channel_id=1, source_target_pairs={{0,3},{1,2},{2,1},{3,0},{4,5},{5,4},{6,7},{7,6},{8,11},{9,10},{10,... | collective-permute-start | bytes 1572872 | tf_op jit(solution)/shard_map/ppermute | solution.py:49
  12.0 9.7 %collective-permute-start.4 = (bf16[4,128,256]{2,1,0:T(8,128)(2,1)S(1)}, bf16[4,128,256]{2,1,0:T(8,128)(2,1)S(1)}, u32[]{:S(2)}, u32[]{:S(2)}) collective-permute-start(bf16[4,128,256]{2,1,0:T(8,128)(2,1)S(1)} %join.5.refs_0_), channel_id=1, source_target_pairs={{0,24},{1,25},{2,26},{3,27},{4,100},{5,101},{6,102},{7,103},{8,16}... | collective-permute-start | bytes 786440 | tf_op jit(solution)/shard_map/ppermute | solution.py:49
  15.8 5.8 %collective-permute-start.5 = (bf16[4,128,256]{2,1,0:T(8,128)(2,1)S(1)}, bf16[4,128,256]{2,1,0:T(8,128)(2,1)S(1)}, u32[]{:S(2)}, u32[]{:S(2)}) collective-permute-start(bf16[4,128,256]{2,1,0:T(8,128)(2,1)S(1)} %join.6.refs_1_.refs_4_), channel_id=1, source_target_pairs={{0,8},{1,9},{2,10},{3,11},{4,36},{5,37},{6,38},{7,39},{8,0},{9,1},... | collective-permute-start | bytes 786440 | tf_op jit(solution)/shard_map/ppermute | solution.py:49
  23.9 9.0 %collective-permute-start.6 = (bf16[32,128,256]{2,1,0:T(8,128)(2,1)S(1)}, bf16[32,128,256]{2,1,0:T(8,128)(2,1)S(1)}, u32[]{:S(2)}, u32[]{:S(2)}) collective-permute-start(bf16[32,128,256]{2,1,0:T(8,128)(2,1)S(1)} %products_3.1.refs_0_), channel_id=1, source_target_pairs={{0,4},{1,5},{2,6},{3,7},{4,0},{5,1},{6,2},{7,3},{8,12},{9,13},{10,... | collective-permute-start | bytes 6291464 | tf_op jit(solution)/shard_map/ppermute | solution.py:54
  30.1 6.5 %collective-permute-start.7 = (bf16[32,128,256]{2,1,0:T(8,128)(2,1)S(1)}, bf16[32,128,256]{2,1,0:T(8,128)(2,1)S(1)}, u32[]{:S(2)}, u32[]{:S(2)}) collective-permute-start(bf16[32,128,256]{2,1,0:T(8,128)(2,1)S(1)} %products_2.1.refs_0_), channel_id=1, source_target_pairs={{0,4},{1,5},{2,6},{3,7},{4,0},{5,1},{6,2},{7,3},{8,12},{9,13},{10,... | collective-permute-start | bytes 6291464 | tf_op jit(solution)/shard_map/ppermute | solution.py:54
  33.3 14.0 %collective-permute-start.8 = (bf16[16,128,256]{2,1,0:T(8,128)(2,1)S(1)}, bf16[16,128,256]{2,1,0:T(8,128)(2,1)S(1)}, u32[]{:S(2)}, u32[]{:S(2)}) collective-permute-start(bf16[16,128,256]{2,1,0:T(8,128)(2,1)S(1)} %get-tuple-element.36.refs_0_), channel_id=1, source_target_pairs={{0,8},{1,9},{2,10},{3,11},{4,36},{5,37},{6,38},{7,39},{8,0},{9,1},... | collective-permute-start | bytes 3145736 | tf_op jit(solution)/shard_map/ppermute | solution.py:49
  33.7 15.5 %collective-permute-start.11 = (bf16[16,128,256]{2,1,0:T(8,128)(2,1)S(1)}, bf16[16,128,256]{2,1,0:T(8,128)(2,1)S(1)}, u32[]{:S(2)}, u32[]{:S(2)}) collective-permute-start(bf16[16,128,256]{2,1,0:T(8,128)(2,1)S(1)} %get-tuple-element.37.refs_1_), channel_id=1, source_target_pairs={{0,24},{1,25},{2,26},{3,27},{4,100},{5,101},{6,102},{7,103},{8,16}... | collective-permute-start | bytes 3145736 | tf_op jit(solution)/shard_map/ppermute | solution.py:49
  47.6 8.4 %collective-permute-start.9 = (bf16[8,128,256]{2,1,0:T(8,128)(2,1)S(1)}, bf16[8,128,256]{2,1,0:T(8,128)(2,1)S(1)}, u32[]{:S(2)}, u32[]{:S(2)}) collective-permute-start(bf16[8,128,256]{2,1,0:T(8,128)(2,1)S(1)} %get-tuple-element.40), channel_id=1, source_target_pairs={{0,32},{1,33},{2,34},{3,35},{4,12},{5,13},{6,14},{7,15},{8,40},{9,... | collective-permute-start | bytes 1572872 | tf_op jit(solution)/shard_map/ppermute | solution.py:49
  49.4 9.6 %collective-permute-start.12 = (bf16[8,128,256]{2,1,0:T(8,128)(2,1)S(1)}, bf16[8,128,256]{2,1,0:T(8,128)(2,1)S(1)}, u32[]{:S(2)}, u32[]{:S(2)}) collective-permute-start(bf16[8,128,256]{2,1,0:T(8,128)(2,1)S(1)} %get-tuple-element.45), channel_id=1, source_target_pairs={{0,96},{1,97},{2,98},{3,99},{4,28},{5,29},{6,30},{7,31},{8,104},{9... | collective-permute-start | bytes 1572872 | tf_op jit(solution)/shard_map/ppermute | solution.py:49
  56.2 15.5 %collective-permute-start.10 = (bf16[4,128,256]{2,1,0:T(8,128)(2,1)S(1)}, bf16[4,128,256]{2,1,0:T(8,128)(2,1)S(1)}, u32[]{:S(2)}, u32[]{:S(2)}) collective-permute-start(bf16[4,128,256]{2,1,0:T(8,128)(2,1)S(1)} %get-tuple-element.42.refs_3_), channel_id=1, source_target_pairs={{0,24},{1,25},{2,26},{3,27},{4,100},{5,101},{6,102},{7,103},{8,16}... | collective-permute-start | bytes 786440 | tf_op jit(solution)/shard_map/ppermute | solution.py:49
  59.1 12.7 %collective-permute-start.17 = (bf16[4,128,256]{2,1,0:T(8,128)(2,1)S(1)}, bf16[4,128,256]{2,1,0:T(8,128)(2,1)S(1)}, u32[]{:S(2)}, u32[]{:S(2)}) collective-permute-start(bf16[4,128,256]{2,1,0:T(8,128)(2,1)S(1)} %get-tuple-element.47.refs_7_), channel_id=1, source_target_pairs={{0,8},{1,9},{2,10},{3,11},{4,36},{5,37},{6,38},{7,39},{8,0},{9,1},... | collective-permute-start | bytes 786440 | tf_op jit(solution)/shard_map/ppermute | solution.py:49
  59.7 38.6 %copy-start = (bf16[256,256]{1,0:T(8,128)(2,1)S(1)}, bf16[256,256]{1,0:T(8,128)(2,1)}, u32[]{:S(2)}) copy-start(bf16[256,256]{1,0:T(8,128)(2,1)} %weight_ref.1) | copy-start | bytes 393220
  59.7 7.1 %collective-permute-start.13 = (bf16[128,256]{1,0:T(8,128)(2,1)S(1)}, bf16[128,256]{1,0:T(8,128)(2,1)S(1)}, u32[]{:S(2)}, u32[]{:S(2)}) collective-permute-start(bf16[128,256]{1,0:T(8,128)(2,1)S(1)} %get-tuple-element.49), channel_id=1, source_target_pairs={{0,4},{1,5},{2,6},{3,7},{4,0},{5,1},{6,2},{7,3},{8,12},{9,13},{10,... | collective-permute-start | bytes 196616 | tf_op jit(solution)/shard_map/ppermute | solution.py:54
  67.0 4.4 %collective-permute-start.14 = (bf16[128,256]{1,0:T(8,128)(2,1)S(1)}, bf16[128,256]{1,0:T(8,128)(2,1)S(1)}, u32[]{:S(2)}, u32[]{:S(2)}) collective-permute-start(bf16[128,256]{1,0:T(8,128)(2,1)S(1)} %fold.23.kept_ref), channel_id=1, source_target_pairs={{0,1},{1,0},{2,3},{3,2},{4,7},{5,6},{6,5},{7,4},{8,9},{9,8},{10,11... | collective-permute-start | bytes 196616 | tf_op jit(solution)/shard_map/ppermute | solution.py:49
  71.5 3.2 %collective-permute-start.16 = (bf16[128,256]{1,0:T(8,128)(2,1)S(1)}, bf16[128,256]{1,0:T(8,128)(2,1)S(1)}, u32[]{:S(2)}, u32[]{:S(2)}) collective-permute-start(bf16[128,256]{1,0:T(8,128)(2,1)S(1)} %fold.24.refs_0_.kept_ref), channel_id=1, source_target_pairs={{0,3},{1,2},{2,1},{3,0},{4,5},{5,4},{6,7},{7,6},{8,11},{9,10},{10,... | collective-permute-start | bytes 196616 | tf_op jit(solution)/shard_map/ppermute | solution.py:49
  71.7 9.3 %collective-permute-start.15 = (bf16[2,128,256]{2,1,0:T(8,128)(2,1)S(1)}, bf16[2,128,256]{2,1,0:T(8,128)(2,1)S(1)}, u32[]{:S(2)}, u32[]{:S(2)}) collective-permute-start(bf16[2,128,256]{2,1,0:T(8,128)(2,1)S(1)} %get-tuple-element.51), channel_id=1, source_target_pairs={{0,96},{1,97},{2,98},{3,99},{4,28},{5,29},{6,30},{7,31},{8,104},{9... | collective-permute-start | bytes 393224 | tf_op jit(solution)/shard_map/ppermute | solution.py:49
  71.9 9.1 %collective-permute-start.19 = (bf16[2,128,256]{2,1,0:T(8,128)(2,1)S(1)}, bf16[2,128,256]{2,1,0:T(8,128)(2,1)S(1)}, u32[]{:S(2)}, u32[]{:S(2)}) collective-permute-start(bf16[2,128,256]{2,1,0:T(8,128)(2,1)S(1)} %get-tuple-element.53), channel_id=1, source_target_pairs={{0,32},{1,33},{2,34},{3,35},{4,12},{5,13},{6,14},{7,15},{8,40},{9,... | collective-permute-start | bytes 393224 | tf_op jit(solution)/shard_map/ppermute | solution.py:49
  74.9 4.2 %collective-permute-start.18 = (bf16[128,256]{1,0:T(8,128)(2,1)S(1)}, bf16[128,256]{1,0:T(8,128)(2,1)S(1)}, u32[]{:S(2)}, u32[]{:S(2)}) collective-permute-start(bf16[128,256]{1,0:T(8,128)(2,1)S(1)} %fold.27.kept_ref), channel_id=1, source_target_pairs={{0,8},{1,9},{2,10},{3,11},{4,36},{5,37},{6,38},{7,39},{8,0},{9,1},... | collective-permute-start | bytes 196616 | tf_op jit(solution)/shard_map/ppermute | solution.py:49
  79.2 3.5 %collective-permute-start.20 = (bf16[128,256]{1,0:T(8,128)(2,1)S(1)}, bf16[128,256]{1,0:T(8,128)(2,1)S(1)}, u32[]{:S(2)}, u32[]{:S(2)}) collective-permute-start(bf16[128,256]{1,0:T(8,128)(2,1)S(1)} %fold.28.refs_0_.kept_ref), channel_id=1, source_target_pairs={{0,32},{1,33},{2,34},{3,35},{4,12},{5,13},{6,14},{7,15},{8,40},{9,... | collective-permute-start | bytes 196616 | tf_op jit(solution)/shard_map/ppermute | solution.py:49
  82.7 4.4 %collective-permute-start.21 = (bf16[128,256]{1,0:T(8,128)(2,1)S(1)}, bf16[128,256]{1,0:T(8,128)(2,1)S(1)}, u32[]{:S(2)}, u32[]{:S(2)}) collective-permute-start(bf16[128,256]{1,0:T(8,128)(2,1)S(1)} %fold.31.kept_ref), channel_id=1, source_target_pairs={{0,24},{1,25},{2,26},{3,27},{4,100},{5,101},{6,102},{7,103},{8,16}... | collective-permute-start | bytes 196616 | tf_op jit(solution)/shard_map/ppermute | solution.py:49
  87.3 4.7 %collective-permute-start.22 = (bf16[128,256]{1,0:T(8,128)(2,1)S(1)}, bf16[128,256]{1,0:T(8,128)(2,1)S(1)}, u32[]{:S(2)}, u32[]{:S(2)}) collective-permute-start(bf16[128,256]{1,0:T(8,128)(2,1)S(1)} %fold.32.kept_ref), channel_id=1, source_target_pairs={{0,96},{1,97},{2,98},{3,99},{4,28},{5,29},{6,30},{7,31},{8,104},{9... | collective-permute-start | bytes 196616 | tf_op jit(solution)/shard_map/ppermute | solution.py:49
  92.1 7.2 %collective-permute-start.23 = (bf16[128,256]{1,0:T(8,128)(2,1)S(1)}, bf16[128,256]{1,0:T(8,128)(2,1)S(1)}, u32[]{:S(2)}, u32[]{:S(2)}) collective-permute-start(bf16[128,256]{1,0:T(8,128)(2,1)S(1)} %fold.33), channel_id=1, source_target_pairs={{0,4},{1,5},{2,6},{3,7},{4,0},{5,1},{6,2},{7,3},{8,12},{9,13},{10,... | collective-permute-start | bytes 196616 | tf_op jit(solution)/shard_map/ppermute | solution.py:54

commit v3 on v2

--- a/solution.py
+++ b/solution.py
@@ -18,7 +18,6 @@
 CALL_SLOTS = 32
 MAX_PAIRS = 256
 UNROLL = 16
-AFTER = {1: 2, 3: 3}
 NO_BLOCK = ROWBLK << 9
 
 FLIP = {"x0": ("x", 1), "x1": ("x", 3), "z0": ("z", 1), "z1": ("z", 3), "y0": ("y", 1), "y1": ("y", 3)}
@@ -47,6 +46,19 @@
 
 def exchange(value, first, second):
     return lax.ppermute(value, AXES, exchange_pairs(first, second))
+
+
+def shift(value, first, second, hops):
+    pairs = []
+    for z in range(RING):
+        for x in range(RING):
+            for c in range(2):
+                for y in range(RING):
+                    at = {"z": z, "x": x, "c": c, "y": y}
+                    axis = first if c == 0 else second
+                    at[axis] = (at[axis] + hops) % RING
+                    pairs.append((linear(z, x, c, y), linear(**at)))
+    return lax.ppermute(value, AXES, pairs)
 
 
 def swap_cores(value):
@@ -247,6 +259,25 @@
     )(in_vmem(kept), in_vmem(got), *gates)
 
 
+def ring_kernel(own_ref, opposite_ref, left_ref, right_ref, *refs):
+    own, opposite, left, right = (
+        r[...].astype(jnp.float32) for r in (own_ref, opposite_ref, left_ref, right_ref)
+    )
+    refs[-1][...] = ((own + opposite) + (left + right)).astype(jnp.bfloat16)
+
+
+def ring_sum(own, got, gates=()):
+    return pl.pallas_call(
+        ring_kernel,
+        out_shape=pltpu.VMEM(own.shape, jnp.bfloat16),
+        in_specs=[IN_VMEM] * 4 + [ANYWHERE] * len(gates),
+        out_specs=IN_VMEM,
+        compiler_params=pltpu.CompilerParams(vmem_limit_bytes=4 << 20),
+        cost_estimate=TINY,
+        name="ring_sum",
+    )(in_vmem(own), *(in_vmem(v) for v in got), *gates)
+
+
 def features_kernel(first_ref, second_ref, weight_ref, out_ref):
     for k, ref in enumerate((first_ref, second_ref)):
         for b in range(2):
@@ -377,10 +408,11 @@
     held = [(v[p], w[p]) for p in (0, 1) for v, w in ((feats, lower), (far, upper))]
     term, other = weight_terms(core, held)
     (term,) = fold(term, swap_cores(other), 1)
-    for k, dims in enumerate((("y0", "y1"), ("y1", "y0"), ("x0", "z0"), ("z0", "x0"), ("x1", "z1"), ("z1", "x1"))):
-        got = exchange(term, *dims)
-        gates = halve(AFTER[k], [term]) if k in AFTER else ()
-        (term,) = fold(term, got, 1, gates)
+    for k, rings in enumerate((("x", "z"), ("z", "x"), ("y", "y"))):
+        got = [shift(term, *rings, hops) for hops in (2, 1, 3)]
+        term = ring_sum(term, got, lower)
+        if k < 2:
+            halve(2 + k, [term])
     theirs = swap_cores(term)
     grad_weight = jnp.concatenate([jnp.where(c == 0, term, theirs), jnp.where(c == 0, theirs, term)])
     return features_gradient(*lower, weight), grad_weight.astype(jnp.float32)

time: 99.3 us -> 90.2 us (0.908)
  waiting for transfers between devices: 42.9 us -> 24.4 us
  starting transfers between devices: 34.5 us -> 45 us
  Pallas kernels: 20.9 us -> 19.1 us
    ppermute x20 -> x14, waiting for transfers between devices: 42 us -> 20 us  [exchange(): return lax.ppermute(value, AXES, exchange_pairs(first, second))]
    ppermute x0 -> x9, starting transfers between devices: none -> 14.1 us  [shift(): return lax.ppermute(value, AXES, pairs)]
    ppermute x0 -> x9, waiting for transfers between devices: none -> 3.47 us  [shift(): return lax.ppermute(value, AXES, pairs)]
    ppermute x4, starting transfers between devices: 16.5 us -> 13.1 us  [swap_cores(): return lax.ppermute(value, AXES, pairs)]
    pallas_call x4, Pallas kernels: 9.56 us -> 8.54 us  [products(): pl.pallas_call(products_kernel, out_shape=pltpu.VMEM((CALL_SLOTS, BLOCK,...]
    pallas_call x17 -> x11, Pallas kernels: 2.9 us -> 2.2 us  [fold(): pl.pallas_call(functools.partial(fold_kernel, halves), out_shape=out, in_...]
    ppermute x20 -> x14, starting transfers between devices: 18 us -> 17.8 us  [exchange(): return lax.ppermute(value, AXES, exchange_pairs(first, second))]
  transfers between devices with their start and end apart: 24 -> 27, of which waited for: 12 -> 11; matrix products, arithmetic and copies ran while one was open for 0% -> 0% of each run, Pallas kernels for 17% -> 17%
where the time goes in v3:
time: 90.2 us; the launch traced here: 90.3 us
  starting transfers between devices  45 us (50%)
  waiting for transfers between devices  24.4 us (27%)
  Pallas kernels  19.1 us (21%)
  between operations  0.93 us (1%)
    ppermute x14, waiting for transfers between devices, exchange(): return lax.ppermute(value, AXES, exchange_pairs(first, second))  20 us
    ppermute x14, starting transfers between devices, exchange(): return lax.ppermute(value, AXES, exchange_pairs(first, second))  17.8 us
    ppermute x9, starting transfers between devices, shift(): return lax.ppermute(value, AXES, pairs)  14.1 us
    ppermute x4, starting transfers between devices, swap_cores(): return lax.ppermute(value, AXES, pairs)  13.1 us
    pallas_call x4, Pallas kernels, products(): pl.pallas_call(products_kernel, out_shape=pltpu.VMEM((CALL_SLOTS, BLOCK,...  8.54 us
    pallas_call x1, Pallas kernels, prepare(): pl.pallas_call(prepare_kernel, out_shape=(pltpu.VMEM(shape, jnp.bfloat16)...  5.41 us
    ppermute x9, waiting for transfers between devices, shift(): return lax.ppermute(value, AXES, pairs)  3.47 us
    pallas_call x11, Pallas kernels, fold(): pl.pallas_call(functools.partial(fold_kernel, halves), out_shape=out, in_...  2.2 us
  transfers between devices with their start and end apart: 27, of which 11 were waited for; matrix products, arithmetic and copies ran while one was open for 0% of the time, Pallas kernels for 17%

profile of v3, /device:TPU:1, one launch (start us, length us, event | category | flops | bytes accessed | tf_op | source)
XLA Modules:
  0.0 90.3 jit_solution(15881796622443225930)
XLA Ops:
  0.6 1.2 %load.1 = (bf16[4,128,256]{2,1,0:T(8,128)(2,1)S(1)}, bf16[2,128,256]{2,1,0:T(8,128)(2,1)S(1)}, bf16[2,128,256]{2,1,0:T(8,128)(2,1)S(1)}) custom-call(bf16[4,128,256]{2,1,0:T(8,128)(2,1)} %bitcast.10, bf16[4,128,256]{2,1,0:T(8,128)(2,1)} %bitcast.11, bf16[4,128,256]{2,1,0:T(8,128)(2,1)} %bitcast.12), custom_call_target="tpu_custom_call" | custom-call | bytes 1024 | tf_op jit(solution)/shard_map/load/pallas_call | solution.py:203
  1.9 3.6 %collective-permute-start.1 = (bf16[4,128,256]{2,1,0:T(8,128)(2,1)S(1)}, bf16[4,128,256]{2,1,0:T(8,128)(2,1)S(1)}, u32[]{:S(2)}, u32[]{:S(2)}) collective-permute-start(bf16[4,128,256]{2,1,0:T(8,128)(2,1)S(1)} %get-tuple-element.29.refs_0_), channel_id=1, source_target_pairs={{0,1},{1,0},{2,3},{3,2},{4,7},{5,6},{6,5},{7,4},{8,9},{9,8},{10,11... | collective-permute-start | bytes 786440 | tf_op jit(solution)/shard_map/ppermute | solution.py:48
  5.5 2.5 %collective-permute-start = (bf16[2,128,256]{2,1,0:T(8,128)(2,1)S(1)}, bf16[2,128,256]{2,1,0:T(8,128)(2,1)S(1)}, u32[]{:S(2)}, u32[]{:S(2)}) collective-permute-start(bf16[2,128,256]{2,1,0:T(8,128)(2,1)S(1)} %get-tuple-element.28.refs_0_), channel_id=1, source_target_pairs={{0,96},{1,97},{2,98},{3,99},{4,28},{5,29},{6,30},{7,31},{8,104},{9... | collective-permute-start | bytes 393224 | tf_op jit(solution)/shard_map/ppermute | solution.py:48
  8.0 2.8 %collective-permute-done.refs_2_.refs_1_ = bf16[2,128,256]{2,1,0:T(8,128)(2,1)S(1)} collective-permute-done((bf16[2,128,256]{2,1,0:T(8,128)(2,1)S(1)}, bf16[2,128,256]{2,1,0:T(8,128)(2,1)S(1)}, u32[]{:S(2)}, u32[]{:S(2)}) %collective-permute-start) | collective-permute-done | bytes 131104 | tf_op jit(solution)/shard_map/ppermute | solution.py:48
  10.8 1.0 %collective-permute-done.2.refs_3_.refs_1_ = bf16[2,128,256]{2,1,0:T(8,128)(2,1)S(1)} collective-permute-done((bf16[2,128,256]{2,1,0:T(8,128)(2,1)S(1)}, bf16[2,128,256]{2,1,0:T(8,128)(2,1)S(1)}, u32[]{:S(2)}, u32[]{:S(2)}) %collective-permute-start.2) | collective-permute-done | bytes 131104 | tf_op jit(solution)/shard_map/ppermute | solution.py:48
  12.0 3.8 %collective-permute-start.4 = (bf16[4,128,256]{2,1,0:T(8,128)(2,1)S(1)}, bf16[4,128,256]{2,1,0:T(8,128)(2,1)S(1)}, u32[]{:S(2)}, u32[]{:S(2)}) collective-permute-start(bf16[4,128,256]{2,1,0:T(8,128)(2,1)S(1)} %join.5.refs_0_), channel_id=1, source_target_pairs={{0,24},{1,25},{2,26},{3,27},{4,100},{5,101},{6,102},{7,103},{8,16}... | collective-permute-start | bytes 786440 | tf_op jit(solution)/shard_map/ppermute | solution.py:48
  16.0 5.4 %prepare.1 = (bf16[512,128,128]{2,1,0:T(8,128)(2,1)S(1)}, s32[1,640]{1,0:T(1,128)S(1)}, s32[1,640]{1,0:T(1,128)S(1)}, s32[1,640]{1,0:T(1,128)S(1)}, s32[1,640]{1,0:T(1,128)S(1)}) custom-call(s32[4]{0:T(128)S(1)} %pad_add_fusion.where_ref, s32[16]{0:T(128)} %bitcast.13, s32[16,32]{1,0:T(8,128)} %cols_ref.1, bf16[512,128,128]{2,1,0:T(8,128)(2,1)} %bitcast.9, ...), custom_call_target="tpu_custom_call" | custom-call | bytes 1024 | tf_op jit(solution)/shard_map/prepare/pallas_call | solution.py:158
  21.6 2.1 %products_3.1.refs_0_ = bf16[32,128,256]{2,1,0:T(8,128)(2,1)S(1)} custom-call(s32[1,640]{1,0:T(1,128)S(1)} %get-tuple-element.35.words_ref, bf16[17,128,256]{2,1,0:T(8,128)(2,1)S(1)} %join.7.grad_ref, bf16[512,128,128]{2,1,0:T(8,128)(2,1)S(1)} %get-tuple-element.32.refs_2_.adj_ref), custom_call_target="tpu_custom_call" | custom-call | bytes 1024 | tf_op jit(solution)/shard_map/products_3/pallas_call | solution.py:356
  23.7 4.3 %collective-permute-start.6 = (bf16[32,128,256]{2,1,0:T(8,128)(2,1)S(1)}, bf16[32,128,256]{2,1,0:T(8,128)(2,1)S(1)}, u32[]{:S(2)}, u32[]{:S(2)}) collective-permute-start(bf16[32,128,256]{2,1,0:T(8,128)(2,1)S(1)} %products_3.1.refs_0_), channel_id=1, source_target_pairs={{0,4},{1,5},{2,6},{3,7},{4,0},{5,1},{6,2},{7,3},{8,12},{9,13},{10,... | collective-permute-start | bytes 6291464 | tf_op jit(solution)/shard_map/ppermute | solution.py:66
  28.0 2.1 %products_2.1.refs_0_ = bf16[32,128,256]{2,1,0:T(8,128)(2,1)S(1)} custom-call(s32[1,640]{1,0:T(1,128)S(1)} %get-tuple-element.34.words_ref, bf16[17,128,256]{2,1,0:T(8,128)(2,1)S(1)} %join.7.grad_ref, bf16[512,128,128]{2,1,0:T(8,128)(2,1)S(1)} %get-tuple-element.32.refs_2_.adj_ref, bf16[32,128,256]{2,1,0:T(8,128)(2,1)S(1)} %products_3.1.refs_0_), custom_call_target="tpu_custom_call" | custom-call | bytes 1024 | tf_op jit(solution)/shard_map/products_2/pallas_call | solution.py:356
  30.2 2.1 %products_1.1.kept_ref = bf16[32,128,256]{2,1,0:T(8,128)(2,1)S(1)} custom-call(s32[1,640]{1,0:T(1,128)S(1)} %get-tuple-element.33.words_ref, bf16[17,128,256]{2,1,0:T(8,128)(2,1)S(1)} %join.7.grad_ref, bf16[512,128,128]{2,1,0:T(8,128)(2,1)S(1)} %get-tuple-element.32.refs_2_.adj_ref, bf16[32,128,256]{2,1,0:T(8,128)(2,1)S(1)} %products_2.1.refs_0_), custom_call_target="tpu_custom_call" | custom-call | bytes 1024 | tf_op jit(solution)/shard_map/products_1/pallas_call | solution.py:356
  32.9 1.5 %collective-permute-start.11 = (bf16[16,128,256]{2,1,0:T(8,128)(2,1)S(1)}, bf16[16,128,256]{2,1,0:T(8,128)(2,1)S(1)}, u32[]{:S(2)}, u32[]{:S(2)}) collective-permute-start(bf16[16,128,256]{2,1,0:T(8,128)(2,1)S(1)} %get-tuple-element.37.refs_1_), channel_id=1, source_target_pairs={{0,24},{1,25},{2,26},{3,27},{4,100},{5,101},{6,102},{7,103},{8,16}... | collective-permute-start | bytes 3145736 | tf_op jit(solution)/shard_map/ppermute | solution.py:48
  34.4 2.1 %products_0.1.kept_ref = bf16[32,128,256]{2,1,0:T(8,128)(2,1)S(1)} custom-call(s32[1,640]{1,0:T(1,128)S(1)} %get-tuple-element.31.words_ref, bf16[17,128,256]{2,1,0:T(8,128)(2,1)S(1)} %join.7.grad_ref, bf16[512,128,128]{2,1,0:T(8,128)(2,1)S(1)} %get-tuple-element.32.refs_2_.adj_ref, bf16[16,128,256]{2,1,0:T(8,128)(2,1)S(1)} %get-tuple-element.36.refs_0_, ...), custom_call_target="tpu_custom_call" | custom-call | bytes 1024 | tf_op jit(solution)/shard_map/products_0/pallas_call | solution.py:356
  37.1 9.7 %collective-permute-done.8.got_ref = bf16[16,128,256]{2,1,0:T(8,128)(2,1)S(1)} collective-permute-done((bf16[16,128,256]{2,1,0:T(8,128)(2,1)S(1)}, bf16[16,128,256]{2,1,0:T(8,128)(2,1)S(1)}, u32[]{:S(2)}, u32[]{:S(2)}) %collective-permute-start.8) | collective-permute-done | bytes 1048608 | tf_op jit(solution)/shard_map/ppermute | solution.py:48
  47.1 1.0 %collective-permute-start.9 = (bf16[8,128,256]{2,1,0:T(8,128)(2,1)S(1)}, bf16[8,128,256]{2,1,0:T(8,128)(2,1)S(1)}, u32[]{:S(2)}, u32[]{:S(2)}) collective-permute-start(bf16[8,128,256]{2,1,0:T(8,128)(2,1)S(1)} %get-tuple-element.40), channel_id=1, source_target_pairs={{0,32},{1,33},{2,34},{3,35},{4,12},{5,13},{6,14},{7,15},{8,40},{9,... | collective-permute-start | bytes 1572872 | tf_op jit(solution)/shard_map/ppermute | solution.py:48
  48.4 2.1 %collective-permute-start.12 = (bf16[8,128,256]{2,1,0:T(8,128)(2,1)S(1)}, bf16[8,128,256]{2,1,0:T(8,128)(2,1)S(1)}, u32[]{:S(2)}, u32[]{:S(2)}) collective-permute-start(bf16[8,128,256]{2,1,0:T(8,128)(2,1)S(1)} %get-tuple-element.45), channel_id=1, source_target_pairs={{0,96},{1,97},{2,98},{3,99},{4,28},{5,29},{6,30},{7,31},{8,104},{9... | collective-permute-start | bytes 1572872 | tf_op jit(solution)/shard_map/ppermute | solution.py:48
  50.5 5.0 %collective-permute-done.9.got_ref = bf16[8,128,256]{2,1,0:T(8,128)(2,1)S(1)} collective-permute-done((bf16[8,128,256]{2,1,0:T(8,128)(2,1)S(1)}, bf16[8,128,256]{2,1,0:T(8,128)(2,1)S(1)}, u32[]{:S(2)}, u32[]{:S(2)}) %collective-permute-start.9) | collective-permute-done | bytes 524320 | tf_op jit(solution)/shard_map/ppermute | solution.py:48
  55.7 1.0 %collective-permute-start.10 = (bf16[4,128,256]{2,1,0:T(8,128)(2,1)S(1)}, bf16[4,128,256]{2,1,0:T(8,128)(2,1)S(1)}, u32[]{:S(2)}, u32[]{:S(2)}) collective-permute-start(bf16[4,128,256]{2,1,0:T(8,128)(2,1)S(1)} %get-tuple-element.42.refs_3_), channel_id=1, source_target_pairs={{0,24},{1,25},{2,26},{3,27},{4,100},{5,101},{6,102},{7,103},{8,16}... | collective-permute-start | bytes 786440 | tf_op jit(solution)/shard_map/ppermute | solution.py:48
  56.7 1.3 %collective-permute-done.12.got_ref = bf16[8,128,256]{2,1,0:T(8,128)(2,1)S(1)} collective-permute-done((bf16[8,128,256]{2,1,0:T(8,128)(2,1)S(1)}, bf16[8,128,256]{2,1,0:T(8,128)(2,1)S(1)}, u32[]{:S(2)}, u32[]{:S(2)}) %collective-permute-start.12) | collective-permute-done | bytes 524320 | tf_op jit(solution)/shard_map/ppermute | solution.py:48
  59.0 4.3 %collective-permute-start.13 = (bf16[128,256]{1,0:T(8,128)(2,1)S(1)}, bf16[128,256]{1,0:T(8,128)(2,1)S(1)}, u32[]{:S(2)}, u32[]{:S(2)}) collective-permute-start(bf16[128,256]{1,0:T(8,128)(2,1)S(1)} %get-tuple-element.49), channel_id=1, source_target_pairs={{0,4},{1,5},{2,6},{3,7},{4,0},{5,1},{6,2},{7,3},{8,12},{9,13},{10,... | collective-permute-start | bytes 196616 | tf_op jit(solution)/shard_map/ppermute | solution.py:66
  64.4 1.9 %collective-permute-start.14 = (bf16[128,256]{1,0:T(8,128)(2,1)S(1)}, bf16[128,256]{1,0:T(8,128)(2,1)S(1)}, u32[]{:S(2)}, u32[]{:S(2)}) collective-permute-start(bf16[128,256]{1,0:T(8,128)(2,1)S(1)} %fold.17.own_ref), channel_id=1, source_target_pairs={{0,16},{1,17},{2,18},{3,19},{4,68},{5,69},{6,70},{7,71},{8,24},{9,... | collective-permute-start | bytes 196616 | tf_op jit(solution)/shard_map/ppermute | solution.py:61
  67.1 1.9 %collective-permute-start.16 = (bf16[128,256]{1,0:T(8,128)(2,1)S(1)}, bf16[128,256]{1,0:T(8,128)(2,1)S(1)}, u32[]{:S(2)}, u32[]{:S(2)}) collective-permute-start(bf16[128,256]{1,0:T(8,128)(2,1)S(1)} %fold.17.own_ref), channel_id=1, source_target_pairs={{0,24},{1,25},{2,26},{3,27},{4,100},{5,101},{6,102},{7,103},{8,0},... | collective-permute-start | bytes 196616 | tf_op jit(solution)/shard_map/ppermute | solution.py:61
  69.1 1.5 %collective-permute-done.15.left_ref = bf16[128,256]{1,0:T(8,128)(2,1)S(1)} collective-permute-done((bf16[128,256]{1,0:T(8,128)(2,1)S(1)}, bf16[128,256]{1,0:T(8,128)(2,1)S(1)}, u32[]{:S(2)}, u32[]{:S(2)}) %collective-permute-start.15) | collective-permute-done | bytes 65568 | tf_op jit(solution)/shard_map/ppermute | solution.py:61
  70.7 1.0 %collective-permute-start.18 = (bf16[128,256]{1,0:T(8,128)(2,1)S(1)}, bf16[128,256]{1,0:T(8,128)(2,1)S(1)}, u32[]{:S(2)}, u32[]{:S(2)}) collective-permute-start(bf16[128,256]{1,0:T(8,128)(2,1)S(1)} %ring_sum.3.refs_0_.own_ref), channel_id=1, source_target_pairs={{0,64},{1,65},{2,66},{3,67},{4,20},{5,21},{6,22},{7,23},{8,72},{9,... | collective-permute-start | bytes 196616 | tf_op jit(solution)/shard_map/ppermute | solution.py:61
  71.7 1.1 %collective-permute-start.19 = (bf16[128,256]{1,0:T(8,128)(2,1)S(1)}, bf16[128,256]{1,0:T(8,128)(2,1)S(1)}, u32[]{:S(2)}, u32[]{:S(2)}) collective-permute-start(bf16[128,256]{1,0:T(8,128)(2,1)S(1)} %ring_sum.3.refs_0_.own_ref), channel_id=1, source_target_pairs={{0,32},{1,33},{2,34},{3,35},{4,12},{5,13},{6,14},{7,15},{8,40},{9,... | collective-permute-start | bytes 196616 | tf_op jit(solution)/shard_map/ppermute | solution.py:61
  72.8 2.1 %collective-permute-start.20 = (bf16[128,256]{1,0:T(8,128)(2,1)S(1)}, bf16[128,256]{1,0:T(8,128)(2,1)S(1)}, u32[]{:S(2)}, u32[]{:S(2)}) collective-permute-start(bf16[128,256]{1,0:T(8,128)(2,1)S(1)} %ring_sum.3.refs_0_.own_ref), channel_id=1, source_target_pairs={{0,96},{1,97},{2,98},{3,99},{4,28},{5,29},{6,30},{7,31},{8,104},{9... | collective-permute-start | bytes 196616 | tf_op jit(solution)/shard_map/ppermute | solution.py:61
  75.0 1.5 %collective-permute-start.17 = (bf16[2,128,256]{2,1,0:T(8,128)(2,1)S(1)}, bf16[2,128,256]{2,1,0:T(8,128)(2,1)S(1)}, u32[]{:S(2)}, u32[]{:S(2)}) collective-permute-start(bf16[2,128,256]{2,1,0:T(8,128)(2,1)S(1)} %get-tuple-element.51), channel_id=1, source_target_pairs={{0,96},{1,97},{2,98},{3,99},{4,28},{5,29},{6,30},{7,31},{8,104},{9... | collective-permute-start | bytes 393224 | tf_op jit(solution)/shard_map/ppermute | solution.py:48
  76.7 2.7 %collective-permute-start.23 = (bf16[128,256]{1,0:T(8,128)(2,1)S(1)}, bf16[128,256]{1,0:T(8,128)(2,1)S(1)}, u32[]{:S(2)}, u32[]{:S(2)}) collective-permute-start(bf16[128,256]{1,0:T(8,128)(2,1)S(1)} %ring_sum.4.refs_0_.own_ref), channel_id=1, source_target_pairs={{0,2},{1,3},{2,0},{3,1},{4,6},{5,7},{6,4},{7,5},{8,10},{9,11},{10,... | collective-permute-start | bytes 196616 | tf_op jit(solution)/shard_map/ppermute | solution.py:61
  79.5 2.6 %collective-permute-start.25 = (bf16[128,256]{1,0:T(8,128)(2,1)S(1)}, bf16[128,256]{1,0:T(8,128)(2,1)S(1)}, u32[]{:S(2)}, u32[]{:S(2)}) collective-permute-start(bf16[128,256]{1,0:T(8,128)(2,1)S(1)} %ring_sum.4.refs_0_.own_ref), channel_id=1, source_target_pairs={{0,3},{1,0},{2,1},{3,2},{4,7},{5,4},{6,5},{7,6},{8,11},{9,8},{10,9... | collective-permute-start | bytes 196616 | tf_op jit(solution)/shard_map/ppermute | solution.py:61
  82.2 1.5 %collective-permute-done.24.left_ref = bf16[128,256]{1,0:T(8,128)(2,1)S(1)} collective-permute-done((bf16[128,256]{1,0:T(8,128)(2,1)S(1)}, bf16[128,256]{1,0:T(8,128)(2,1)S(1)}, u32[]{:S(2)}, u32[]{:S(2)}) %collective-permute-start.24) | collective-permute-done | bytes 65568 | tf_op jit(solution)/shard_map/ppermute | solution.py:61
  84.1 4.4 %collective-permute-start.26 = (bf16[128,256]{1,0:T(8,128)(2,1)S(1)}, bf16[128,256]{1,0:T(8,128)(2,1)S(1)}, u32[]{:S(2)}, u32[]{:S(2)}) collective-permute-start(bf16[128,256]{1,0:T(8,128)(2,1)S(1)} %ring_sum.5), channel_id=1, source_target_pairs={{0,4},{1,5},{2,6},{3,7},{4,0},{5,1},{6,2},{7,3},{8,12},{9,13},{10,... | collective-permute-start | bytes 196616 | tf_op jit(solution)/shard_map/ppermute | solution.py:66
  88.5 1.0 %features_gradient.1 = bf16[512,256]{1,0:T(8,128)(2,1)} custom-call(bf16[2,128,256]{2,1,0:T(8,128)(2,1)S(1)} %fold.20.first_ref.refs_0_, bf16[2,128,256]{2,1,0:T(8,128)(2,1)S(1)} %fold.21.second_ref.refs_1_, bf16[256,256]{1,0:T(8,128)(2,1)S(1)} %copy-done), custom_call_target="tpu_custom_call" | custom-call | bytes 1024 | tf_op jit(solution)/shard_map/features_gradient/pallas_call | solution.py:292
  (53 shorter events, 6.8 us)
Async XLA Ops:
  1.9 9.9 %collective-permute-start.1 = (bf16[4,128,256]{2,1,0:T(8,128)(2,1)S(1)}, bf16[4,128,256]{2,1,0:T(8,128)(2,1)S(1)}, u32[]{:S(2)}, u32[]{:S(2)}) collective-permute-start(bf16[4,128,256]{2,1,0:T(8,128)(2,1)S(1)} %get-tuple-element.29.refs_0_), channel_id=1, source_target_pairs={{0,1},{1,0},{2,3},{3,2},{4,7},{5,6},{6,5},{7,4},{8,9},{9,8},{10,11... | collective-permute-start | bytes 786440 | tf_op jit(solution)/shard_map/ppermute | solution.py:48
  5.5 5.3 %collective-permute-start = (bf16[2,128,256]{2,1,0:T(8,128)(2,1)S(1)}, bf16[2,128,256]{2,1,0:T(8,128)(2,1)S(1)}, u32[]{:S(2)}, u32[]{:S(2)}) collective-permute-start(bf16[2,128,256]{2,1,0:T(8,128)(2,1)S(1)} %get-tuple-element.28.refs_0_), channel_id=1, source_target_pairs={{0,96},{1,97},{2,98},{3,99},{4,28},{5,29},{6,30},{7,31},{8,104},{9... | collective-permute-start | bytes 393224 | tf_op jit(solution)/shard_map/ppermute | solution.py:48
  8.0 3.8 %collective-permute-start.2 = (bf16[2,128,256]{2,1,0:T(8,128)(2,1)S(1)}, bf16[2,128,256]{2,1,0:T(8,128)(2,1)S(1)}, u32[]{:S(2)}, u32[]{:S(2)}) collective-permute-start(bf16[2,128,256]{2,1,0:T(8,128)(2,1)S(1)} %get-tuple-element.30.refs_0_), channel_id=1, source_target_pairs={{0,32},{1,33},{2,34},{3,35},{4,12},{5,13},{6,14},{7,15},{8,40},{9,... | collective-permute-start | bytes 393224 | tf_op jit(solution)/shard_map/ppermute | solution.py:48
  11.8 9.6 %collective-permute-start.3 = (bf16[8,128,256]{2,1,0:T(8,128)(2,1)S(1)}, bf16[8,128,256]{2,1,0:T(8,128)(2,1)S(1)}, u32[]{:S(2)}, u32[]{:S(2)}) collective-permute-start(bf16[8,128,256]{2,1,0:T(8,128)(2,1)S(1)} %join.4.refs_2_.refs_0_), channel_id=1, source_target_pairs={{0,3},{1,2},{2,1},{3,0},{4,5},{5,4},{6,7},{7,6},{8,11},{9,10},{10,... | collective-permute-start | bytes 1572872 | tf_op jit(solution)/shard_map/ppermute | solution.py:48
  12.0 9.5 %collective-permute-start.4 = (bf16[4,128,256]{2,1,0:T(8,128)(2,1)S(1)}, bf16[4,128,256]{2,1,0:T(8,128)(2,1)S(1)}, u32[]{:S(2)}, u32[]{:S(2)}) collective-permute-start(bf16[4,128,256]{2,1,0:T(8,128)(2,1)S(1)} %join.5.refs_0_), channel_id=1, source_target_pairs={{0,24},{1,25},{2,26},{3,27},{4,100},{5,101},{6,102},{7,103},{8,16}... | collective-permute-start | bytes 786440 | tf_op jit(solution)/shard_map/ppermute | solution.py:48
  15.8 5.6 %collective-permute-start.5 = (bf16[4,128,256]{2,1,0:T(8,128)(2,1)S(1)}, bf16[4,128,256]{2,1,0:T(8,128)(2,1)S(1)}, u32[]{:S(2)}, u32[]{:S(2)}) collective-permute-start(bf16[4,128,256]{2,1,0:T(8,128)(2,1)S(1)} %join.6.refs_1_.refs_4_), channel_id=1, source_target_pairs={{0,8},{1,9},{2,10},{3,11},{4,36},{5,37},{6,38},{7,39},{8,0},{9,1},... | collective-permute-start | bytes 786440 | tf_op jit(solution)/shard_map/ppermute | solution.py:48
  23.7 8.6 %collective-permute-start.6 = (bf16[32,128,256]{2,1,0:T(8,128)(2,1)S(1)}, bf16[32,128,256]{2,1,0:T(8,128)(2,1)S(1)}, u32[]{:S(2)}, u32[]{:S(2)}) collective-permute-start(bf16[32,128,256]{2,1,0:T(8,128)(2,1)S(1)} %products_3.1.refs_0_), channel_id=1, source_target_pairs={{0,4},{1,5},{2,6},{3,7},{4,0},{5,1},{6,2},{7,3},{8,12},{9,13},{10,... | collective-permute-start | bytes 6291464 | tf_op jit(solution)/shard_map/ppermute | solution.py:66
  30.1 6.5 %collective-permute-start.7 = (bf16[32,128,256]{2,1,0:T(8,128)(2,1)S(1)}, bf16[32,128,256]{2,1,0:T(8,128)(2,1)S(1)}, u32[]{:S(2)}, u32[]{:S(2)}) collective-permute-start(bf16[32,128,256]{2,1,0:T(8,128)(2,1)S(1)} %products_2.1.refs_0_), channel_id=1, source_target_pairs={{0,4},{1,5},{2,6},{3,7},{4,0},{5,1},{6,2},{7,3},{8,12},{9,13},{10,... | collective-permute-start | bytes 6291464 | tf_op jit(solution)/shard_map/ppermute | solution.py:66
  32.8 14.0 %collective-permute-start.8 = (bf16[16,128,256]{2,1,0:T(8,128)(2,1)S(1)}, bf16[16,128,256]{2,1,0:T(8,128)(2,1)S(1)}, u32[]{:S(2)}, u32[]{:S(2)}) collective-permute-start(bf16[16,128,256]{2,1,0:T(8,128)(2,1)S(1)} %get-tuple-element.36.refs_0_), channel_id=1, source_target_pairs={{0,8},{1,9},{2,10},{3,11},{4,36},{5,37},{6,38},{7,39},{8,0},{9,1},... | collective-permute-start | bytes 3145736 | tf_op jit(solution)/shard_map/ppermute | solution.py:48
  32.9 15.2 %collective-permute-start.11 = (bf16[16,128,256]{2,1,0:T(8,128)(2,1)S(1)}, bf16[16,128,256]{2,1,0:T(8,128)(2,1)S(1)}, u32[]{:S(2)}, u32[]{:S(2)}) collective-permute-start(bf16[16,128,256]{2,1,0:T(8,128)(2,1)S(1)} %get-tuple-element.37.refs_1_), channel_id=1, source_target_pairs={{0,24},{1,25},{2,26},{3,27},{4,100},{5,101},{6,102},{7,103},{8,16}... | collective-permute-start | bytes 3145736 | tf_op jit(solution)/shard_map/ppermute | solution.py:48
  47.1 8.4 %collective-permute-start.9 = (bf16[8,128,256]{2,1,0:T(8,128)(2,1)S(1)}, bf16[8,128,256]{2,1,0:T(8,128)(2,1)S(1)}, u32[]{:S(2)}, u32[]{:S(2)}) collective-permute-start(bf16[8,128,256]{2,1,0:T(8,128)(2,1)S(1)} %get-tuple-element.40), channel_id=1, source_target_pairs={{0,32},{1,33},{2,34},{3,35},{4,12},{5,13},{6,14},{7,15},{8,40},{9,... | collective-permute-start | bytes 1572872 | tf_op jit(solution)/shard_map/ppermute | solution.py:48
  48.4 9.6 %collective-permute-start.12 = (bf16[8,128,256]{2,1,0:T(8,128)(2,1)S(1)}, bf16[8,128,256]{2,1,0:T(8,128)(2,1)S(1)}, u32[]{:S(2)}, u32[]{:S(2)}) collective-permute-start(bf16[8,128,256]{2,1,0:T(8,128)(2,1)S(1)} %get-tuple-element.45), channel_id=1, source_target_pairs={{0,96},{1,97},{2,98},{3,99},{4,28},{5,29},{6,30},{7,31},{8,104},{9... | collective-permute-start | bytes 1572872 | tf_op jit(solution)/shard_map/ppermute | solution.py:48
  55.7 19.2 %collective-permute-start.10 = (bf16[4,128,256]{2,1,0:T(8,128)(2,1)S(1)}, bf16[4,128,256]{2,1,0:T(8,128)(2,1)S(1)}, u32[]{:S(2)}, u32[]{:S(2)}) collective-permute-start(bf16[4,128,256]{2,1,0:T(8,128)(2,1)S(1)} %get-tuple-element.42.refs_3_), channel_id=1, source_target_pairs={{0,24},{1,25},{2,26},{3,27},{4,100},{5,101},{6,102},{7,103},{8,16}... | collective-permute-start | bytes 786440 | tf_op jit(solution)/shard_map/ppermute | solution.py:48
  58.1 18.4 %collective-permute-start.21 = (bf16[4,128,256]{2,1,0:T(8,128)(2,1)S(1)}, bf16[4,128,256]{2,1,0:T(8,128)(2,1)S(1)}, u32[]{:S(2)}, u32[]{:S(2)}) collective-permute-start(bf16[4,128,256]{2,1,0:T(8,128)(2,1)S(1)} %get-tuple-element.47.refs_7_), channel_id=1, source_target_pairs={{0,8},{1,9},{2,10},{3,11},{4,36},{5,37},{6,38},{7,39},{8,0},{9,1},... | collective-permute-start | bytes 786440 | tf_op jit(solution)/shard_map/ppermute | solution.py:48
  59.0 5.2 %collective-permute-start.13 = (bf16[128,256]{1,0:T(8,128)(2,1)S(1)}, bf16[128,256]{1,0:T(8,128)(2,1)S(1)}, u32[]{:S(2)}, u32[]{:S(2)}) collective-permute-start(bf16[128,256]{1,0:T(8,128)(2,1)S(1)} %get-tuple-element.49), channel_id=1, source_target_pairs={{0,4},{1,5},{2,6},{3,7},{4,0},{5,1},{6,2},{7,3},{8,12},{9,13},{10,... | collective-permute-start | bytes 196616 | tf_op jit(solution)/shard_map/ppermute | solution.py:66
  64.4 24.1 %copy-start = (bf16[256,256]{1,0:T(8,128)(2,1)S(1)}, bf16[256,256]{1,0:T(8,128)(2,1)}, u32[]{:S(2)}) copy-start(bf16[256,256]{1,0:T(8,128)(2,1)} %weight_ref.1) | copy-start | bytes 393220
  64.4 4.7 %collective-permute-start.14 = (bf16[128,256]{1,0:T(8,128)(2,1)S(1)}, bf16[128,256]{1,0:T(8,128)(2,1)S(1)}, u32[]{:S(2)}, u32[]{:S(2)}) collective-permute-start(bf16[128,256]{1,0:T(8,128)(2,1)S(1)} %fold.17.own_ref), channel_id=1, source_target_pairs={{0,16},{1,17},{2,18},{3,19},{4,68},{5,69},{6,70},{7,71},{8,24},{9,... | collective-permute-start | bytes 196616 | tf_op jit(solution)/shard_map/ppermute | solution.py:61
  66.3 4.3 %collective-permute-start.15 = (bf16[128,256]{1,0:T(8,128)(2,1)S(1)}, bf16[128,256]{1,0:T(8,128)(2,1)S(1)}, u32[]{:S(2)}, u32[]{:S(2)}) collective-permute-start(bf16[128,256]{1,0:T(8,128)(2,1)S(1)} %fold.17.own_ref), channel_id=1, source_target_pairs={{0,8},{1,9},{2,10},{3,11},{4,36},{5,37},{6,38},{7,39},{8,16},{9,17... | collective-permute-start | bytes 196616 | tf_op jit(solution)/shard_map/ppermute | solution.py:61
  67.1 3.6 %collective-permute-start.16 = (bf16[128,256]{1,0:T(8,128)(2,1)S(1)}, bf16[128,256]{1,0:T(8,128)(2,1)S(1)}, u32[]{:S(2)}, u32[]{:S(2)}) collective-permute-start(bf16[128,256]{1,0:T(8,128)(2,1)S(1)} %fold.17.own_ref), channel_id=1, source_target_pairs={{0,24},{1,25},{2,26},{3,27},{4,100},{5,101},{6,102},{7,103},{8,0},... | collective-permute-start | bytes 196616 | tf_op jit(solution)/shard_map/ppermute | solution.py:61
  70.7 6.0 %collective-permute-start.18 = (bf16[128,256]{1,0:T(8,128)(2,1)S(1)}, bf16[128,256]{1,0:T(8,128)(2,1)S(1)}, u32[]{:S(2)}, u32[]{:S(2)}) collective-permute-start(bf16[128,256]{1,0:T(8,128)(2,1)S(1)} %ring_sum.3.refs_0_.own_ref), channel_id=1, source_target_pairs={{0,64},{1,65},{2,66},{3,67},{4,20},{5,21},{6,22},{7,23},{8,72},{9,... | collective-permute-start | bytes 196616 | tf_op jit(solution)/shard_map/ppermute | solution.py:61
  71.7 5.0 %collective-permute-start.19 = (bf16[128,256]{1,0:T(8,128)(2,1)S(1)}, bf16[128,256]{1,0:T(8,128)(2,1)S(1)}, u32[]{:S(2)}, u32[]{:S(2)}) collective-permute-start(bf16[128,256]{1,0:T(8,128)(2,1)S(1)} %ring_sum.3.refs_0_.own_ref), channel_id=1, source_target_pairs={{0,32},{1,33},{2,34},{3,35},{4,12},{5,13},{6,14},{7,15},{8,40},{9,... | collective-permute-start | bytes 196616 | tf_op jit(solution)/shard_map/ppermute | solution.py:61
  72.8 3.9 %collective-permute-start.20 = (bf16[128,256]{1,0:T(8,128)(2,1)S(1)}, bf16[128,256]{1,0:T(8,128)(2,1)S(1)}, u32[]{:S(2)}, u32[]{:S(2)}) collective-permute-start(bf16[128,256]{1,0:T(8,128)(2,1)S(1)} %ring_sum.3.refs_0_.own_ref), channel_id=1, source_target_pairs={{0,96},{1,97},{2,98},{3,99},{4,28},{5,29},{6,30},{7,31},{8,104},{9... | collective-permute-start | bytes 196616 | tf_op jit(solution)/shard_map/ppermute | solution.py:61
  75.0 7.2 %collective-permute-start.17 = (bf16[2,128,256]{2,1,0:T(8,128)(2,1)S(1)}, bf16[2,128,256]{2,1,0:T(8,128)(2,1)S(1)}, u32[]{:S(2)}, u32[]{:S(2)}) collective-permute-start(bf16[2,128,256]{2,1,0:T(8,128)(2,1)S(1)} %get-tuple-element.51), channel_id=1, source_target_pairs={{0,96},{1,97},{2,98},{3,99},{4,28},{5,29},{6,30},{7,31},{8,104},{9... | collective-permute-start | bytes 393224 | tf_op jit(solution)/shard_map/ppermute | solution.py:48
  76.6 5.6 %collective-permute-start.22 = (bf16[2,128,256]{2,1,0:T(8,128)(2,1)S(1)}, bf16[2,128,256]{2,1,0:T(8,128)(2,1)S(1)}, u32[]{:S(2)}, u32[]{:S(2)}) collective-permute-start(bf16[2,128,256]{2,1,0:T(8,128)(2,1)S(1)} %get-tuple-element.53), channel_id=1, source_target_pairs={{0,32},{1,33},{2,34},{3,35},{4,12},{5,13},{6,14},{7,15},{8,40},{9,... | collective-permute-start | bytes 393224 | tf_op jit(solution)/shard_map/ppermute | solution.py:48
  76.7 5.5 %collective-permute-start.23 = (bf16[128,256]{1,0:T(8,128)(2,1)S(1)}, bf16[128,256]{1,0:T(8,128)(2,1)S(1)}, u32[]{:S(2)}, u32[]{:S(2)}) collective-permute-start(bf16[128,256]{1,0:T(8,128)(2,1)S(1)} %ring_sum.4.refs_0_.own_ref), channel_id=1, source_target_pairs={{0,2},{1,3},{2,0},{3,1},{4,6},{5,7},{6,4},{7,5},{8,10},{9,11},{10,... | collective-permute-start | bytes 196616 | tf_op jit(solution)/shard_map/ppermute | solution.py:61
  79.4 4.3 %collective-permute-start.24 = (bf16[128,256]{1,0:T(8,128)(2,1)S(1)}, bf16[128,256]{1,0:T(8,128)(2,1)S(1)}, u32[]{:S(2)}, u32[]{:S(2)}) collective-permute-start(bf16[128,256]{1,0:T(8,128)(2,1)S(1)} %ring_sum.4.refs_0_.own_ref), channel_id=1, source_target_pairs={{0,1},{1,2},{2,3},{3,0},{4,5},{5,6},{6,7},{7,4},{8,9},{9,10},{10,1... | collective-permute-start | bytes 196616 | tf_op jit(solution)/shard_map/ppermute | solution.py:61
  79.5 4.5 %collective-permute-start.25 = (bf16[128,256]{1,0:T(8,128)(2,1)S(1)}, bf16[128,256]{1,0:T(8,128)(2,1)S(1)}, u32[]{:S(2)}, u32[]{:S(2)}) collective-permute-start(bf16[128,256]{1,0:T(8,128)(2,1)S(1)} %ring_sum.4.refs_0_.own_ref), channel_id=1, source_target_pairs={{0,3},{1,0},{2,1},{3,2},{4,7},{5,4},{6,5},{7,6},{8,11},{9,8},{10,9... | collective-permute-start | bytes 196616 | tf_op jit(solution)/shard_map/ppermute | solution.py:61
  84.1 5.5 %collective-permute-start.26 = (bf16[128,256]{1,0:T(8,128)(2,1)S(1)}, bf16[128,256]{1,0:T(8,128)(2,1)S(1)}, u32[]{:S(2)}, u32[]{:S(2)}) collective-permute-start(bf16[128,256]{1,0:T(8,128)(2,1)S(1)} %ring_sum.5), channel_id=1, source_target_pairs={{0,4},{1,5},{2,6},{3,7},{4,0},{5,1},{6,2},{7,3},{8,12},{9,13},{10,... | collective-permute-start | bytes 196616 | tf_op jit(solution)/shard_map/ppermute | solution.py:66

commit v4 on v3

--- a/solution.py
+++ b/solution.py
@@ -408,6 +408,7 @@
     held = [(v[p], w[p]) for p in (0, 1) for v, w in ((feats, lower), (far, upper))]
     term, other = weight_terms(core, held)
     (term,) = fold(term, swap_cores(other), 1)
+    upper[1] = join([upper[1]], [term])
     for k, rings in enumerate((("x", "z"), ("z", "x"), ("y", "y"))):
         got = [shift(term, *rings, hops) for hops in (2, 1, 3)]
         term = ring_sum(term, got, lower)

time: 90.2 us -> 89.4 us (level)
  starting transfers between devices: 45 us -> 39.1 us
  waiting for transfers between devices: 24.4 us -> 29.8 us
    ppermute x14, waiting for transfers between devices: 20 us -> 22.8 us  [exchange(): return lax.ppermute(value, AXES, exchange_pairs(first, second))]
    ppermute x9, starting transfers between devices: 14.1 us -> 11.5 us  [shift(): return lax.ppermute(value, AXES, pairs)]
    ppermute x9, waiting for transfers between devices: 3.47 us -> 6.06 us  [shift(): return lax.ppermute(value, AXES, pairs)]
    ppermute x4, starting transfers between devices: 13.1 us -> 11.4 us  [swap_cores(): return lax.ppermute(value, AXES, pairs)]
    ppermute x14, starting transfers between devices: 17.8 us -> 16.3 us  [exchange(): return lax.ppermute(value, AXES, exchange_pairs(first, second))]
  transfers between devices with their start and end apart: 27 -> 27, of which waited for: 11 -> 13; matrix products, arithmetic and copies ran while one was open for 0% -> 0% of each run, Pallas kernels for 17% -> 16%
where the time goes in v4:
time: 89.4 us; the launch traced here: 89.5 us
  starting transfers between devices  39.1 us (44%)
  waiting for transfers between devices  29.8 us (33%)
  Pallas kernels  18.9 us (21%)
  between operations  0.91 us (1%)
    ppermute x14, waiting for transfers between devices, exchange(): return lax.ppermute(value, AXES, exchange_pairs(first, second))  22.8 us
    ppermute x14, starting transfers between devices, exchange(): return lax.ppermute(value, AXES, exchange_pairs(first, second))  16.3 us
    ppermute x9, starting transfers between devices, shift(): return lax.ppermute(value, AXES, pairs)  11.5 us
    ppermute x4, starting transfers between devices, swap_cores(): return lax.ppermute(value, AXES, pairs)  11.4 us
    pallas_call x4, Pallas kernels, products(): pl.pallas_call(products_kernel, out_shape=pltpu.VMEM((CALL_SLOTS, BLOCK,...  8.54 us
    ppermute x9, waiting for transfers between devices, shift(): return lax.ppermute(value, AXES, pairs)  6.06 us
    pallas_call x1, Pallas kernels, prepare(): pl.pallas_call(prepare_kernel, out_shape=(pltpu.VMEM(shape, jnp.bfloat16)...  5.14 us
    pallas_call x11, Pallas kernels, fold(): pl.pallas_call(functools.partial(fold_kernel, halves), out_shape=out, in_...  2.2 us
  transfers between devices with their start and end apart: 27, of which 13 were waited for; matrix products, arithmetic and copies ran while one was open for 0% of the time, Pallas kernels for 16%

profile of v4, /device:TPU:1, one launch (start us, length us, event | category | flops | bytes accessed | tf_op | source)
XLA Modules:
  0.0 89.5 jit_solution(2906872483480390989)
XLA Ops:
  0.6 1.2 %load.1 = (bf16[4,128,256]{2,1,0:T(8,128)(2,1)S(1)}, bf16[2,128,256]{2,1,0:T(8,128)(2,1)S(1)}, bf16[2,128,256]{2,1,0:T(8,128)(2,1)S(1)}) custom-call(bf16[4,128,256]{2,1,0:T(8,128)(2,1)} %bitcast.10, bf16[4,128,256]{2,1,0:T(8,128)(2,1)} %bitcast.11, bf16[4,128,256]{2,1,0:T(8,128)(2,1)} %bitcast.12), custom_call_target="tpu_custom_call" | custom-call | bytes 1024 | tf_op jit(solution)/shard_map/load/pallas_call | solution.py:203
  1.9 3.6 %collective-permute-start.1 = (bf16[4,128,256]{2,1,0:T(8,128)(2,1)S(1)}, bf16[4,128,256]{2,1,0:T(8,128)(2,1)S(1)}, u32[]{:S(2)}, u32[]{:S(2)}) collective-permute-start(bf16[4,128,256]{2,1,0:T(8,128)(2,1)S(1)} %get-tuple-element.29.refs_0_), channel_id=1, source_target_pairs={{0,1},{1,0},{2,3},{3,2},{4,7},{5,6},{6,5},{7,4},{8,9},{9,8},{10,11... | collective-permute-start | bytes 786440 | tf_op jit(solution)/shard_map/ppermute | solution.py:48
  5.5 2.5 %collective-permute-start = (bf16[2,128,256]{2,1,0:T(8,128)(2,1)S(1)}, bf16[2,128,256]{2,1,0:T(8,128)(2,1)S(1)}, u32[]{:S(2)}, u32[]{:S(2)}) collective-permute-start(bf16[2,128,256]{2,1,0:T(8,128)(2,1)S(1)} %get-tuple-element.28.refs_0_), channel_id=1, source_target_pairs={{0,96},{1,97},{2,98},{3,99},{4,28},{5,29},{6,30},{7,31},{8,104},{9... | collective-permute-start | bytes 393224 | tf_op jit(solution)/shard_map/ppermute | solution.py:48
  8.0 2.8 %collective-permute-done.refs_2_.refs_1_ = bf16[2,128,256]{2,1,0:T(8,128)(2,1)S(1)} collective-permute-done((bf16[2,128,256]{2,1,0:T(8,128)(2,1)S(1)}, bf16[2,128,256]{2,1,0:T(8,128)(2,1)S(1)}, u32[]{:S(2)}, u32[]{:S(2)}) %collective-permute-start) | collective-permute-done | bytes 131104 | tf_op jit(solution)/shard_map/ppermute | solution.py:48
  10.8 1.0 %collective-permute-done.2.refs_3_.refs_1_ = bf16[2,128,256]{2,1,0:T(8,128)(2,1)S(1)} collective-permute-done((bf16[2,128,256]{2,1,0:T(8,128)(2,1)S(1)}, bf16[2,128,256]{2,1,0:T(8,128)(2,1)S(1)}, u32[]{:S(2)}, u32[]{:S(2)}) %collective-permute-start.2) | collective-permute-done | bytes 131104 | tf_op jit(solution)/shard_map/ppermute | solution.py:48
  12.0 3.8 %collective-permute-start.4 = (bf16[4,128,256]{2,1,0:T(8,128)(2,1)S(1)}, bf16[4,128,256]{2,1,0:T(8,128)(2,1)S(1)}, u32[]{:S(2)}, u32[]{:S(2)}) collective-permute-start(bf16[4,128,256]{2,1,0:T(8,128)(2,1)S(1)} %join.6.refs_0_), channel_id=1, source_target_pairs={{0,24},{1,25},{2,26},{3,27},{4,100},{5,101},{6,102},{7,103},{8,16}... | collective-permute-start | bytes 786440 | tf_op jit(solution)/shard_map/ppermute | solution.py:48
  16.0 5.1 %prepare.1 = (bf16[512,128,128]{2,1,0:T(8,128)(2,1)S(1)}, s32[1,640]{1,0:T(1,128)S(1)}, s32[1,640]{1,0:T(1,128)S(1)}, s32[1,640]{1,0:T(1,128)S(1)}, s32[1,640]{1,0:T(1,128)S(1)}) custom-call(s32[4]{0:T(128)S(1)} %pad_add_fusion.where_ref, s32[16]{0:T(128)} %bitcast.13, s32[16,32]{1,0:T(8,128)} %cols_ref.1, bf16[512,128,128]{2,1,0:T(8,128)(2,1)} %bitcast.9, ...), custom_call_target="tpu_custom_call" | custom-call | bytes 1024 | tf_op jit(solution)/shard_map/prepare/pallas_call | solution.py:158
  21.5 2.1 %products_3.1.refs_0_ = bf16[32,128,256]{2,1,0:T(8,128)(2,1)S(1)} custom-call(s32[1,640]{1,0:T(1,128)S(1)} %get-tuple-element.35.words_ref, bf16[17,128,256]{2,1,0:T(8,128)(2,1)S(1)} %join.8.grad_ref, bf16[512,128,128]{2,1,0:T(8,128)(2,1)S(1)} %get-tuple-element.32.refs_2_.adj_ref), custom_call_target="tpu_custom_call" | custom-call | bytes 1024 | tf_op jit(solution)/shard_map/products_3/pallas_call | solution.py:356
  23.6 4.3 %collective-permute-start.6 = (bf16[32,128,256]{2,1,0:T(8,128)(2,1)S(1)}, bf16[32,128,256]{2,1,0:T(8,128)(2,1)S(1)}, u32[]{:S(2)}, u32[]{:S(2)}) collective-permute-start(bf16[32,128,256]{2,1,0:T(8,128)(2,1)S(1)} %products_3.1.refs_0_), channel_id=1, source_target_pairs={{0,4},{1,5},{2,6},{3,7},{4,0},{5,1},{6,2},{7,3},{8,12},{9,13},{10,... | collective-permute-start | bytes 6291464 | tf_op jit(solution)/shard_map/ppermute | solution.py:66
  28.0 2.1 %products_2.1.refs_0_ = bf16[32,128,256]{2,1,0:T(8,128)(2,1)S(1)} custom-call(s32[1,640]{1,0:T(1,128)S(1)} %get-tuple-element.34.words_ref, bf16[17,128,256]{2,1,0:T(8,128)(2,1)S(1)} %join.8.grad_ref, bf16[512,128,128]{2,1,0:T(8,128)(2,1)S(1)} %get-tuple-element.32.refs_2_.adj_ref, bf16[32,128,256]{2,1,0:T(8,128)(2,1)S(1)} %products_3.1.refs_0_), custom_call_target="tpu_custom_call" | custom-call | bytes 1024 | tf_op jit(solution)/shard_map/products_2/pallas_call | solution.py:356
  30.2 2.1 %products_1.1.kept_ref = bf16[32,128,256]{2,1,0:T(8,128)(2,1)S(1)} custom-call(s32[1,640]{1,0:T(1,128)S(1)} %get-tuple-element.33.words_ref, bf16[17,128,256]{2,1,0:T(8,128)(2,1)S(1)} %join.8.grad_ref, bf16[512,128,128]{2,1,0:T(8,128)(2,1)S(1)} %get-tuple-element.32.refs_2_.adj_ref, bf16[32,128,256]{2,1,0:T(8,128)(2,1)S(1)} %products_2.1.refs_0_), custom_call_target="tpu_custom_call" | custom-call | bytes 1024 | tf_op jit(solution)/shard_map/products_1/pallas_call | solution.py:356
  32.9 1.0 %collective-permute-start.11 = (bf16[16,128,256]{2,1,0:T(8,128)(2,1)S(1)}, bf16[16,128,256]{2,1,0:T(8,128)(2,1)S(1)}, u32[]{:S(2)}, u32[]{:S(2)}) collective-permute-start(bf16[16,128,256]{2,1,0:T(8,128)(2,1)S(1)} %get-tuple-element.37.refs_1_), channel_id=1, source_target_pairs={{0,24},{1,25},{2,26},{3,27},{4,100},{5,101},{6,102},{7,103},{8,16}... | collective-permute-start | bytes 3145736 | tf_op jit(solution)/shard_map/ppermute | solution.py:48
  33.9 2.1 %products_0.1.kept_ref = bf16[32,128,256]{2,1,0:T(8,128)(2,1)S(1)} custom-call(s32[1,640]{1,0:T(1,128)S(1)} %get-tuple-element.31.words_ref, bf16[17,128,256]{2,1,0:T(8,128)(2,1)S(1)} %join.8.grad_ref, bf16[512,128,128]{2,1,0:T(8,128)(2,1)S(1)} %get-tuple-element.32.refs_2_.adj_ref, bf16[16,128,256]{2,1,0:T(8,128)(2,1)S(1)} %get-tuple-element.36.refs_0_, ...), custom_call_target="tpu_custom_call" | custom-call | bytes 1024 | tf_op jit(solution)/shard_map/products_0/pallas_call | solution.py:356
  36.6 10.2 %collective-permute-done.8.got_ref = bf16[16,128,256]{2,1,0:T(8,128)(2,1)S(1)} collective-permute-done((bf16[16,128,256]{2,1,0:T(8,128)(2,1)S(1)}, bf16[16,128,256]{2,1,0:T(8,128)(2,1)S(1)}, u32[]{:S(2)}, u32[]{:S(2)}) %collective-permute-start.8) | collective-permute-done | bytes 1048608 | tf_op jit(solution)/shard_map/ppermute | solution.py:48
  47.1 2.7 %collective-permute-start.9 = (bf16[8,128,256]{2,1,0:T(8,128)(2,1)S(1)}, bf16[8,128,256]{2,1,0:T(8,128)(2,1)S(1)}, u32[]{:S(2)}, u32[]{:S(2)}) collective-permute-start(bf16[8,128,256]{2,1,0:T(8,128)(2,1)S(1)} %get-tuple-element.40), channel_id=1, source_target_pairs={{0,32},{1,33},{2,34},{3,35},{4,12},{5,13},{6,14},{7,15},{8,40},{9,... | collective-permute-start | bytes 1572872 | tf_op jit(solution)/shard_map/ppermute | solution.py:48
  50.1 0.9 %collective-permute-start.12 = (bf16[8,128,256]{2,1,0:T(8,128)(2,1)S(1)}, bf16[8,128,256]{2,1,0:T(8,128)(2,1)S(1)}, u32[]{:S(2)}, u32[]{:S(2)}) collective-permute-start(bf16[8,128,256]{2,1,0:T(8,128)(2,1)S(1)} %get-tuple-element.45), channel_id=1, source_target_pairs={{0,96},{1,97},{2,98},{3,99},{4,28},{5,29},{6,30},{7,31},{8,104},{9... | collective-permute-start | bytes 1572872 | tf_op jit(solution)/shard_map/ppermute | solution.py:48
  51.0 5.7 %collective-permute-done.9.got_ref = bf16[8,128,256]{2,1,0:T(8,128)(2,1)S(1)} collective-permute-done((bf16[8,128,256]{2,1,0:T(8,128)(2,1)S(1)}, bf16[8,128,256]{2,1,0:T(8,128)(2,1)S(1)}, u32[]{:S(2)}, u32[]{:S(2)}) %collective-permute-start.9) | collective-permute-done | bytes 524320 | tf_op jit(solution)/shard_map/ppermute | solution.py:48
  56.8 2.9 %collective-permute-done.12.got_ref = bf16[8,128,256]{2,1,0:T(8,128)(2,1)S(1)} collective-permute-done((bf16[8,128,256]{2,1,0:T(8,128)(2,1)S(1)}, bf16[8,128,256]{2,1,0:T(8,128)(2,1)S(1)}, u32[]{:S(2)}, u32[]{:S(2)}) %collective-permute-start.12) | collective-permute-done | bytes 524320 | tf_op jit(solution)/shard_map/ppermute | solution.py:48
  60.3 3.5 %collective-permute-start.13 = (bf16[128,256]{1,0:T(8,128)(2,1)S(1)}, bf16[128,256]{1,0:T(8,128)(2,1)S(1)}, u32[]{:S(2)}, u32[]{:S(2)}) collective-permute-start(bf16[128,256]{1,0:T(8,128)(2,1)S(1)} %get-tuple-element.49), channel_id=1, source_target_pairs={{0,4},{1,5},{2,6},{3,7},{4,0},{5,1},{6,2},{7,3},{8,12},{9,13},{10,... | collective-permute-start | bytes 196616 | tf_op jit(solution)/shard_map/ppermute | solution.py:66
  63.7 0.9 %collective-permute-done.13.got_ref = bf16[128,256]{1,0:T(8,128)(2,1)S(1)} collective-permute-done((bf16[128,256]{1,0:T(8,128)(2,1)S(1)}, bf16[128,256]{1,0:T(8,128)(2,1)S(1)}, u32[]{:S(2)}, u32[]{:S(2)}) %collective-permute-start.13) | collective-permute-done | bytes 65568 | tf_op jit(solution)/shard_map/ppermute | solution.py:66
  65.0 2.9 %collective-permute-start.14 = (bf16[128,256]{1,0:T(8,128)(2,1)S(1)}, bf16[128,256]{1,0:T(8,128)(2,1)S(1)}, u32[]{:S(2)}, u32[]{:S(2)}) collective-permute-start(bf16[128,256]{1,0:T(8,128)(2,1)S(1)} %fold.17.own_ref.refs_1_), channel_id=1, source_target_pairs={{0,16},{1,17},{2,18},{3,19},{4,68},{5,69},{6,70},{7,71},{8,24},{9,... | collective-permute-start | bytes 196616 | tf_op jit(solution)/shard_map/ppermute | solution.py:61
  68.0 2.7 %collective-permute-start.16 = (bf16[128,256]{1,0:T(8,128)(2,1)S(1)}, bf16[128,256]{1,0:T(8,128)(2,1)S(1)}, u32[]{:S(2)}, u32[]{:S(2)}) collective-permute-start(bf16[128,256]{1,0:T(8,128)(2,1)S(1)} %fold.17.own_ref.refs_1_), channel_id=1, source_target_pairs={{0,24},{1,25},{2,26},{3,27},{4,100},{5,101},{6,102},{7,103},{8,0},... | collective-permute-start | bytes 196616 | tf_op jit(solution)/shard_map/ppermute | solution.py:61
  70.6 1.9 %collective-permute-done.14.opposite_ref = bf16[128,256]{1,0:T(8,128)(2,1)S(1)} collective-permute-done((bf16[128,256]{1,0:T(8,128)(2,1)S(1)}, bf16[128,256]{1,0:T(8,128)(2,1)S(1)}, u32[]{:S(2)}, u32[]{:S(2)}) %collective-permute-start.14) | collective-permute-done | bytes 65568 | tf_op jit(solution)/shard_map/ppermute | solution.py:61
  72.5 0.8 collective-permute-done.15.left_ref
  73.4 1.4 %collective-permute-start.19 = (bf16[128,256]{1,0:T(8,128)(2,1)S(1)}, bf16[128,256]{1,0:T(8,128)(2,1)S(1)}, u32[]{:S(2)}, u32[]{:S(2)}) collective-permute-start(bf16[128,256]{1,0:T(8,128)(2,1)S(1)} %ring_sum.3.refs_0_.own_ref), channel_id=1, source_target_pairs={{0,32},{1,33},{2,34},{3,35},{4,12},{5,13},{6,14},{7,15},{8,40},{9,... | collective-permute-start | bytes 196616 | tf_op jit(solution)/shard_map/ppermute | solution.py:61
  74.8 1.5 %collective-permute-start.20 = (bf16[128,256]{1,0:T(8,128)(2,1)S(1)}, bf16[128,256]{1,0:T(8,128)(2,1)S(1)}, u32[]{:S(2)}, u32[]{:S(2)}) collective-permute-start(bf16[128,256]{1,0:T(8,128)(2,1)S(1)} %ring_sum.3.refs_0_.own_ref), channel_id=1, source_target_pairs={{0,96},{1,97},{2,98},{3,99},{4,28},{5,29},{6,30},{7,31},{8,104},{9... | collective-permute-start | bytes 196616 | tf_op jit(solution)/shard_map/ppermute | solution.py:61
  76.9 0.9 %collective-permute-start.22 = (bf16[2,128,256]{2,1,0:T(8,128)(2,1)S(1)}, bf16[2,128,256]{2,1,0:T(8,128)(2,1)S(1)}, u32[]{:S(2)}, u32[]{:S(2)}) collective-permute-start(bf16[2,128,256]{2,1,0:T(8,128)(2,1)S(1)} %get-tuple-element.53), channel_id=1, source_target_pairs={{0,32},{1,33},{2,34},{3,35},{4,12},{5,13},{6,14},{7,15},{8,40},{9,... | collective-permute-start | bytes 393224 | tf_op jit(solution)/shard_map/ppermute | solution.py:48
  79.3 2.3 %collective-permute-start.25 = (bf16[128,256]{1,0:T(8,128)(2,1)S(1)}, bf16[128,256]{1,0:T(8,128)(2,1)S(1)}, u32[]{:S(2)}, u32[]{:S(2)}) collective-permute-start(bf16[128,256]{1,0:T(8,128)(2,1)S(1)} %ring_sum.4.refs_0_.own_ref), channel_id=1, source_target_pairs={{0,3},{1,0},{2,1},{3,2},{4,7},{5,4},{6,5},{7,6},{8,11},{9,8},{10,9... | collective-permute-start | bytes 196616 | tf_op jit(solution)/shard_map/ppermute | solution.py:61
  81.7 1.9 %collective-permute-done.23.opposite_ref = bf16[128,256]{1,0:T(8,128)(2,1)S(1)} collective-permute-done((bf16[128,256]{1,0:T(8,128)(2,1)S(1)}, bf16[128,256]{1,0:T(8,128)(2,1)S(1)}, u32[]{:S(2)}, u32[]{:S(2)}) %collective-permute-start.23) | collective-permute-done | bytes 65568 | tf_op jit(solution)/shard_map/ppermute | solution.py:61
  84.2 3.5 %collective-permute-start.26 = (bf16[128,256]{1,0:T(8,128)(2,1)S(1)}, bf16[128,256]{1,0:T(8,128)(2,1)S(1)}, u32[]{:S(2)}, u32[]{:S(2)}) collective-permute-start(bf16[128,256]{1,0:T(8,128)(2,1)S(1)} %ring_sum.5), channel_id=1, source_target_pairs={{0,4},{1,5},{2,6},{3,7},{4,0},{5,1},{6,2},{7,3},{8,12},{9,13},{10,... | collective-permute-start | bytes 196616 | tf_op jit(solution)/shard_map/ppermute | solution.py:66
  87.7 1.0 %features_gradient.1 = bf16[512,256]{1,0:T(8,128)(2,1)} custom-call(bf16[2,128,256]{2,1,0:T(8,128)(2,1)S(1)} %fold.20.first_ref.refs_0_, bf16[2,128,256]{2,1,0:T(8,128)(2,1)S(1)} %fold.21.second_ref.refs_1_, bf16[256,256]{1,0:T(8,128)(2,1)S(1)} %copy-done), custom_call_target="tpu_custom_call" | custom-call | bytes 1024 | tf_op jit(solution)/shard_map/features_gradient/pallas_call | solution.py:292
  88.7 0.7 maximum_convert_fusion
  (54 shorter events, 6.3 us)
Async XLA Ops:
  1.9 9.9 %collective-permute-start.1 = (bf16[4,128,256]{2,1,0:T(8,128)(2,1)S(1)}, bf16[4,128,256]{2,1,0:T(8,128)(2,1)S(1)}, u32[]{:S(2)}, u32[]{:S(2)}) collective-permute-start(bf16[4,128,256]{2,1,0:T(8,128)(2,1)S(1)} %get-tuple-element.29.refs_0_), channel_id=1, source_target_pairs={{0,1},{1,0},{2,3},{3,2},{4,7},{5,6},{6,5},{7,4},{8,9},{9,8},{10,11... | collective-permute-start | bytes 786440 | tf_op jit(solution)/shard_map/ppermute | solution.py:48
  5.5 5.3 %collective-permute-start = (bf16[2,128,256]{2,1,0:T(8,128)(2,1)S(1)}, bf16[2,128,256]{2,1,0:T(8,128)(2,1)S(1)}, u32[]{:S(2)}, u32[]{:S(2)}) collective-permute-start(bf16[2,128,256]{2,1,0:T(8,128)(2,1)S(1)} %get-tuple-element.28.refs_0_), channel_id=1, source_target_pairs={{0,96},{1,97},{2,98},{3,99},{4,28},{5,29},{6,30},{7,31},{8,104},{9... | collective-permute-start | bytes 393224 | tf_op jit(solution)/shard_map/ppermute | solution.py:48
  8.0 3.8 %collective-permute-start.2 = (bf16[2,128,256]{2,1,0:T(8,128)(2,1)S(1)}, bf16[2,128,256]{2,1,0:T(8,128)(2,1)S(1)}, u32[]{:S(2)}, u32[]{:S(2)}) collective-permute-start(bf16[2,128,256]{2,1,0:T(8,128)(2,1)S(1)} %get-tuple-element.30.refs_0_), channel_id=1, source_target_pairs={{0,32},{1,33},{2,34},{3,35},{4,12},{5,13},{6,14},{7,15},{8,40},{9,... | collective-permute-start | bytes 393224 | tf_op jit(solution)/shard_map/ppermute | solution.py:48
  11.8 9.6 %collective-permute-start.3 = (bf16[8,128,256]{2,1,0:T(8,128)(2,1)S(1)}, bf16[8,128,256]{2,1,0:T(8,128)(2,1)S(1)}, u32[]{:S(2)}, u32[]{:S(2)}) collective-permute-start(bf16[8,128,256]{2,1,0:T(8,128)(2,1)S(1)} %join.5.refs_2_.refs_0_), channel_id=1, source_target_pairs={{0,3},{1,2},{2,1},{3,0},{4,5},{5,4},{6,7},{7,6},{8,11},{9,10},{10,... | collective-permute-start | bytes 1572872 | tf_op jit(solution)/shard_map/ppermute | solution.py:48
  12.0 9.2 %collective-permute-start.4 = (bf16[4,128,256]{2,1,0:T(8,128)(2,1)S(1)}, bf16[4,128,256]{2,1,0:T(8,128)(2,1)S(1)}, u32[]{:S(2)}, u32[]{:S(2)}) collective-permute-start(bf16[4,128,256]{2,1,0:T(8,128)(2,1)S(1)} %join.6.refs_0_), channel_id=1, source_target_pairs={{0,24},{1,25},{2,26},{3,27},{4,100},{5,101},{6,102},{7,103},{8,16}... | collective-permute-start | bytes 786440 | tf_op jit(solution)/shard_map/ppermute | solution.py:48
  15.8 5.6 %collective-permute-start.5 = (bf16[4,128,256]{2,1,0:T(8,128)(2,1)S(1)}, bf16[4,128,256]{2,1,0:T(8,128)(2,1)S(1)}, u32[]{:S(2)}, u32[]{:S(2)}) collective-permute-start(bf16[4,128,256]{2,1,0:T(8,128)(2,1)S(1)} %join.7.refs_1_.refs_4_), channel_id=1, source_target_pairs={{0,8},{1,9},{2,10},{3,11},{4,36},{5,37},{6,38},{7,39},{8,0},{9,1},... | collective-permute-start | bytes 786440 | tf_op jit(solution)/shard_map/ppermute | solution.py:48
  23.6 8.7 %collective-permute-start.6 = (bf16[32,128,256]{2,1,0:T(8,128)(2,1)S(1)}, bf16[32,128,256]{2,1,0:T(8,128)(2,1)S(1)}, u32[]{:S(2)}, u32[]{:S(2)}) collective-permute-start(bf16[32,128,256]{2,1,0:T(8,128)(2,1)S(1)} %products_3.1.refs_0_), channel_id=1, source_target_pairs={{0,4},{1,5},{2,6},{3,7},{4,0},{5,1},{6,2},{7,3},{8,12},{9,13},{10,... | collective-permute-start | bytes 6291464 | tf_op jit(solution)/shard_map/ppermute | solution.py:66
  30.1 6.0 %collective-permute-start.7 = (bf16[32,128,256]{2,1,0:T(8,128)(2,1)S(1)}, bf16[32,128,256]{2,1,0:T(8,128)(2,1)S(1)}, u32[]{:S(2)}, u32[]{:S(2)}) collective-permute-start(bf16[32,128,256]{2,1,0:T(8,128)(2,1)S(1)} %products_2.1.refs_0_), channel_id=1, source_target_pairs={{0,4},{1,5},{2,6},{3,7},{4,0},{5,1},{6,2},{7,3},{8,12},{9,13},{10,... | collective-permute-start | bytes 6291464 | tf_op jit(solution)/shard_map/ppermute | solution.py:66
  32.8 14.0 %collective-permute-start.8 = (bf16[16,128,256]{2,1,0:T(8,128)(2,1)S(1)}, bf16[16,128,256]{2,1,0:T(8,128)(2,1)S(1)}, u32[]{:S(2)}, u32[]{:S(2)}) collective-permute-start(bf16[16,128,256]{2,1,0:T(8,128)(2,1)S(1)} %get-tuple-element.36.refs_0_), channel_id=1, source_target_pairs={{0,8},{1,9},{2,10},{3,11},{4,36},{5,37},{6,38},{7,39},{8,0},{9,1},... | collective-permute-start | bytes 3145736 | tf_op jit(solution)/shard_map/ppermute | solution.py:48
  32.9 16.9 %collective-permute-start.11 = (bf16[16,128,256]{2,1,0:T(8,128)(2,1)S(1)}, bf16[16,128,256]{2,1,0:T(8,128)(2,1)S(1)}, u32[]{:S(2)}, u32[]{:S(2)}) collective-permute-start(bf16[16,128,256]{2,1,0:T(8,128)(2,1)S(1)} %get-tuple-element.37.refs_1_), channel_id=1, source_target_pairs={{0,24},{1,25},{2,26},{3,27},{4,100},{5,101},{6,102},{7,103},{8,16}... | collective-permute-start | bytes 3145736 | tf_op jit(solution)/shard_map/ppermute | solution.py:48
  47.1 9.5 %collective-permute-start.9 = (bf16[8,128,256]{2,1,0:T(8,128)(2,1)S(1)}, bf16[8,128,256]{2,1,0:T(8,128)(2,1)S(1)}, u32[]{:S(2)}, u32[]{:S(2)}) collective-permute-start(bf16[8,128,256]{2,1,0:T(8,128)(2,1)S(1)} %get-tuple-element.40), channel_id=1, source_target_pairs={{0,32},{1,33},{2,34},{3,35},{4,12},{5,13},{6,14},{7,15},{8,40},{9,... | collective-permute-start | bytes 1572872 | tf_op jit(solution)/shard_map/ppermute | solution.py:48
  50.1 9.6 %collective-permute-start.12 = (bf16[8,128,256]{2,1,0:T(8,128)(2,1)S(1)}, bf16[8,128,256]{2,1,0:T(8,128)(2,1)S(1)}, u32[]{:S(2)}, u32[]{:S(2)}) collective-permute-start(bf16[8,128,256]{2,1,0:T(8,128)(2,1)S(1)} %get-tuple-element.45), channel_id=1, source_target_pairs={{0,96},{1,97},{2,98},{3,99},{4,28},{5,29},{6,30},{7,31},{8,104},{9... | collective-permute-start | bytes 1572872 | tf_op jit(solution)/shard_map/ppermute | solution.py:48
  60.3 4.4 %collective-permute-start.13 = (bf16[128,256]{1,0:T(8,128)(2,1)S(1)}, bf16[128,256]{1,0:T(8,128)(2,1)S(1)}, u32[]{:S(2)}, u32[]{:S(2)}) collective-permute-start(bf16[128,256]{1,0:T(8,128)(2,1)S(1)} %get-tuple-element.49), channel_id=1, source_target_pairs={{0,4},{1,5},{2,6},{3,7},{4,0},{5,1},{6,2},{7,3},{8,12},{9,13},{10,... | collective-permute-start | bytes 196616 | tf_op jit(solution)/shard_map/ppermute | solution.py:66
  63.7 12.6 %collective-permute-start.10 = (bf16[4,128,256]{2,1,0:T(8,128)(2,1)S(1)}, bf16[4,128,256]{2,1,0:T(8,128)(2,1)S(1)}, u32[]{:S(2)}, u32[]{:S(2)}) collective-permute-start(bf16[4,128,256]{2,1,0:T(8,128)(2,1)S(1)} %get-tuple-element.42.refs_3_), channel_id=1, source_target_pairs={{0,24},{1,25},{2,26},{3,27},{4,100},{5,101},{6,102},{7,103},{8,16}... | collective-permute-start | bytes 786440 | tf_op jit(solution)/shard_map/ppermute | solution.py:48
  64.9 22.8 %copy-start = (bf16[256,256]{1,0:T(8,128)(2,1)S(1)}, bf16[256,256]{1,0:T(8,128)(2,1)}, u32[]{:S(2)}) copy-start(bf16[256,256]{1,0:T(8,128)(2,1)} %weight_ref.1) | copy-start | bytes 393220
  64.9 11.9 %collective-permute-start.21 = (bf16[4,128,256]{2,1,0:T(8,128)(2,1)S(1)}, bf16[4,128,256]{2,1,0:T(8,128)(2,1)S(1)}, u32[]{:S(2)}, u32[]{:S(2)}) collective-permute-start(bf16[4,128,256]{2,1,0:T(8,128)(2,1)S(1)} %join.9), channel_id=1, source_target_pairs={{0,8},{1,9},{2,10},{3,11},{4,36},{5,37},{6,38},{7,39},{8,0},{9,1},... | collective-permute-start | bytes 786440 | tf_op jit(solution)/shard_map/ppermute | solution.py:48
  65.0 7.5 %collective-permute-start.14 = (bf16[128,256]{1,0:T(8,128)(2,1)S(1)}, bf16[128,256]{1,0:T(8,128)(2,1)S(1)}, u32[]{:S(2)}, u32[]{:S(2)}) collective-permute-start(bf16[128,256]{1,0:T(8,128)(2,1)S(1)} %fold.17.own_ref.refs_1_), channel_id=1, source_target_pairs={{0,16},{1,17},{2,18},{3,19},{4,68},{5,69},{6,70},{7,71},{8,24},{9,... | collective-permute-start | bytes 196616 | tf_op jit(solution)/shard_map/ppermute | solution.py:61
  68.0 5.3 %collective-permute-start.15 = (bf16[128,256]{1,0:T(8,128)(2,1)S(1)}, bf16[128,256]{1,0:T(8,128)(2,1)S(1)}, u32[]{:S(2)}, u32[]{:S(2)}) collective-permute-start(bf16[128,256]{1,0:T(8,128)(2,1)S(1)} %fold.17.own_ref.refs_1_), channel_id=1, source_target_pairs={{0,8},{1,9},{2,10},{3,11},{4,36},{5,37},{6,38},{7,39},{8,16},{9,17... | collective-permute-start | bytes 196616 | tf_op jit(solution)/shard_map/ppermute | solution.py:61
  68.0 5.3 %collective-permute-start.16 = (bf16[128,256]{1,0:T(8,128)(2,1)S(1)}, bf16[128,256]{1,0:T(8,128)(2,1)S(1)}, u32[]{:S(2)}, u32[]{:S(2)}) collective-permute-start(bf16[128,256]{1,0:T(8,128)(2,1)S(1)} %fold.17.own_ref.refs_1_), channel_id=1, source_target_pairs={{0,24},{1,25},{2,26},{3,27},{4,100},{5,101},{6,102},{7,103},{8,0},... | collective-permute-start | bytes 196616 | tf_op jit(solution)/shard_map/ppermute | solution.py:61
  73.3 4.8 %collective-permute-start.18 = (bf16[128,256]{1,0:T(8,128)(2,1)S(1)}, bf16[128,256]{1,0:T(8,128)(2,1)S(1)}, u32[]{:S(2)}, u32[]{:S(2)}) collective-permute-start(bf16[128,256]{1,0:T(8,128)(2,1)S(1)} %ring_sum.3.refs_0_.own_ref), channel_id=1, source_target_pairs={{0,64},{1,65},{2,66},{3,67},{4,20},{5,21},{6,22},{7,23},{8,72},{9,... | collective-permute-start | bytes 196616 | tf_op jit(solution)/shard_map/ppermute | solution.py:61
  73.4 5.3 %collective-permute-start.19 = (bf16[128,256]{1,0:T(8,128)(2,1)S(1)}, bf16[128,256]{1,0:T(8,128)(2,1)S(1)}, u32[]{:S(2)}, u32[]{:S(2)}) collective-permute-start(bf16[128,256]{1,0:T(8,128)(2,1)S(1)} %ring_sum.3.refs_0_.own_ref), channel_id=1, source_target_pairs={{0,32},{1,33},{2,34},{3,35},{4,12},{5,13},{6,14},{7,15},{8,40},{9,... | collective-permute-start | bytes 196616 | tf_op jit(solution)/shard_map/ppermute | solution.py:61
  74.8 3.9 %collective-permute-start.20 = (bf16[128,256]{1,0:T(8,128)(2,1)S(1)}, bf16[128,256]{1,0:T(8,128)(2,1)S(1)}, u32[]{:S(2)}, u32[]{:S(2)}) collective-permute-start(bf16[128,256]{1,0:T(8,128)(2,1)S(1)} %ring_sum.3.refs_0_.own_ref), channel_id=1, source_target_pairs={{0,96},{1,97},{2,98},{3,99},{4,28},{5,29},{6,30},{7,31},{8,104},{9... | collective-permute-start | bytes 196616 | tf_op jit(solution)/shard_map/ppermute | solution.py:61
  76.4 5.2 %collective-permute-start.17 = (bf16[2,128,256]{2,1,0:T(8,128)(2,1)S(1)}, bf16[2,128,256]{2,1,0:T(8,128)(2,1)S(1)}, u32[]{:S(2)}, u32[]{:S(2)}) collective-permute-start(bf16[2,128,256]{2,1,0:T(8,128)(2,1)S(1)} %get-tuple-element.51), channel_id=1, source_target_pairs={{0,96},{1,97},{2,98},{3,99},{4,28},{5,29},{6,30},{7,31},{8,104},{9... | collective-permute-start | bytes 393224 | tf_op jit(solution)/shard_map/ppermute | solution.py:48
  76.9 4.7 %collective-permute-start.22 = (bf16[2,128,256]{2,1,0:T(8,128)(2,1)S(1)}, bf16[2,128,256]{2,1,0:T(8,128)(2,1)S(1)}, u32[]{:S(2)}, u32[]{:S(2)}) collective-permute-start(bf16[2,128,256]{2,1,0:T(8,128)(2,1)S(1)} %get-tuple-element.53), channel_id=1, source_target_pairs={{0,32},{1,33},{2,34},{3,35},{4,12},{5,13},{6,14},{7,15},{8,40},{9,... | collective-permute-start | bytes 393224 | tf_op jit(solution)/shard_map/ppermute | solution.py:48
  78.7 4.8 %collective-permute-start.23 = (bf16[128,256]{1,0:T(8,128)(2,1)S(1)}, bf16[128,256]{1,0:T(8,128)(2,1)S(1)}, u32[]{:S(2)}, u32[]{:S(2)}) collective-permute-start(bf16[128,256]{1,0:T(8,128)(2,1)S(1)} %ring_sum.4.refs_0_.own_ref), channel_id=1, source_target_pairs={{0,2},{1,3},{2,0},{3,1},{4,6},{5,7},{6,4},{7,5},{8,10},{9,11},{10,... | collective-permute-start | bytes 196616 | tf_op jit(solution)/shard_map/ppermute | solution.py:61
  78.8 5.4 %collective-permute-start.24 = (bf16[128,256]{1,0:T(8,128)(2,1)S(1)}, bf16[128,256]{1,0:T(8,128)(2,1)S(1)}, u32[]{:S(2)}, u32[]{:S(2)}) collective-permute-start(bf16[128,256]{1,0:T(8,128)(2,1)S(1)} %ring_sum.4.refs_0_.own_ref), channel_id=1, source_target_pairs={{0,1},{1,2},{2,3},{3,0},{4,5},{5,6},{6,7},{7,4},{8,9},{9,10},{10,1... | collective-permute-start | bytes 196616 | tf_op jit(solution)/shard_map/ppermute | solution.py:61
  79.3 4.9 %collective-permute-start.25 = (bf16[128,256]{1,0:T(8,128)(2,1)S(1)}, bf16[128,256]{1,0:T(8,128)(2,1)S(1)}, u32[]{:S(2)}, u32[]{:S(2)}) collective-permute-start(bf16[128,256]{1,0:T(8,128)(2,1)S(1)} %ring_sum.4.refs_0_.own_ref), channel_id=1, source_target_pairs={{0,3},{1,0},{2,1},{3,2},{4,7},{5,4},{6,5},{7,6},{8,11},{9,8},{10,9... | collective-permute-start | bytes 196616 | tf_op jit(solution)/shard_map/ppermute | solution.py:61
  84.2 4.5 %collective-permute-start.26 = (bf16[128,256]{1,0:T(8,128)(2,1)S(1)}, bf16[128,256]{1,0:T(8,128)(2,1)S(1)}, u32[]{:S(2)}, u32[]{:S(2)}) collective-permute-start(bf16[128,256]{1,0:T(8,128)(2,1)S(1)} %ring_sum.5), channel_id=1, source_target_pairs={{0,4},{1,5},{2,6},{3,7},{4,0},{5,1},{6,2},{7,3},{8,12},{9,13},{10,... | collective-permute-start | bytes 196616 | tf_op jit(solution)/shard_map/ppermute | solution.py:66

commit v5 on v3

--- a/solution.py
+++ b/solution.py
@@ -259,6 +259,43 @@
     )(in_vmem(kept), in_vmem(got), *gates)
 
 
+def fold_through_kernel(kept_ref, got_ref, value_ref, out_ref, through_ref):
+    out_ref[...] = (kept_ref[...].astype(jnp.float32) + got_ref[...].astype(jnp.float32)).astype(jnp.bfloat16)
+    through_ref[...] = value_ref[...]
+
+
+def fold_through(kept, got, value):
+    return pl.pallas_call(
+        fold_through_kernel,
+        out_shape=tuple(pltpu.VMEM(v.shape, jnp.bfloat16) for v in (kept, value)),
+        in_specs=[IN_VMEM] * 3,
+        out_specs=(IN_VMEM,) * 2,
+        compiler_params=pltpu.CompilerParams(vmem_limit_bytes=4 << 20),
+        cost_estimate=TINY,
+        name="fold_through",
+    )(*(in_vmem(v) for v in (kept, got, value)))
+
+
+def join_two_kernel(*refs):
+    for p, out_ref in enumerate(refs[-2:]):
+        size = refs[p].shape[0]
+        out_ref[:size] = refs[p][...]
+        out_ref[size:] = refs[2 + p][...]
+
+
+def join_two(first, second, gate):
+    out = tuple(pltpu.VMEM((2 * v.shape[0], *v.shape[1:]), v.dtype) for v in first)
+    return pl.pallas_call(
+        join_two_kernel,
+        out_shape=out,
+        in_specs=[IN_VMEM] * 4 + [ANYWHERE],
+        out_specs=(IN_VMEM,) * 2,
+        compiler_params=pltpu.CompilerParams(vmem_limit_bytes=4 << 20),
+        cost_estimate=TINY,
+        name="join_two",
+    )(*(in_vmem(v) for v in (*first, *second)), gate)
+
+
 def ring_kernel(own_ref, opposite_ref, left_ref, right_ref, *refs):
     own, opposite, left, right = (
         r[...].astype(jnp.float32) for r in (own_ref, opposite_ref, left_ref, right_ref)
@@ -379,7 +416,7 @@
     near = [exchange(mine[p], ORDER[p][0][3], ORDER[p][1][3]) for p in (0, 1)]
     half = join([own, got], near)
     got = exchange(half, "y1", "y0")
-    feats = [join([mine[p], near[p]], [half]) for p in (0, 1)]
+    feats = join_two(mine, near, half)
     far = [exchange(feats[p], ORDER[p][0][2], ORDER[p][1][2]) for p in (0, 1)]
     where = jnp.stack([z, x, c, y]).astype(jnp.int32)
     adj, *words = prepare(adj_values, adj_cols, adj_counts, where, feats)
@@ -407,7 +444,7 @@
     halve(1)
     held = [(v[p], w[p]) for p in (0, 1) for v, w in ((feats, lower), (far, upper))]
     term, other = weight_terms(core, held)
-    (term,) = fold(term, swap_cores(other), 1)
+    term, upper[1] = fold_through(term, swap_cores(other), upper[1])
     for k, rings in enumerate((("x", "z"), ("z", "x"), ("y", "y"))):
         got = [shift(term, *rings, hops) for hops in (2, 1, 3)]
         term = ring_sum(term, got, lower)

time: 90.2 us -> 89.4 us (level)
  starting transfers between devices: 45 us -> 40.6 us
  waiting for transfers between devices: 24.4 us -> 28.3 us
    ppermute x9, starting transfers between devices: 14.1 us -> 11.2 us  [shift(): return lax.ppermute(value, AXES, pairs)]
    ppermute x14, waiting for transfers between devices: 20 us -> 22.9 us  [exchange(): return lax.ppermute(value, AXES, exchange_pairs(first, second))]
    ppermute x9, waiting for transfers between devices: 3.47 us -> 5.47 us  [shift(): return lax.ppermute(value, AXES, pairs)]
    ppermute x4, starting transfers between devices: 13.1 us -> 11.4 us  [swap_cores(): return lax.ppermute(value, AXES, pairs)]
    pallas_call x11 -> x10, Pallas kernels: 2.2 us -> 1.97 us  [fold(): pl.pallas_call(functools.partial(fold_kernel, halves), out_shape=out, in_...]
  transfers between devices with their start and end apart: 27 -> 27, of which waited for: 11 -> 13; matrix products, arithmetic and copies ran while one was open for 0% -> 0% of each run, Pallas kernels for 17% -> 16%
where the time goes in v5:
time: 89.4 us; the launch traced here: 89.5 us
  starting transfers between devices  40.6 us (45%)
  waiting for transfers between devices  28.3 us (32%)
  Pallas kernels  18.9 us (21%)
    ppermute x14, waiting for transfers between devices, exchange(): return lax.ppermute(value, AXES, exchange_pairs(first, second))  22.9 us
    ppermute x14, starting transfers between devices, exchange(): return lax.ppermute(value, AXES, exchange_pairs(first, second))  18 us
    ppermute x4, starting transfers between devices, swap_cores(): return lax.ppermute(value, AXES, pairs)  11.4 us
    ppermute x9, starting transfers between devices, shift(): return lax.ppermute(value, AXES, pairs)  11.2 us
    pallas_call x4, Pallas kernels, products(): pl.pallas_call(products_kernel, out_shape=pltpu.VMEM((CALL_SLOTS, BLOCK,...  8.54 us
    ppermute x9, waiting for transfers between devices, shift(): return lax.ppermute(value, AXES, pairs)  5.47 us
    pallas_call x1, Pallas kernels, prepare(): pl.pallas_call(prepare_kernel, out_shape=(pltpu.VMEM(shape, jnp.bfloat16)...  5.35 us
    pallas_call x10, Pallas kernels, fold(): pl.pallas_call(functools.partial(fold_kernel, halves), out_shape=out, in_...  1.97 us
  transfers between devices with their start and end apart: 27, of which 13 were waited for; matrix products, arithmetic and copies ran while one was open for 0% of the time, Pallas kernels for 16%

profile of v5, /device:TPU:1, one launch (start us, length us, event | category | flops | bytes accessed | tf_op | source)
XLA Modules:
  0.0 89.5 jit_solution(1449179040136661049)
XLA Ops:
  0.6 1.2 %load.1 = (bf16[4,128,256]{2,1,0:T(8,128)(2,1)S(1)}, bf16[2,128,256]{2,1,0:T(8,128)(2,1)S(1)}, bf16[2,128,256]{2,1,0:T(8,128)(2,1)S(1)}) custom-call(bf16[4,128,256]{2,1,0:T(8,128)(2,1)} %bitcast.10, bf16[4,128,256]{2,1,0:T(8,128)(2,1)} %bitcast.11, bf16[4,128,256]{2,1,0:T(8,128)(2,1)} %bitcast.12), custom_call_target="tpu_custom_call" | custom-call | bytes 1024 | tf_op jit(solution)/shard_map/load/pallas_call | solution.py:203
  1.9 3.6 %collective-permute-start.2 = (bf16[4,128,256]{2,1,0:T(8,128)(2,1)S(1)}, bf16[4,128,256]{2,1,0:T(8,128)(2,1)S(1)}, u32[]{:S(2)}, u32[]{:S(2)}) collective-permute-start(bf16[4,128,256]{2,1,0:T(8,128)(2,1)S(1)} %get-tuple-element.34.refs_0_), channel_id=1, source_target_pairs={{0,1},{1,0},{2,3},{3,2},{4,7},{5,6},{6,5},{7,4},{8,9},{9,8},{10,11... | collective-permute-start | bytes 786440 | tf_op jit(solution)/shard_map/ppermute | solution.py:48
  5.5 2.5 %collective-permute-start = (bf16[2,128,256]{2,1,0:T(8,128)(2,1)S(1)}, bf16[2,128,256]{2,1,0:T(8,128)(2,1)S(1)}, u32[]{:S(2)}, u32[]{:S(2)}) collective-permute-start(bf16[2,128,256]{2,1,0:T(8,128)(2,1)S(1)} %get-tuple-element.32.refs_0_), channel_id=1, source_target_pairs={{0,96},{1,97},{2,98},{3,99},{4,28},{5,29},{6,30},{7,31},{8,104},{9... | collective-permute-start | bytes 393224 | tf_op jit(solution)/shard_map/ppermute | solution.py:48
  8.0 2.8 %collective-permute-done.refs_2_ = bf16[2,128,256]{2,1,0:T(8,128)(2,1)S(1)} collective-permute-done((bf16[2,128,256]{2,1,0:T(8,128)(2,1)S(1)}, bf16[2,128,256]{2,1,0:T(8,128)(2,1)S(1)}, u32[]{:S(2)}, u32[]{:S(2)}) %collective-permute-start) | collective-permute-done | bytes 131104 | tf_op jit(solution)/shard_map/ppermute | solution.py:48
  10.8 1.0 %collective-permute-done.1.refs_3_ = bf16[2,128,256]{2,1,0:T(8,128)(2,1)S(1)} collective-permute-done((bf16[2,128,256]{2,1,0:T(8,128)(2,1)S(1)}, bf16[2,128,256]{2,1,0:T(8,128)(2,1)S(1)}, u32[]{:S(2)}, u32[]{:S(2)}) %collective-permute-start.1) | collective-permute-done | bytes 131104 | tf_op jit(solution)/shard_map/ppermute | solution.py:48
  12.0 3.8 %collective-permute-start.4 = (bf16[4,128,256]{2,1,0:T(8,128)(2,1)S(1)}, bf16[4,128,256]{2,1,0:T(8,128)(2,1)S(1)}, u32[]{:S(2)}, u32[]{:S(2)}) collective-permute-start(bf16[4,128,256]{2,1,0:T(8,128)(2,1)S(1)} %get-tuple-element.35.refs_0_), channel_id=1, source_target_pairs={{0,24},{1,25},{2,26},{3,27},{4,100},{5,101},{6,102},{7,103},{8,16}... | collective-permute-start | bytes 786440 | tf_op jit(solution)/shard_map/ppermute | solution.py:48
  15.9 5.4 %prepare.1 = (bf16[512,128,128]{2,1,0:T(8,128)(2,1)S(1)}, s32[1,640]{1,0:T(1,128)S(1)}, s32[1,640]{1,0:T(1,128)S(1)}, s32[1,640]{1,0:T(1,128)S(1)}, s32[1,640]{1,0:T(1,128)S(1)}) custom-call(s32[4]{0:T(128)S(1)} %pad_add_fusion.where_ref, s32[16]{0:T(128)} %bitcast.13, s32[16,32]{1,0:T(8,128)} %cols_ref.1, bf16[512,128,128]{2,1,0:T(8,128)(2,1)} %bitcast.9, ...), custom_call_target="tpu_custom_call" | custom-call | bytes 1024 | tf_op jit(solution)/shard_map/prepare/pallas_call | solution.py:158
  21.4 2.1 %products_3.1.refs_0_ = bf16[32,128,256]{2,1,0:T(8,128)(2,1)S(1)} custom-call(s32[1,640]{1,0:T(1,128)S(1)} %get-tuple-element.41.words_ref, bf16[17,128,256]{2,1,0:T(8,128)(2,1)S(1)} %join.3.grad_ref, bf16[512,128,128]{2,1,0:T(8,128)(2,1)S(1)} %get-tuple-element.38.refs_2_.adj_ref), custom_call_target="tpu_custom_call" | custom-call | bytes 1024 | tf_op jit(solution)/shard_map/products_3/pallas_call | solution.py:393
  23.6 4.3 %collective-permute-start.6 = (bf16[32,128,256]{2,1,0:T(8,128)(2,1)S(1)}, bf16[32,128,256]{2,1,0:T(8,128)(2,1)S(1)}, u32[]{:S(2)}, u32[]{:S(2)}) collective-permute-start(bf16[32,128,256]{2,1,0:T(8,128)(2,1)S(1)} %products_3.1.refs_0_), channel_id=1, source_target_pairs={{0,4},{1,5},{2,6},{3,7},{4,0},{5,1},{6,2},{7,3},{8,12},{9,13},{10,... | collective-permute-start | bytes 6291464 | tf_op jit(solution)/shard_map/ppermute | solution.py:66
  27.9 2.1 %products_2.1.refs_0_ = bf16[32,128,256]{2,1,0:T(8,128)(2,1)S(1)} custom-call(s32[1,640]{1,0:T(1,128)S(1)} %get-tuple-element.40.words_ref, bf16[17,128,256]{2,1,0:T(8,128)(2,1)S(1)} %join.3.grad_ref, bf16[512,128,128]{2,1,0:T(8,128)(2,1)S(1)} %get-tuple-element.38.refs_2_.adj_ref, bf16[32,128,256]{2,1,0:T(8,128)(2,1)S(1)} %products_3.1.refs_0_), custom_call_target="tpu_custom_call" | custom-call | bytes 1024 | tf_op jit(solution)/shard_map/products_2/pallas_call | solution.py:393
  30.1 2.1 %products_1.1.kept_ref = bf16[32,128,256]{2,1,0:T(8,128)(2,1)S(1)} custom-call(s32[1,640]{1,0:T(1,128)S(1)} %get-tuple-element.39.words_ref, bf16[17,128,256]{2,1,0:T(8,128)(2,1)S(1)} %join.3.grad_ref, bf16[512,128,128]{2,1,0:T(8,128)(2,1)S(1)} %get-tuple-element.38.refs_2_.adj_ref, bf16[32,128,256]{2,1,0:T(8,128)(2,1)S(1)} %products_2.1.refs_0_), custom_call_target="tpu_custom_call" | custom-call | bytes 1024 | tf_op jit(solution)/shard_map/products_1/pallas_call | solution.py:393
  32.8 0.8 collective-permute-start.8
  33.9 2.1 %products_0.1.kept_ref = bf16[32,128,256]{2,1,0:T(8,128)(2,1)S(1)} custom-call(s32[1,640]{1,0:T(1,128)S(1)} %get-tuple-element.37.words_ref, bf16[17,128,256]{2,1,0:T(8,128)(2,1)S(1)} %join.3.grad_ref, bf16[512,128,128]{2,1,0:T(8,128)(2,1)S(1)} %get-tuple-element.38.refs_2_.adj_ref, bf16[16,128,256]{2,1,0:T(8,128)(2,1)S(1)} %get-tuple-element.42.refs_0_, ...), custom_call_target="tpu_custom_call" | custom-call | bytes 1024 | tf_op jit(solution)/shard_map/products_0/pallas_call | solution.py:393
  36.6 10.2 %collective-permute-done.8.got_ref = bf16[16,128,256]{2,1,0:T(8,128)(2,1)S(1)} collective-permute-done((bf16[16,128,256]{2,1,0:T(8,128)(2,1)S(1)}, bf16[16,128,256]{2,1,0:T(8,128)(2,1)S(1)}, u32[]{:S(2)}, u32[]{:S(2)}) %collective-permute-start.8) | collective-permute-done | bytes 1048608 | tf_op jit(solution)/shard_map/ppermute | solution.py:48
  47.1 1.1 %collective-permute-start.9 = (bf16[8,128,256]{2,1,0:T(8,128)(2,1)S(1)}, bf16[8,128,256]{2,1,0:T(8,128)(2,1)S(1)}, u32[]{:S(2)}, u32[]{:S(2)}) collective-permute-start(bf16[8,128,256]{2,1,0:T(8,128)(2,1)S(1)} %get-tuple-element.46), channel_id=1, source_target_pairs={{0,32},{1,33},{2,34},{3,35},{4,12},{5,13},{6,14},{7,15},{8,40},{9,... | collective-permute-start | bytes 1572872 | tf_op jit(solution)/shard_map/ppermute | solution.py:48
  49.0 1.4 %collective-permute-start.12 = (bf16[8,128,256]{2,1,0:T(8,128)(2,1)S(1)}, bf16[8,128,256]{2,1,0:T(8,128)(2,1)S(1)}, u32[]{:S(2)}, u32[]{:S(2)}) collective-permute-start(bf16[8,128,256]{2,1,0:T(8,128)(2,1)S(1)} %get-tuple-element.51), channel_id=1, source_target_pairs={{0,96},{1,97},{2,98},{3,99},{4,28},{5,29},{6,30},{7,31},{8,104},{9... | collective-permute-start | bytes 1572872 | tf_op jit(solution)/shard_map/ppermute | solution.py:48
  50.4 5.1 %collective-permute-done.9.got_ref = bf16[8,128,256]{2,1,0:T(8,128)(2,1)S(1)} collective-permute-done((bf16[8,128,256]{2,1,0:T(8,128)(2,1)S(1)}, bf16[8,128,256]{2,1,0:T(8,128)(2,1)S(1)}, u32[]{:S(2)}, u32[]{:S(2)}) %collective-permute-start.9) | collective-permute-done | bytes 524320 | tf_op jit(solution)/shard_map/ppermute | solution.py:48
  55.6 3.0 %collective-permute-done.12.got_ref = bf16[8,128,256]{2,1,0:T(8,128)(2,1)S(1)} collective-permute-done((bf16[8,128,256]{2,1,0:T(8,128)(2,1)S(1)}, bf16[8,128,256]{2,1,0:T(8,128)(2,1)S(1)}, u32[]{:S(2)}, u32[]{:S(2)}) %collective-permute-start.12) | collective-permute-done | bytes 524320 | tf_op jit(solution)/shard_map/ppermute | solution.py:48
  59.2 2.6 %collective-permute-start.13 = (bf16[128,256]{1,0:T(8,128)(2,1)S(1)}, bf16[128,256]{1,0:T(8,128)(2,1)S(1)}, u32[]{:S(2)}, u32[]{:S(2)}) collective-permute-start(bf16[128,256]{1,0:T(8,128)(2,1)S(1)} %get-tuple-element.55), channel_id=1, source_target_pairs={{0,4},{1,5},{2,6},{3,7},{4,0},{5,1},{6,2},{7,3},{8,12},{9,13},{10,... | collective-permute-start | bytes 196616 | tf_op jit(solution)/shard_map/ppermute | solution.py:66
  61.8 3.0 %collective-permute-start.10 = (bf16[4,128,256]{2,1,0:T(8,128)(2,1)S(1)}, bf16[4,128,256]{2,1,0:T(8,128)(2,1)S(1)}, u32[]{:S(2)}, u32[]{:S(2)}) collective-permute-start(bf16[4,128,256]{2,1,0:T(8,128)(2,1)S(1)} %get-tuple-element.48.refs_3_), channel_id=1, source_target_pairs={{0,24},{1,25},{2,26},{3,27},{4,100},{5,101},{6,102},{7,103},{8,16}... | collective-permute-start | bytes 786440 | tf_op jit(solution)/shard_map/ppermute | solution.py:48
  64.9 2.1 %collective-permute-start.14 = (bf16[128,256]{1,0:T(8,128)(2,1)S(1)}, bf16[128,256]{1,0:T(8,128)(2,1)S(1)}, u32[]{:S(2)}, u32[]{:S(2)}) collective-permute-start(bf16[128,256]{1,0:T(8,128)(2,1)S(1)} %get-tuple-element.56.own_ref), channel_id=1, source_target_pairs={{0,16},{1,17},{2,18},{3,19},{4,68},{5,69},{6,70},{7,71},{8,24},{9,... | collective-permute-start | bytes 196616 | tf_op jit(solution)/shard_map/ppermute | solution.py:61
  67.0 2.7 %collective-permute-start.16 = (bf16[128,256]{1,0:T(8,128)(2,1)S(1)}, bf16[128,256]{1,0:T(8,128)(2,1)S(1)}, u32[]{:S(2)}, u32[]{:S(2)}) collective-permute-start(bf16[128,256]{1,0:T(8,128)(2,1)S(1)} %get-tuple-element.56.own_ref), channel_id=1, source_target_pairs={{0,24},{1,25},{2,26},{3,27},{4,100},{5,101},{6,102},{7,103},{8,0},... | collective-permute-start | bytes 196616 | tf_op jit(solution)/shard_map/ppermute | solution.py:61
  69.7 1.9 %collective-permute-done.14.opposite_ref = bf16[128,256]{1,0:T(8,128)(2,1)S(1)} collective-permute-done((bf16[128,256]{1,0:T(8,128)(2,1)S(1)}, bf16[128,256]{1,0:T(8,128)(2,1)S(1)}, u32[]{:S(2)}, u32[]{:S(2)}) %collective-permute-start.14) | collective-permute-done | bytes 65568 | tf_op jit(solution)/shard_map/ppermute | solution.py:61
  72.3 0.8 collective-permute-start.19
  73.1 2.1 %collective-permute-start.20 = (bf16[128,256]{1,0:T(8,128)(2,1)S(1)}, bf16[128,256]{1,0:T(8,128)(2,1)S(1)}, u32[]{:S(2)}, u32[]{:S(2)}) collective-permute-start(bf16[128,256]{1,0:T(8,128)(2,1)S(1)} %ring_sum.3.refs_0_.own_ref), channel_id=1, source_target_pairs={{0,96},{1,97},{2,98},{3,99},{4,28},{5,29},{6,30},{7,31},{8,104},{9... | collective-permute-start | bytes 196616 | tf_op jit(solution)/shard_map/ppermute | solution.py:61
  75.7 0.9 %collective-permute-start.22 = (bf16[2,128,256]{2,1,0:T(8,128)(2,1)S(1)}, bf16[2,128,256]{2,1,0:T(8,128)(2,1)S(1)}, u32[]{:S(2)}, u32[]{:S(2)}) collective-permute-start(bf16[2,128,256]{2,1,0:T(8,128)(2,1)S(1)} %get-tuple-element.61), channel_id=1, source_target_pairs={{0,32},{1,33},{2,34},{3,35},{4,12},{5,13},{6,14},{7,15},{8,40},{9,... | collective-permute-start | bytes 393224 | tf_op jit(solution)/shard_map/ppermute | solution.py:48
  77.0 0.9 collective-permute-done.19.left_ref
  78.7 1.4 %collective-permute-start.24 = (bf16[128,256]{1,0:T(8,128)(2,1)S(1)}, bf16[128,256]{1,0:T(8,128)(2,1)S(1)}, u32[]{:S(2)}, u32[]{:S(2)}) collective-permute-start(bf16[128,256]{1,0:T(8,128)(2,1)S(1)} %ring_sum.4.refs_0_.own_ref), channel_id=1, source_target_pairs={{0,1},{1,2},{2,3},{3,0},{4,5},{5,6},{6,7},{7,4},{8,9},{9,10},{10,1... | collective-permute-start | bytes 196616 | tf_op jit(solution)/shard_map/ppermute | solution.py:61
  80.1 1.3 %collective-permute-start.25 = (bf16[128,256]{1,0:T(8,128)(2,1)S(1)}, bf16[128,256]{1,0:T(8,128)(2,1)S(1)}, u32[]{:S(2)}, u32[]{:S(2)}) collective-permute-start(bf16[128,256]{1,0:T(8,128)(2,1)S(1)} %ring_sum.4.refs_0_.own_ref), channel_id=1, source_target_pairs={{0,3},{1,0},{2,1},{3,2},{4,7},{5,4},{6,5},{7,6},{8,11},{9,8},{10,9... | collective-permute-start | bytes 196616 | tf_op jit(solution)/shard_map/ppermute | solution.py:61
  81.4 1.2 %collective-permute-done.23.opposite_ref = bf16[128,256]{1,0:T(8,128)(2,1)S(1)} collective-permute-done((bf16[128,256]{1,0:T(8,128)(2,1)S(1)}, bf16[128,256]{1,0:T(8,128)(2,1)S(1)}, u32[]{:S(2)}, u32[]{:S(2)}) %collective-permute-start.23) | collective-permute-done | bytes 65568 | tf_op jit(solution)/shard_map/ppermute | solution.py:61
  83.3 4.4 %collective-permute-start.26 = (bf16[128,256]{1,0:T(8,128)(2,1)S(1)}, bf16[128,256]{1,0:T(8,128)(2,1)S(1)}, u32[]{:S(2)}, u32[]{:S(2)}) collective-permute-start(bf16[128,256]{1,0:T(8,128)(2,1)S(1)} %ring_sum.5), channel_id=1, source_target_pairs={{0,4},{1,5},{2,6},{3,7},{4,0},{5,1},{6,2},{7,3},{8,12},{9,13},{10,... | collective-permute-start | bytes 196616 | tf_op jit(solution)/shard_map/ppermute | solution.py:66
  87.7 1.0 %features_gradient.1 = bf16[512,256]{1,0:T(8,128)(2,1)} custom-call(bf16[2,128,256]{2,1,0:T(8,128)(2,1)S(1)} %fold.18.first_ref.refs_0_, bf16[2,128,256]{2,1,0:T(8,128)(2,1)S(1)} %fold.19.second_ref.refs_1_, bf16[256,256]{1,0:T(8,128)(2,1)S(1)} %copy-done), custom_call_target="tpu_custom_call" | custom-call | bytes 1024 | tf_op jit(solution)/shard_map/features_gradient/pallas_call | solution.py:329
  (52 shorter events, 7.6 us)
Async XLA Ops:
  1.9 9.9 %collective-permute-start.2 = (bf16[4,128,256]{2,1,0:T(8,128)(2,1)S(1)}, bf16[4,128,256]{2,1,0:T(8,128)(2,1)S(1)}, u32[]{:S(2)}, u32[]{:S(2)}) collective-permute-start(bf16[4,128,256]{2,1,0:T(8,128)(2,1)S(1)} %get-tuple-element.34.refs_0_), channel_id=1, source_target_pairs={{0,1},{1,0},{2,3},{3,2},{4,7},{5,6},{6,5},{7,4},{8,9},{9,8},{10,11... | collective-permute-start | bytes 786440 | tf_op jit(solution)/shard_map/ppermute | solution.py:48
  5.5 5.3 %collective-permute-start = (bf16[2,128,256]{2,1,0:T(8,128)(2,1)S(1)}, bf16[2,128,256]{2,1,0:T(8,128)(2,1)S(1)}, u32[]{:S(2)}, u32[]{:S(2)}) collective-permute-start(bf16[2,128,256]{2,1,0:T(8,128)(2,1)S(1)} %get-tuple-element.32.refs_0_), channel_id=1, source_target_pairs={{0,96},{1,97},{2,98},{3,99},{4,28},{5,29},{6,30},{7,31},{8,104},{9... | collective-permute-start | bytes 393224 | tf_op jit(solution)/shard_map/ppermute | solution.py:48
  8.0 3.8 %collective-permute-start.1 = (bf16[2,128,256]{2,1,0:T(8,128)(2,1)S(1)}, bf16[2,128,256]{2,1,0:T(8,128)(2,1)S(1)}, u32[]{:S(2)}, u32[]{:S(2)}) collective-permute-start(bf16[2,128,256]{2,1,0:T(8,128)(2,1)S(1)} %get-tuple-element.33.refs_1_), channel_id=1, source_target_pairs={{0,32},{1,33},{2,34},{3,35},{4,12},{5,13},{6,14},{7,15},{8,40},{9,... | collective-permute-start | bytes 393224 | tf_op jit(solution)/shard_map/ppermute | solution.py:48
  11.8 9.5 %collective-permute-start.3 = (bf16[8,128,256]{2,1,0:T(8,128)(2,1)S(1)}, bf16[8,128,256]{2,1,0:T(8,128)(2,1)S(1)}, u32[]{:S(2)}, u32[]{:S(2)}) collective-permute-start(bf16[8,128,256]{2,1,0:T(8,128)(2,1)S(1)} %join.2.refs_4_.refs_0_), channel_id=1, source_target_pairs={{0,3},{1,2},{2,1},{3,0},{4,5},{5,4},{6,7},{7,6},{8,11},{9,10},{10,... | collective-permute-start | bytes 1572872 | tf_op jit(solution)/shard_map/ppermute | solution.py:48
  12.0 9.3 %collective-permute-start.4 = (bf16[4,128,256]{2,1,0:T(8,128)(2,1)S(1)}, bf16[4,128,256]{2,1,0:T(8,128)(2,1)S(1)}, u32[]{:S(2)}, u32[]{:S(2)}) collective-permute-start(bf16[4,128,256]{2,1,0:T(8,128)(2,1)S(1)} %get-tuple-element.35.refs_0_), channel_id=1, source_target_pairs={{0,24},{1,25},{2,26},{3,27},{4,100},{5,101},{6,102},{7,103},{8,16}... | collective-permute-start | bytes 786440 | tf_op jit(solution)/shard_map/ppermute | solution.py:48
  15.8 5.5 %collective-permute-start.5 = (bf16[4,128,256]{2,1,0:T(8,128)(2,1)S(1)}, bf16[4,128,256]{2,1,0:T(8,128)(2,1)S(1)}, u32[]{:S(2)}, u32[]{:S(2)}) collective-permute-start(bf16[4,128,256]{2,1,0:T(8,128)(2,1)S(1)} %get-tuple-element.36.refs_1_.refs_4_), channel_id=1, source_target_pairs={{0,8},{1,9},{2,10},{3,11},{4,36},{5,37},{6,38},{7,39},{8,0},{9,1},... | collective-permute-start | bytes 786440 | tf_op jit(solution)/shard_map/ppermute | solution.py:48
  23.6 8.7 %collective-permute-start.6 = (bf16[32,128,256]{2,1,0:T(8,128)(2,1)S(1)}, bf16[32,128,256]{2,1,0:T(8,128)(2,1)S(1)}, u32[]{:S(2)}, u32[]{:S(2)}) collective-permute-start(bf16[32,128,256]{2,1,0:T(8,128)(2,1)S(1)} %products_3.1.refs_0_), channel_id=1, source_target_pairs={{0,4},{1,5},{2,6},{3,7},{4,0},{5,1},{6,2},{7,3},{8,12},{9,13},{10,... | collective-permute-start | bytes 6291464 | tf_op jit(solution)/shard_map/ppermute | solution.py:66
  30.0 6.0 %collective-permute-start.7 = (bf16[32,128,256]{2,1,0:T(8,128)(2,1)S(1)}, bf16[32,128,256]{2,1,0:T(8,128)(2,1)S(1)}, u32[]{:S(2)}, u32[]{:S(2)}) collective-permute-start(bf16[32,128,256]{2,1,0:T(8,128)(2,1)S(1)} %products_2.1.refs_0_), channel_id=1, source_target_pairs={{0,4},{1,5},{2,6},{3,7},{4,0},{5,1},{6,2},{7,3},{8,12},{9,13},{10,... | collective-permute-start | bytes 6291464 | tf_op jit(solution)/shard_map/ppermute | solution.py:66
  32.8 14.0 %collective-permute-start.8 = (bf16[16,128,256]{2,1,0:T(8,128)(2,1)S(1)}, bf16[16,128,256]{2,1,0:T(8,128)(2,1)S(1)}, u32[]{:S(2)}, u32[]{:S(2)}) collective-permute-start(bf16[16,128,256]{2,1,0:T(8,128)(2,1)S(1)} %get-tuple-element.42.refs_0_), channel_id=1, source_target_pairs={{0,8},{1,9},{2,10},{3,11},{4,36},{5,37},{6,38},{7,39},{8,0},{9,1},... | collective-permute-start | bytes 3145736 | tf_op jit(solution)/shard_map/ppermute | solution.py:48
  33.6 15.2 %collective-permute-start.11 = (bf16[16,128,256]{2,1,0:T(8,128)(2,1)S(1)}, bf16[16,128,256]{2,1,0:T(8,128)(2,1)S(1)}, u32[]{:S(2)}, u32[]{:S(2)}) collective-permute-start(bf16[16,128,256]{2,1,0:T(8,128)(2,1)S(1)} %get-tuple-element.43.refs_1_), channel_id=1, source_target_pairs={{0,24},{1,25},{2,26},{3,27},{4,100},{5,101},{6,102},{7,103},{8,16}... | collective-permute-start | bytes 3145736 | tf_op jit(solution)/shard_map/ppermute | solution.py:48
  47.1 8.4 %collective-permute-start.9 = (bf16[8,128,256]{2,1,0:T(8,128)(2,1)S(1)}, bf16[8,128,256]{2,1,0:T(8,128)(2,1)S(1)}, u32[]{:S(2)}, u32[]{:S(2)}) collective-permute-start(bf16[8,128,256]{2,1,0:T(8,128)(2,1)S(1)} %get-tuple-element.46), channel_id=1, source_target_pairs={{0,32},{1,33},{2,34},{3,35},{4,12},{5,13},{6,14},{7,15},{8,40},{9,... | collective-permute-start | bytes 1572872 | tf_op jit(solution)/shard_map/ppermute | solution.py:48
  49.0 9.6 %collective-permute-start.12 = (bf16[8,128,256]{2,1,0:T(8,128)(2,1)S(1)}, bf16[8,128,256]{2,1,0:T(8,128)(2,1)S(1)}, u32[]{:S(2)}, u32[]{:S(2)}) collective-permute-start(bf16[8,128,256]{2,1,0:T(8,128)(2,1)S(1)} %get-tuple-element.51), channel_id=1, source_target_pairs={{0,96},{1,97},{2,98},{3,99},{4,28},{5,29},{6,30},{7,31},{8,104},{9... | collective-permute-start | bytes 1572872 | tf_op jit(solution)/shard_map/ppermute | solution.py:48
  59.2 5.6 %collective-permute-start.13 = (bf16[128,256]{1,0:T(8,128)(2,1)S(1)}, bf16[128,256]{1,0:T(8,128)(2,1)S(1)}, u32[]{:S(2)}, u32[]{:S(2)}) collective-permute-start(bf16[128,256]{1,0:T(8,128)(2,1)S(1)} %get-tuple-element.55), channel_id=1, source_target_pairs={{0,4},{1,5},{2,6},{3,7},{4,0},{5,1},{6,2},{7,3},{8,12},{9,13},{10,... | collective-permute-start | bytes 196616 | tf_op jit(solution)/shard_map/ppermute | solution.py:66
  61.8 13.3 %collective-permute-start.10 = (bf16[4,128,256]{2,1,0:T(8,128)(2,1)S(1)}, bf16[4,128,256]{2,1,0:T(8,128)(2,1)S(1)}, u32[]{:S(2)}, u32[]{:S(2)}) collective-permute-start(bf16[4,128,256]{2,1,0:T(8,128)(2,1)S(1)} %get-tuple-element.48.refs_3_), channel_id=1, source_target_pairs={{0,24},{1,25},{2,26},{3,27},{4,100},{5,101},{6,102},{7,103},{8,16}... | collective-permute-start | bytes 786440 | tf_op jit(solution)/shard_map/ppermute | solution.py:48
  64.8 22.9 %copy-start = (bf16[256,256]{1,0:T(8,128)(2,1)S(1)}, bf16[256,256]{1,0:T(8,128)(2,1)}, u32[]{:S(2)}) copy-start(bf16[256,256]{1,0:T(8,128)(2,1)} %weight_ref.1) | copy-start | bytes 393220
  64.8 10.8 %collective-permute-start.21 = (bf16[4,128,256]{2,1,0:T(8,128)(2,1)S(1)}, bf16[4,128,256]{2,1,0:T(8,128)(2,1)S(1)}, u32[]{:S(2)}, u32[]{:S(2)}) collective-permute-start(bf16[4,128,256]{2,1,0:T(8,128)(2,1)S(1)} %get-tuple-element.59), channel_id=1, source_target_pairs={{0,8},{1,9},{2,10},{3,11},{4,36},{5,37},{6,38},{7,39},{8,0},{9,1},... | collective-permute-start | bytes 786440 | tf_op jit(solution)/shard_map/ppermute | solution.py:48
  64.9 6.6 %collective-permute-start.14 = (bf16[128,256]{1,0:T(8,128)(2,1)S(1)}, bf16[128,256]{1,0:T(8,128)(2,1)S(1)}, u32[]{:S(2)}, u32[]{:S(2)}) collective-permute-start(bf16[128,256]{1,0:T(8,128)(2,1)S(1)} %get-tuple-element.56.own_ref), channel_id=1, source_target_pairs={{0,16},{1,17},{2,18},{3,19},{4,68},{5,69},{6,70},{7,71},{8,24},{9,... | collective-permute-start | bytes 196616 | tf_op jit(solution)/shard_map/ppermute | solution.py:61
  67.0 5.1 %collective-permute-start.15 = (bf16[128,256]{1,0:T(8,128)(2,1)S(1)}, bf16[128,256]{1,0:T(8,128)(2,1)S(1)}, u32[]{:S(2)}, u32[]{:S(2)}) collective-permute-start(bf16[128,256]{1,0:T(8,128)(2,1)S(1)} %get-tuple-element.56.own_ref), channel_id=1, source_target_pairs={{0,8},{1,9},{2,10},{3,11},{4,36},{5,37},{6,38},{7,39},{8,16},{9,17... | collective-permute-start | bytes 196616 | tf_op jit(solution)/shard_map/ppermute | solution.py:61
  67.0 5.1 %collective-permute-start.16 = (bf16[128,256]{1,0:T(8,128)(2,1)S(1)}, bf16[128,256]{1,0:T(8,128)(2,1)S(1)}, u32[]{:S(2)}, u32[]{:S(2)}) collective-permute-start(bf16[128,256]{1,0:T(8,128)(2,1)S(1)} %get-tuple-element.56.own_ref), channel_id=1, source_target_pairs={{0,24},{1,25},{2,26},{3,27},{4,100},{5,101},{6,102},{7,103},{8,0},... | collective-permute-start | bytes 196616 | tf_op jit(solution)/shard_map/ppermute | solution.py:61
  72.2 4.8 %collective-permute-start.18 = (bf16[128,256]{1,0:T(8,128)(2,1)S(1)}, bf16[128,256]{1,0:T(8,128)(2,1)S(1)}, u32[]{:S(2)}, u32[]{:S(2)}) collective-permute-start(bf16[128,256]{1,0:T(8,128)(2,1)S(1)} %ring_sum.3.refs_0_.own_ref), channel_id=1, source_target_pairs={{0,64},{1,65},{2,66},{3,67},{4,20},{5,21},{6,22},{7,23},{8,72},{9,... | collective-permute-start | bytes 196616 | tf_op jit(solution)/shard_map/ppermute | solution.py:61
  72.3 5.6 %collective-permute-start.19 = (bf16[128,256]{1,0:T(8,128)(2,1)S(1)}, bf16[128,256]{1,0:T(8,128)(2,1)S(1)}, u32[]{:S(2)}, u32[]{:S(2)}) collective-permute-start(bf16[128,256]{1,0:T(8,128)(2,1)S(1)} %ring_sum.3.refs_0_.own_ref), channel_id=1, source_target_pairs={{0,32},{1,33},{2,34},{3,35},{4,12},{5,13},{6,14},{7,15},{8,40},{9,... | collective-permute-start | bytes 196616 | tf_op jit(solution)/shard_map/ppermute | solution.py:61
  73.1 4.8 %collective-permute-start.20 = (bf16[128,256]{1,0:T(8,128)(2,1)S(1)}, bf16[128,256]{1,0:T(8,128)(2,1)S(1)}, u32[]{:S(2)}, u32[]{:S(2)}) collective-permute-start(bf16[128,256]{1,0:T(8,128)(2,1)S(1)} %ring_sum.3.refs_0_.own_ref), channel_id=1, source_target_pairs={{0,96},{1,97},{2,98},{3,99},{4,28},{5,29},{6,30},{7,31},{8,104},{9... | collective-permute-start | bytes 196616 | tf_op jit(solution)/shard_map/ppermute | solution.py:61
  75.3 6.1 %collective-permute-start.17 = (bf16[2,128,256]{2,1,0:T(8,128)(2,1)S(1)}, bf16[2,128,256]{2,1,0:T(8,128)(2,1)S(1)}, u32[]{:S(2)}, u32[]{:S(2)}) collective-permute-start(bf16[2,128,256]{2,1,0:T(8,128)(2,1)S(1)} %get-tuple-element.58), channel_id=1, source_target_pairs={{0,96},{1,97},{2,98},{3,99},{4,28},{5,29},{6,30},{7,31},{8,104},{9... | collective-permute-start | bytes 393224 | tf_op jit(solution)/shard_map/ppermute | solution.py:48
  75.7 5.7 %collective-permute-start.22 = (bf16[2,128,256]{2,1,0:T(8,128)(2,1)S(1)}, bf16[2,128,256]{2,1,0:T(8,128)(2,1)S(1)}, u32[]{:S(2)}, u32[]{:S(2)}) collective-permute-start(bf16[2,128,256]{2,1,0:T(8,128)(2,1)S(1)} %get-tuple-element.61), channel_id=1, source_target_pairs={{0,32},{1,33},{2,34},{3,35},{4,12},{5,13},{6,14},{7,15},{8,40},{9,... | collective-permute-start | bytes 393224 | tf_op jit(solution)/shard_map/ppermute | solution.py:48
  77.9 4.7 %collective-permute-start.23 = (bf16[128,256]{1,0:T(8,128)(2,1)S(1)}, bf16[128,256]{1,0:T(8,128)(2,1)S(1)}, u32[]{:S(2)}, u32[]{:S(2)}) collective-permute-start(bf16[128,256]{1,0:T(8,128)(2,1)S(1)} %ring_sum.4.refs_0_.own_ref), channel_id=1, source_target_pairs={{0,2},{1,3},{2,0},{3,1},{4,6},{5,7},{6,4},{7,5},{8,10},{9,11},{10,... | collective-permute-start | bytes 196616 | tf_op jit(solution)/shard_map/ppermute | solution.py:61
  78.7 4.6 %collective-permute-start.24 = (bf16[128,256]{1,0:T(8,128)(2,1)S(1)}, bf16[128,256]{1,0:T(8,128)(2,1)S(1)}, u32[]{:S(2)}, u32[]{:S(2)}) collective-permute-start(bf16[128,256]{1,0:T(8,128)(2,1)S(1)} %ring_sum.4.refs_0_.own_ref), channel_id=1, source_target_pairs={{0,1},{1,2},{2,3},{3,0},{4,5},{5,6},{6,7},{7,4},{8,9},{9,10},{10,1... | collective-permute-start | bytes 196616 | tf_op jit(solution)/shard_map/ppermute | solution.py:61
  80.1 3.2 %collective-permute-start.25 = (bf16[128,256]{1,0:T(8,128)(2,1)S(1)}, bf16[128,256]{1,0:T(8,128)(2,1)S(1)}, u32[]{:S(2)}, u32[]{:S(2)}) collective-permute-start(bf16[128,256]{1,0:T(8,128)(2,1)S(1)} %ring_sum.4.refs_0_.own_ref), channel_id=1, source_target_pairs={{0,3},{1,0},{2,1},{3,2},{4,7},{5,4},{6,5},{7,6},{8,11},{9,8},{10,9... | collective-permute-start | bytes 196616 | tf_op jit(solution)/shard_map/ppermute | solution.py:61
  83.3 5.4 %collective-permute-start.26 = (bf16[128,256]{1,0:T(8,128)(2,1)S(1)}, bf16[128,256]{1,0:T(8,128)(2,1)S(1)}, u32[]{:S(2)}, u32[]{:S(2)}) collective-permute-start(bf16[128,256]{1,0:T(8,128)(2,1)S(1)} %ring_sum.5), channel_id=1, source_target_pairs={{0,4},{1,5},{2,6},{3,7},{4,0},{5,1},{6,2},{7,3},{8,12},{9,13},{10,... | collective-permute-start | bytes 196616 | tf_op jit(solution)/shard_map/ppermute | solution.py:66
